TPU v7x, 512 devices: a whole 4x4x16 slice. The times are simulated.
512 devices in a mesh: gz: 128 (over z_hi, x, y, core), gy: 4 (over z_lo).
Axes of the slice: x: 4, y: 4, z: 16 (z_hi: 4, z_lo: 4; z = z_hi * 4 + z_lo), core: 2. Of those that a mesh axis runs over, the one named last changes fastest.
Arguments:
- density: float32 [512, 128, 512], P('gz', 'gy'), may hold values from 0.1 to 10
- right_side: float32 [512, 128, 512], P('gz', 'gy'), may hold values from -6 to 6
- pressure_guess: float32 [512, 128, 512], P('gz', 'gy'), may hold values from -6 to 6
Outputs:
- pressure: float32 [512, 128, 512], P('gz', 'gy')
All inputs are finite; a program needn't handle non-finite values.
Results may differ from a plain program's by a relative error of at most 0.0001.
Values sent between devices are 32-bit elements; how exact they have to be, the bound alone decides.
A program may use at most 128 MiB of HBM per device.

v0:
```python
import jax
import jax.numpy as jnp
from jax import lax
from jax.sharding import PartitionSpec as P

COARSE_SWEEPS = 8


relaxation = 0.8


def with_halo(block, sides, width):
    for axis, dim in sides:
        count = lax.axis_size(axis)
        forward = [(i, i + 1) for i in range(count - 1)]
        backward = [(target, source) for source, target in forward]
        low = lax.ppermute(
            lax.slice_in_dim(block, block.shape[dim] - width, None, axis=dim), axis, forward
        )
        high = lax.ppermute(lax.slice_in_dim(block, 0, width, axis=dim), axis, backward)
        block = jnp.concatenate([low, block, high], axis=dim)
    return block


def edge_pad(values, axis_num):
    length = values.shape[axis_num]
    first_layer = lax.slice_in_dim(values, 0, 1, axis=axis_num)
    last_layer = lax.slice_in_dim(values, length - 1, length, axis=axis_num)
    return jnp.concatenate([first_layer, values, last_layer], axis=axis_num)


def zero_pad(values, axis_num):
    widths = [(0, 0)] * values.ndim
    widths[axis_num] = (1, 1)
    return jnp.pad(values, widths)


def alternate(even_part, odd_part, axis_num):
    stacked = jnp.stack([even_part, odd_part], axis=axis_num + 1)
    new_shape = list(even_part.shape)
    new_shape[axis_num] = 2 * new_shape[axis_num]
    return stacked.reshape(new_shape)


def rimmed(values):
    return with_halo(values, (("gz", 0), ("gy", 1)), 1)


def rimmed_corners(values):
    return with_halo(values, (("gz", 0), ("gy", 1)), 1)


def coarse_total(values):
    return jnp.sum(values)


def boundary_flags():
    z_index = lax.axis_index("gz")
    y_index = lax.axis_index("gy")
    return (
        z_index == 0,
        z_index == lax.axis_size("gz") - 1,
        y_index == 0,
        y_index == lax.axis_size("gy") - 1,
    )


def fill_axis(padded, rim_width, axis_num, at_low, at_high):
    length = padded.shape[axis_num]
    inner_low = lax.slice_in_dim(padded, rim_width, rim_width + 1, axis=axis_num)
    inner_high = lax.slice_in_dim(padded, length - rim_width - 1, length - rim_width, axis=axis_num)
    low_rims = lax.slice_in_dim(padded, 0, rim_width, axis=axis_num)
    high_rims = lax.slice_in_dim(padded, length - rim_width, length, axis=axis_num)
    middle_part = lax.slice_in_dim(padded, rim_width, length - rim_width, axis=axis_num)
    low_rims = jnp.where(at_low, inner_low, low_rims)
    high_rims = jnp.where(at_high, inner_high, high_rims)
    return jnp.concatenate([low_rims, middle_part, high_rims], axis=axis_num)


def edge_fill(padded, rim_width, boundary):
    z_low, z_high, y_low, y_high = boundary
    padded = fill_axis(padded, rim_width, 0, z_low, z_high)
    return fill_axis(padded, rim_width, 1, y_low, y_high)


def local_coefficients(padded):
    inner_dens = padded[1:-1, 1:-1]
    dens_z = padded[:, 1:-1]
    face_z = 2.0 / (dens_z[:-1] + dens_z[1:])
    dens_y = padded[1:-1]
    face_y = 2.0 / (dens_y[:, :-1] + dens_y[:, 1:])
    dens_x = edge_pad(inner_dens, 2)
    face_x = 2.0 / (dens_x[..., :-1] + dens_x[..., 1:])
    diagonal = (
        face_z[:-1]
        + face_z[1:]
        + face_y[:, :-1]
        + face_y[:, 1:]
        + face_x[..., :-1]
        + face_x[..., 1:]
    )
    return (face_z, face_y, face_x, diagonal)


def local_operator(padded, coeffs):
    face_z, face_y, face_x, diagonal = coeffs
    inner_vals = padded[1:-1, 1:-1]
    x_padded = zero_pad(inner_vals, 2)
    summed = diagonal * inner_vals
    summed = summed - face_z[:-1] * padded[:-2, 1:-1]
    summed = summed - face_z[1:] * padded[2:, 1:-1]
    summed = summed - face_y[:, :-1] * padded[1:-1, :-2]
    summed = summed - face_y[:, 1:] * padded[1:-1, 2:]
    summed = summed - face_x[..., :-1] * x_padded[..., :-2]
    summed = summed - face_x[..., 1:] * x_padded[..., 2:]
    return summed


def jacobi_local(padded, source, coeffs, level_scale):
    inner_vals = padded[1:-1, 1:-1]
    return inner_vals + relaxation * (source - level_scale * local_operator(padded, coeffs)) / (
        level_scale * coeffs[3]
    )


def restrict_local(values):
    depth, height, breadth = values.shape
    return values.reshape(depth // 2, 2, height // 2, 2, breadth // 2, 2).mean(axis=(1, 3, 5))


def prolong_local(coarse):
    padded = rimmed_corners(coarse)
    inner_z = padded[1:-1]
    fine_z = alternate(0.75 * inner_z + 0.25 * padded[:-2], 0.75 * inner_z + 0.25 * padded[2:], 0)
    inner_y = fine_z[:, 1:-1]
    fine_y = alternate(
        0.75 * inner_y + 0.25 * fine_z[:, :-2], 0.75 * inner_y + 0.25 * fine_z[:, 2:], 1
    )
    x_padded = zero_pad(fine_y, 2)
    return alternate(
        0.75 * fine_y + 0.25 * x_padded[..., :-2], 0.75 * fine_y + 0.25 * x_padded[..., 2:], 2
    )


def pair_sum(values):
    depth, height, breadth = values.shape
    summed = values.reshape(depth, height // 2, 2, breadth // 2, 2).sum(axis=(2, 4))
    return summed.reshape(depth, height // 2 * (breadth // 2))


def z_pairs(values):
    depth, flat_len = values.shape
    return values.reshape(depth // 2, 2, flat_len).sum(axis=1) * 0.125


def flat_coefficients(dens, low_rows, high_rows, col_first, col_last, row_len):
    dens_z = jnp.concatenate([dens[:1], dens, dens[-1:]], 0)
    face_z = 2.0 / (dens_z[:-1] + dens_z[1:])
    dens_y = jnp.concatenate([low_rows, dens, high_rows], 1)
    face_y = 2.0 / (dens_y[:, :-row_len] + dens_y[:, row_len:])
    prev_dens = jnp.concatenate([dens[:, :1], dens[:, :-1]], 1)
    next_dens = jnp.concatenate([dens[:, 1:], dens[:, -1:]], 1)
    x_low = 2.0 / (jnp.where(col_first, dens, prev_dens) + dens)
    x_high = 2.0 / (dens + jnp.where(col_last, dens, next_dens))
    y_low = face_y[:, :-row_len]
    y_high = face_y[:, row_len:]
    diagonal = face_z[:-1] + face_z[1:] + y_low + y_high + x_low + x_high
    return (face_z[:-1], face_z[1:], y_low, y_high, x_low, x_high, diagonal)


def flat_operator(values, low_vals, high_vals, coeffs, col_first, col_last, row_len):
    z_lowf, z_highf, y_lowf, y_highf, x_lowf, x_highf, diagonal = coeffs
    plane_zero = jnp.zeros_like(values[:1])
    below_z = jnp.concatenate([plane_zero, values[:-1]], 0)
    above_z = jnp.concatenate([values[1:], plane_zero], 0)
    y_padded = jnp.concatenate([low_vals, values, high_vals], 1)
    below_y = y_padded[:, : -2 * row_len]
    above_y = y_padded[:, 2 * row_len :]
    zero_col = jnp.zeros_like(values[:, :1])
    below_x = jnp.where(col_first, 0.0, jnp.concatenate([zero_col, values[:, :-1]], 1))
    above_x = jnp.where(col_last, 0.0, jnp.concatenate([values[:, 1:], zero_col], 1))
    summed = diagonal * values
    summed = summed - z_lowf * below_z
    summed = summed - z_highf * above_z
    summed = summed - y_lowf * below_y
    summed = summed - y_highf * above_y
    summed = summed - x_lowf * below_x
    summed = summed - x_highf * above_x
    return summed


def per_device(density, right_side, pressure_guess):
    boundary = boundary_flags()
    fine_coeffs = local_coefficients(edge_fill(rimmed(density), 1, boundary))
    pressure = jacobi_local(rimmed(pressure_guess), right_side, fine_coeffs, 1.0)
    residual = right_side - 1.0 * local_operator(rimmed(pressure), fine_coeffs)
    dens_one = restrict_local(density)
    coeffs_one = local_coefficients(edge_fill(rimmed(dens_one), 1, boundary))
    source_one = restrict_local(residual)
    corr_one = relaxation * source_one / (0.25 * coeffs_one[3])
    resid_one = source_one - 0.25 * local_operator(rimmed(corr_one), coeffs_one)
    dens_two = restrict_local(dens_one)
    coeffs_two = local_coefficients(edge_fill(rimmed(dens_two), 1, boundary))
    source_two = restrict_local(resid_one)
    corr_two = relaxation * source_two / (0.0625 * coeffs_two[3])
    resid_two = source_two - 0.0625 * local_operator(rimmed(corr_two), coeffs_two)
    row_len = resid_two.shape[2] // 2
    strip_rows = resid_two.shape[1] // 2
    gathered = (
        lax.all_gather(pair_sum(resid_two), "gz", axis=0, tiled=True),
        lax.all_gather(pair_sum(dens_two), "gz", axis=0, tiled=True),
    )
    gathered = (
        lax.all_gather(gathered[0], "gy", axis=1, tiled=True),
        lax.all_gather(gathered[1], "gy", axis=1, tiled=True),
    )
    source_three = z_pairs(gathered[0])
    dens_three = z_pairs(gathered[1])
    flat_len = dens_three.shape[1]
    col_at = jnp.arange(flat_len) % row_len
    col_first = col_at == 0
    col_last = col_at == row_len - 1
    low_rows = dens_three[:, :row_len]
    high_rows = dens_three[:, flat_len - row_len :]
    coeffs_three = flat_coefficients(dens_three, low_rows, high_rows, col_first, col_last, row_len)
    scale_three = 0.015625
    blank_rows = jnp.zeros((source_three.shape[0], row_len), jnp.float32)
    corr_three = jnp.zeros_like(source_three)
    resid_three = source_three
    direction = source_three
    norm_now = coarse_total(resid_three * resid_three)
    for sweep_num in range(COARSE_SWEEPS):
        image = scale_three * flat_operator(
            direction, blank_rows, blank_rows, coeffs_three, col_first, col_last, row_len
        )
        alpha = norm_now / coarse_total(direction * image)
        corr_three = corr_three + alpha * direction
        if sweep_num + 1 < COARSE_SWEEPS:
            resid_three = resid_three - alpha * image
            norm_next = coarse_total(resid_three * resid_three)
            direction = resid_three + norm_next / norm_now * direction
            norm_now = norm_next
    bordered = jnp.concatenate([blank_rows, corr_three, blank_rows], 1)
    window = lax.dynamic_slice_in_dim(
        bordered, lax.axis_index("gy") * strip_rows * row_len, (strip_rows + 2) * row_len, 1
    )
    window = window.reshape(window.shape[0], strip_rows + 2, row_len)
    z_padded = zero_pad(window, 0)
    plane_count = resid_two.shape[0]
    first_plane = lax.axis_index("gz") * plane_count
    fine_index = first_plane + 0
    parent = fine_index // 2
    parity = fine_index % 2
    own_plane = lax.dynamic_index_in_dim(z_padded, parent + 1, 0, keepdims=False)
    near_plane = lax.dynamic_index_in_dim(z_padded, parent + 2 * parity, 0, keepdims=False)
    plane_list = [0.75 * own_plane + 0.25 * near_plane]
    fine_z = jnp.stack(plane_list, 0)
    inner_y = fine_z[:, 1:-1]
    fine_y = alternate(
        0.75 * inner_y + 0.25 * fine_z[:, :-2], 0.75 * inner_y + 0.25 * fine_z[:, 2:], 1
    )
    x_padded = zero_pad(fine_y, 2)
    fine_x = alternate(
        0.75 * fine_y + 0.25 * x_padded[..., :-2], 0.75 * fine_y + 0.25 * x_padded[..., 2:], 2
    )
    up_two = jacobi_local(rimmed(corr_two + fine_x), source_two, coeffs_two, 0.0625)
    up_one = jacobi_local(rimmed(corr_one + prolong_local(up_two)), source_one, coeffs_one, 0.25)
    return jacobi_local(rimmed(pressure + prolong_local(up_one)), right_side, fine_coeffs, 1.0)


def solution(mesh):
    in_specs = (P("gz", "gy", None), P("gz", "gy", None), P("gz", "gy", None))
    out_specs = P("gz", "gy", None)
    return jax.shard_map(
        per_device, mesh=mesh, in_specs=in_specs, out_specs=out_specs, check_vma=False
    )
```

profile of v0, /device:TPU:448, one launch (start us, length us, event | category | flops | bytes accessed | tf_op | source)
XLA Modules:
  0.0 846.5 jit_solution(1989793433027681964)
XLA Ops:
  0.0 18.9 %reshape.155 = f32[2,2,16,2,256,2]{5,4,3,2,1,0:T(8,128)} reshape(f32[4,32,512]{2,1,0:T(8,128)} %param.3) | data formatting | bytes 524288 | tf_op jit(solution)/shard_map/reshape | solution.py:128
  18.9 7.0 reduce_sum.231
  27.2 9.5 %collective-permute-start.21 = (f32[1,8,128]{2,1,0:T(8,128)S(1)}, f32[1,8,128]{2,1,0:T(8,128)S(1)}, u32[]{:S(2)}, u32[]{:S(2)}) collective-permute-start(f32[1,8,128]{2,1,0:T(8,128)S(1)} %get-tuple-element.154), channel_id=1, source_target_pairs={{4,0},{8,4},{12,8},{16,12},{20,16},{24,20},{28,24},{32,28},{36,32}... | collective-permute-start | bytes 12296 | tf_op jit(solution)/shard_map/ppermute | solution.py:20
  41.2 11.8 %collective-permute-start.5 = (f32[1,32,512]{2,1,0:T(8,128)}, f32[1,32,512]{2,1,0:T(8,128)S(1)}, u32[]{:S(2)}, u32[]{:S(2)}) collective-permute-start(f32[1,32,512]{2,1,0:T(8,128)} %get-tuple-element.92), channel_id=1, source_target_pairs={{4,0},{8,4},{12,8},{16,12},{20,16},{24,20},{28,24},{32,28},{36,32}... | collective-permute-start | bytes 196616 | tf_op jit(solution)/shard_map/ppermute | solution.py:20
  56.2 214.3 %all-gather.1 = f32[128,1,256]{2,1,0:T(1,128)S(1)} all-gather(f32[1,1,256]{2,1,0:T(1,128)S(1)} %reshape.172), channel_id=1, replica_groups=mesh['gz'=128,'gy'=4] {'gz'}, dimensions={0}, use_global_device_ids=true | all-gather | bytes 132096 | tf_op jit(solution)/shard_map/all_gather | solution.py:211
  270.5 15.4 %all_gather.15 = f32[128,1024]{1,0:T(8,128)S(1)} all-gather(f32[128,256]{1,0:T(8,128)S(1)} %bitcast.62), channel_id=1, replica_groups=mesh['gz'=128,'gy'=4] {'gy'}, dimensions={1}, use_global_device_ids=true | all-gather | bytes 655360 | tf_op jit(solution)/shard_map/all_gather | solution.py:215
  291.1 3.8 collective-permute-start.22
  304.1 11.8 %collective-permute-start.1 = (f32[1,32,512]{2,1,0:T(8,128)}, f32[1,32,512]{2,1,0:T(8,128)S(1)}, u32[]{:S(2)}, u32[]{:S(2)}) collective-permute-start(f32[1,32,512]{2,1,0:T(8,128)} %get-tuple-element.88), channel_id=1, source_target_pairs={{4,0},{8,4},{12,8},{16,12},{20,16},{24,20},{28,24},{32,28},{36,32}... | collective-permute-start | bytes 196616 | tf_op jit(solution)/shard_map/ppermute | solution.py:20
  318.7 3.5 collective-permute-done.14
  330.7 3.2 collective-permute-start.2
  336.7 3.2 collective-permute-start.6
  348.1 11.8 %collective-permute-done.8 = f32[1,32,512]{2,1,0:T(8,128)S(1)} collective-permute-done((f32[1,32,512]{2,1,0:T(8,128)S(1)}, f32[1,32,512]{2,1,0:T(8,128)S(1)}, u32[]{:S(2)}, u32[]{:S(2)}) %collective-permute-start.8) | collective-permute-done | bytes 65568 | tf_op jit(solution)/shard_map/ppermute | solution.py:17
  361.8 4.1 collective-permute-start.10
  367.9 18.1 %reshape.154 = f32[2,2,16,2,256,2]{5,4,3,2,1,0:T(8,128)} reshape(f32[4,32,512]{2,1,0:T(8,128)S(1)} %fusion.68) | data formatting | bytes 524288 | tf_op jit(solution)/shard_map/reshape | solution.py:128
  385.9 7.0 reduce_sum.230
  397.4 10.7 %collective-permute-done.16 = f32[1,16,256]{2,1,0:T(8,128)S(1)} collective-permute-done((f32[1,16,256]{2,1,0:T(8,128)S(1)}, f32[1,16,256]{2,1,0:T(8,128)S(1)}, u32[]{:S(2)}, u32[]{:S(2)}) %collective-permute-start.16) | collective-permute-done | bytes 16416 | tf_op jit(solution)/shard_map/ppermute | solution.py:17
  410.1 3.9 collective-permute-start.18
  421.9 10.1 %collective-permute-done.24 = f32[1,8,128]{2,1,0:T(8,128)S(1)} collective-permute-done((f32[1,8,128]{2,1,0:T(8,128)S(1)}, f32[1,8,128]{2,1,0:T(8,128)S(1)}, u32[]{:S(2)}, u32[]{:S(2)}) %collective-permute-start.24) | collective-permute-done | bytes 4128 | tf_op jit(solution)/shard_map/ppermute | solution.py:17
  433.9 3.9 collective-permute-start.26
  439.9 213.4 %all-gather = f32[128,1,256]{2,1,0:T(1,128)S(1)} all-gather(f32[1,1,256]{2,1,0:T(1,128)S(1)} %reshape.170), channel_id=1, replica_groups=mesh['gz'=128,'gy'=4] {'gz'}, dimensions={0}, use_global_device_ids=true | all-gather | bytes 132096 | tf_op jit(solution)/shard_map/all_gather | solution.py:210
  653.3 15.1 %all_gather.13 = f32[128,1024]{1,0:T(8,128)S(1)} all-gather(f32[128,256]{1,0:T(8,128)S(1)} %bitcast.63), channel_id=1, replica_groups=mesh['gz'=128,'gy'=4] {'gy'}, dimensions={1}, use_global_device_ids=true | all-gather | bytes 655360 | tf_op jit(solution)/shard_map/all_gather | solution.py:214
  722.0 11.1 %collective-permute-done.28 = f32[1,8,128]{2,1,0:T(8,128)S(1)} collective-permute-done((f32[1,8,128]{2,1,0:T(8,128)S(1)}, f32[1,8,128]{2,1,0:T(8,128)S(1)}, u32[]{:S(2)}, u32[]{:S(2)}) %collective-permute-start.28) | collective-permute-done | bytes 4128 | tf_op jit(solution)/shard_map/ppermute | solution.py:17
  733.1 3.8 collective-permute-start.31
  747.6 10.6 %collective-permute-done.32 = f32[1,8,128]{2,1,0:T(8,128)S(1)} collective-permute-done((f32[1,8,128]{2,1,0:T(8,128)S(1)}, f32[1,8,128]{2,1,0:T(8,128)S(1)}, u32[]{:S(2)}, u32[]{:S(2)}) %collective-permute-start.32) | collective-permute-done | bytes 4128 | tf_op jit(solution)/shard_map/ppermute | solution.py:17
  760.6 3.5 collective-permute-start.35
  771.6 10.8 %collective-permute-done.36 = f32[1,16,256]{2,1,0:T(8,128)S(1)} collective-permute-done((f32[1,16,256]{2,1,0:T(8,128)S(1)}, f32[1,16,256]{2,1,0:T(8,128)S(1)}, u32[]{:S(2)}, u32[]{:S(2)}) %collective-permute-start.36) | collective-permute-done | bytes 16416 | tf_op jit(solution)/shard_map/ppermute | solution.py:17
  782.4 3.5 collective-permute-start.39
  796.8 10.8 %collective-permute-done.40 = f32[1,16,256]{2,1,0:T(8,128)S(1)} collective-permute-done((f32[1,16,256]{2,1,0:T(8,128)S(1)}, f32[1,16,256]{2,1,0:T(8,128)S(1)}, u32[]{:S(2)}, u32[]{:S(2)}) %collective-permute-start.40) | collective-permute-done | bytes 16416 | tf_op jit(solution)/shard_map/ppermute | solution.py:17
  809.9 3.5 collective-permute-start.43
  822.3 12.5 %collective-permute-done.44 = f32[1,32,512]{2,1,0:T(8,128)S(1)} collective-permute-done((f32[1,32,512]{2,1,0:T(8,128)S(1)}, f32[1,32,512]{2,1,0:T(8,128)S(1)}, u32[]{:S(2)}, u32[]{:S(2)}) %collective-permute-start.44) | collective-permute-done | bytes 65568 | tf_op jit(solution)/shard_map/ppermute | solution.py:17
  834.9 3.6 collective-permute-start.47
  840.8 3.3 collective-permute-done.46
  (305 shorter events, 147.9 us)
Async XLA Ops:
  27.2 262.0 %collective-permute-start.21 = (f32[1,8,128]{2,1,0:T(8,128)S(1)}, f32[1,8,128]{2,1,0:T(8,128)S(1)}, u32[]{:S(2)}, u32[]{:S(2)}) collective-permute-start(f32[1,8,128]{2,1,0:T(8,128)S(1)} %get-tuple-element.154), channel_id=1, source_target_pairs={{4,0},{8,4},{12,8},{16,12},{20,16},{24,20},{28,24},{32,28},{36,32}... | collective-permute-start | bytes 12296 | tf_op jit(solution)/shard_map/ppermute | solution.py:20
  36.7 254.4 %collective-permute-start.20 = (f32[1,8,128]{2,1,0:T(8,128)S(1)}, f32[1,8,128]{2,1,0:T(8,128)S(1)}, u32[]{:S(2)}, u32[]{:S(2)}) collective-permute-start(f32[1,8,128]{2,1,0:T(8,128)S(1)} %get-tuple-element.154), channel_id=1, source_target_pairs={{0,4},{4,8},{8,12},{12,16},{16,20},{20,24},{24,28},{28,32},{32,36}... | collective-permute-start | bytes 12296 | tf_op jit(solution)/shard_map/ppermute | solution.py:17
  39.3 294.6 %collective-permute-start.4 = (f32[1,32,512]{2,1,0:T(8,128)}, f32[1,32,512]{2,1,0:T(8,128)S(1)}, u32[]{:S(2)}, u32[]{:S(2)}) collective-permute-start(f32[1,32,512]{2,1,0:T(8,128)} %get-tuple-element.93), channel_id=1, source_target_pairs={{0,4},{4,8},{8,12},{12,16},{16,20},{20,24},{24,28},{28,32},{32,36}... | collective-permute-start | bytes 196616 | tf_op jit(solution)/shard_map/ppermute | solution.py:17
  41.2 292.8 %collective-permute-start.5 = (f32[1,32,512]{2,1,0:T(8,128)}, f32[1,32,512]{2,1,0:T(8,128)S(1)}, u32[]{:S(2)}, u32[]{:S(2)}) collective-permute-start(f32[1,32,512]{2,1,0:T(8,128)} %get-tuple-element.92), channel_id=1, source_target_pairs={{4,0},{8,4},{12,8},{16,12},{20,16},{24,20},{28,24},{32,28},{36,32}... | collective-permute-start | bytes 196616 | tf_op jit(solution)/shard_map/ppermute | solution.py:20
  53.7 274.3 %collective-permute-start = (f32[1,32,512]{2,1,0:T(8,128)}, f32[1,32,512]{2,1,0:T(8,128)S(1)}, u32[]{:S(2)}, u32[]{:S(2)}) collective-permute-start(f32[1,32,512]{2,1,0:T(8,128)} %get-tuple-element.89), channel_id=1, source_target_pairs={{0,4},{4,8},{8,12},{12,16},{16,20},{20,24},{24,28},{28,32},{32,36}... | collective-permute-start | bytes 196616 | tf_op jit(solution)/shard_map/ppermute | solution.py:17
  289.2 15.0 %collective-permute-start.13 = (f32[1,16,256]{2,1,0:T(8,128)S(1)}, f32[1,16,256]{2,1,0:T(8,128)S(1)}, u32[]{:S(2)}, u32[]{:S(2)}) collective-permute-start(f32[1,16,256]{2,1,0:T(8,128)S(1)} %get-tuple-element.123), channel_id=1, source_target_pairs={{4,0},{8,4},{12,8},{16,12},{20,16},{24,20},{28,24},{32,28},{36,32}... | collective-permute-start | bytes 49160 | tf_op jit(solution)/shard_map/ppermute | solution.py:20
  302.1 13.9 %collective-permute-start.12 = (f32[1,16,256]{2,1,0:T(8,128)S(1)}, f32[1,16,256]{2,1,0:T(8,128)S(1)}, u32[]{:S(2)}, u32[]{:S(2)}) collective-permute-start(f32[1,16,256]{2,1,0:T(8,128)S(1)} %get-tuple-element.122), channel_id=1, source_target_pairs={{0,4},{4,8},{8,12},{12,16},{16,20},{20,24},{24,28},{28,32},{32,36}... | collective-permute-start | bytes 49160 | tf_op jit(solution)/shard_map/ppermute | solution.py:17
  304.1 23.9 %collective-permute-start.1 = (f32[1,32,512]{2,1,0:T(8,128)}, f32[1,32,512]{2,1,0:T(8,128)S(1)}, u32[]{:S(2)}, u32[]{:S(2)}) collective-permute-start(f32[1,32,512]{2,1,0:T(8,128)} %get-tuple-element.88), channel_id=1, source_target_pairs={{4,0},{8,4},{12,8},{16,12},{20,16},{24,20},{28,24},{32,28},{36,32}... | collective-permute-start | bytes 196616 | tf_op jit(solution)/shard_map/ppermute | solution.py:20
  322.2 5.5 collective-permute-start.15
  328.1 11.8 %collective-permute-start.3 = (f32[6,1,512]{2,1,0:T(1,128)S(1)}, f32[6,1,512]{2,1,0:T(1,128)S(1)}, u32[]{:S(2)}, u32[]{:S(2)}) collective-permute-start(f32[6,1,512]{2,1,0:T(1,128)S(1)} %get-tuple-element.41), channel_id=1, source_target_pairs={{1,0},{2,1},{3,2},{5,4},{6,5},{7,6},{9,8},{10,9},{11,10},{13,12},{... | collective-permute-start | bytes 36872 | tf_op jit(solution)/shard_map/ppermute | solution.py:20
  330.7 9.2 %collective-permute-start.2 = (f32[6,1,512]{2,1,0:T(1,128)S(1)}, f32[6,1,512]{2,1,0:T(1,128)S(1)}, u32[]{:S(2)}, u32[]{:S(2)}) collective-permute-start(f32[6,1,512]{2,1,0:T(1,128)S(1)} %get-tuple-element.40), channel_id=1, source_target_pairs={{0,1},{1,2},{2,3},{4,5},{5,6},{6,7},{8,9},{9,10},{10,11},{12,13},{... | collective-permute-start | bytes 36872 | tf_op jit(solution)/shard_map/ppermute | solution.py:17
  334.1 6.4 collective-permute-start.7
  336.7 5.6 collective-permute-start.6
  345.6 14.3 %collective-permute-start.8 = (f32[1,32,512]{2,1,0:T(8,128)S(1)}, f32[1,32,512]{2,1,0:T(8,128)S(1)}, u32[]{:S(2)}, u32[]{:S(2)}) collective-permute-start(f32[1,32,512]{2,1,0:T(8,128)S(1)} %get-tuple-element.86), channel_id=1, source_target_pairs={{0,4},{4,8},{8,12},{12,16},{16,20},{20,24},{24,28},{28,32},{32,36}... | collective-permute-start | bytes 196616 | tf_op jit(solution)/shard_map/ppermute | solution.py:17
  359.9 6.1 collective-permute-start.11
  361.8 5.6 collective-permute-start.10
  395.0 13.2 %collective-permute-start.16 = (f32[1,16,256]{2,1,0:T(8,128)S(1)}, f32[1,16,256]{2,1,0:T(8,128)S(1)}, u32[]{:S(2)}, u32[]{:S(2)}) collective-permute-start(f32[1,16,256]{2,1,0:T(8,128)S(1)} %get-tuple-element.120), channel_id=1, source_target_pairs={{0,4},{4,8},{8,12},{12,16},{16,20},{20,24},{24,28},{28,32},{32,36}... | collective-permute-start | bytes 49160 | tf_op jit(solution)/shard_map/ppermute | solution.py:17
  408.2 5.9 collective-permute-start.19
  418.9 13.1 %collective-permute-start.24 = (f32[1,8,128]{2,1,0:T(8,128)S(1)}, f32[1,8,128]{2,1,0:T(8,128)S(1)}, u32[]{:S(2)}, u32[]{:S(2)}) collective-permute-start(f32[1,8,128]{2,1,0:T(8,128)S(1)} %bitcast_divide_fusion), channel_id=1, source_target_pairs={{0,4},{4,8},{8,12},{12,16},{16,20},{20,24},{24,28},{28,32},{32,36}... | collective-permute-start | bytes 12296 | tf_op jit(solution)/shard_map/ppermute | solution.py:17
  432.0 5.9 collective-permute-start.27
  720.0 13.1 %collective-permute-start.28 = (f32[1,8,128]{2,1,0:T(8,128)S(1)}, f32[1,8,128]{2,1,0:T(8,128)S(1)}, u32[]{:S(2)}, u32[]{:S(2)}) collective-permute-start(f32[1,8,128]{2,1,0:T(8,128)S(1)} %add.461), channel_id=1, source_target_pairs={{0,4},{4,8},{8,12},{12,16},{16,20},{20,24},{24,28},{28,32},{32,36}... | collective-permute-start | bytes 12296 | tf_op jit(solution)/shard_map/ppermute | solution.py:17
  733.1 6.2 collective-permute-start.31
  745.1 13.1 %collective-permute-start.32 = (f32[1,8,128]{2,1,0:T(8,128)S(1)}, f32[1,8,128]{2,1,0:T(8,128)S(1)}, u32[]{:S(2)}, u32[]{:S(2)}) collective-permute-start(f32[1,8,128]{2,1,0:T(8,128)S(1)} %fusion.187), channel_id=1, source_target_pairs={{0,4},{4,8},{8,12},{12,16},{16,20},{20,24},{24,28},{28,32},{32,36}... | collective-permute-start | bytes 12296 | tf_op jit(solution)/shard_map/ppermute | solution.py:17
  758.2 5.9 collective-permute-start.34
  769.2 13.2 %collective-permute-start.36 = (f32[1,16,256]{2,1,0:T(8,128)S(1)}, f32[1,16,256]{2,1,0:T(8,128)S(1)}, u32[]{:S(2)}, u32[]{:S(2)}) collective-permute-start(f32[1,16,256]{2,1,0:T(8,128)S(1)} %get-tuple-element.116), channel_id=1, source_target_pairs={{0,4},{4,8},{8,12},{12,16},{16,20},{20,24},{24,28},{28,32},{32,36}... | collective-permute-start | bytes 49160 | tf_op jit(solution)/shard_map/ppermute | solution.py:17
  782.4 5.9 collective-permute-start.39
  785.9 5.5 collective-permute-start.38
  794.3 13.2 %collective-permute-start.40 = (f32[1,16,256]{2,1,0:T(8,128)S(1)}, f32[1,16,256]{2,1,0:T(8,128)S(1)}, u32[]{:S(2)}, u32[]{:S(2)}) collective-permute-start(f32[1,16,256]{2,1,0:T(8,128)S(1)} %get-tuple-element.114), channel_id=1, source_target_pairs={{0,4},{4,8},{8,12},{12,16},{16,20},{20,24},{24,28},{28,32},{32,36}... | collective-permute-start | bytes 49160 | tf_op jit(solution)/shard_map/ppermute | solution.py:17
  807.6 5.9 collective-permute-start.42
  819.9 15.0 %collective-permute-start.44 = (f32[1,32,512]{2,1,0:T(8,128)S(1)}, f32[1,32,512]{2,1,0:T(8,128)S(1)}, u32[]{:S(2)}, u32[]{:S(2)}) collective-permute-start(f32[1,32,512]{2,1,0:T(8,128)S(1)} %get-tuple-element.44), channel_id=1, source_target_pairs={{0,4},{4,8},{8,12},{12,16},{16,20},{20,24},{24,28},{28,32},{32,36}... | collective-permute-start | bytes 196616 | tf_op jit(solution)/shard_map/ppermute | solution.py:17
  834.9 5.9 collective-permute-start.47
  838.5 5.6 collective-permute-start.46
  (40 other events, 1924.2 us)
where the time goes:
time: 849 us; the launch traced here: 846 us
  blocking collectives  458 us (54%)
  starting transfers between devices  147 us (17%)
  waiting for transfers between devices  119 us (14%)
  other arithmetic  53.1 us (6%)
  local copies, waits for them, and re-layouts  47.8 us (6%)
  between operations  21.1 us (2%)
    all_gather x1, blocking collectives, per_device(): lax.all_gather(pair_sum(dens_two), 'gz', axis=0, tiled=True)  214 us
    all_gather x1, blocking collectives, per_device(): lax.all_gather(pair_sum(resid_two), 'gz', axis=0, tiled=True)  213 us
    ppermute x24, waiting for transfers between devices, with_halo(): lax.ppermute(lax.slice_in_dim(block, block.shape[dim] - width, None, axis...  110 us
    ppermute x24, starting transfers between devices, with_halo(): lax.ppermute(lax.slice_in_dim(block, 0, width, axis=dim), axis, backward)  85.1 us
    ppermute x24, starting transfers between devices, with_halo(): lax.ppermute(lax.slice_in_dim(block, block.shape[dim] - width, None, axis...  62.1 us
    reshape x2, local copies, waits for them, and re-layouts, restrict_local(): values.reshape(depth // 2, 2, height // 2, 2, breadth // 2, 2)  37 us
    reduce_sum x15, other arithmetic, coarse_total(): return jnp.sum(values)  21.8 us
  transfers between devices with their start and end apart: 48, of which 21 were waited for; matrix products, arithmetic and copies ran while one was open for 1% of the time, Pallas kernels for 0%

commit v1 on v0

v1 whole, which is shorter than its diff:
```python
import functools

import jax
import jax.numpy as jnp
from jax import lax
from jax.experimental import pallas as pl
from jax.experimental.pallas import tpu as pltpu
from jax.sharding import PartitionSpec as P

MESH = pl.DeviceIdType.MESH
SWEEPS = 8
OMEGA = 0.8
F32 = jnp.float32
PAD = 8


def dot(a, b):
    return jnp.dot(a, b, precision=lax.Precision.HIGHEST, preferred_element_type=F32)


def twice_inverse(total):
    guess = pltpu.reciprocal(total, approx=True)
    return guess * (4.0 - 2.0 * total * guess)


def iota(shape, axis):
    return lax.broadcasted_iota(jnp.int32, shape, axis)


def pair_matrix(fine):
    rows, cols = iota((fine, fine // 2), 0), iota((fine, fine // 2), 1)
    return jnp.where(rows // 2 == cols, 1.0, 0.0).astype(F32)


def spread_matrix(coarse):
    rows, cols = iota((coarse, 2 * coarse), 0), iota((coarse, 2 * coarse), 1)
    parent = cols // 2
    near = parent + 2 * (cols % 2) - 1
    return (jnp.where(rows == parent, 0.75, 0.0) + jnp.where(rows == near, 0.25, 0.0)).astype(F32)


def padded_spread_matrix(coarse):
    shape = (2 * coarse + 2 * PAD, coarse + 2 * PAD)
    rows, cols = iota(shape, 0), iota(shape, 1)
    parent = rows // 2 + PAD // 2
    near = parent + 2 * (rows % 2) - 1
    return (jnp.where(cols == parent, 0.75, 0.0) + jnp.where(cols == near, 0.25, 0.0)).astype(F32)


class Level:
    def __init__(self, shape, chunk, rho, bx, by, bz, dg, idg):
        self.planes, self.rows, self.cols = shape
        self.chunk = chunk
        self.rho, self.bx, self.by, self.bz, self.dg, self.idg = rho, bx, by, bz, dg, idg

    def chunks(self):
        return [(r, self.chunk) for r in range(0, self.rows, self.chunk)]

    def faces_x(self, plane):
        n = self.cols
        for r, m in self.chunks():
            rho = self.rho[plane + 1, PAD + r : PAD + r + m, :]
            lane = iota((m, n), 1)
            low = twice_inverse(rho + jnp.where(lane == 0, rho, pltpu.roll(rho, 1, 1)))
            high = jnp.where(lane == n - 1, twice_inverse(rho + rho), pltpu.roll(low, n - 1, 1))
            self.dg[plane, r : r + m, :] = low + high
            self.bx[plane, r : r + m, :] = jnp.where(lane == 0, 0.0, low)

    def faces_y(self, plane):
        for r, m in self.chunks():
            low = self.rho[plane + 1, PAD - 1 + r : PAD - 1 + r + m, :]
            high = self.rho[plane + 1, PAD + r : PAD + r + m, :]
            self.by[plane, r : r + m, :] = twice_inverse(low + high)
        end = PAD + self.rows
        low = self.rho[plane + 1, end - 1 : end, :]
        high = self.rho[plane + 1, end : end + 1, :]
        self.by[plane, self.rows : self.rows + 1, :] = twice_inverse(low + high)

    def faces_z(self, face):
        for r, m in self.chunks():
            low = self.rho[face, PAD + r : PAD + r + m, :]
            high = self.rho[face + 1, PAD + r : PAD + r + m, :]
            self.bz[face, r : r + m, :] = twice_inverse(low + high)

    def diagonal(self, plane):
        for r, m in self.chunks():
            total = self.dg[plane, r : r + m, :]
            total = total + self.by[plane, r : r + m, :] + self.by[plane, r + 1 : r + 1 + m, :]
            total = total + self.bz[plane, r : r + m, :] + self.bz[plane + 1, r : r + m, :]
            self.dg[plane, r : r + m, :] = total
            self.idg[plane, r : r + m, :] = (0.5 * OMEGA) * twice_inverse(total)

    def mask_y(self, plane, low, high):
        self.by[plane, 0:1, :] = self.by[plane, 0:1, :] * low
        self.by[plane, self.rows : self.rows + 1, :] = self.by[plane, self.rows : self.rows + 1, :] * high

    def mask_z(self, low, high):
        self.bz[0] = self.bz[0] * low
        self.bz[self.planes] = self.bz[self.planes] * high

    def neighbours(self, val, plane, r, m):
        n = self.cols
        rows = slice(PAD + r, PAD + r + m)
        here = val[plane + 1, rows, :]
        bx = self.bx[plane, r : r + m, :]
        total = self.bz[plane, r : r + m, :] * val[plane, rows, :]
        total = total + self.bz[plane + 1, r : r + m, :] * val[plane + 2, rows, :]
        total = total + self.by[plane, r : r + m, :] * val[plane + 1, PAD - 1 + r : PAD - 1 + r + m, :]
        total = total + self.by[plane, r + 1 : r + 1 + m, :] * val[plane + 1, PAD + 1 + r : PAD + 1 + r + m, :]
        total = total + bx * pltpu.roll(here, 1, 1)
        total = total + pltpu.roll(bx * here, n - 1, 1)
        return here, total


def kernel(
    dens_in, right_in, guess_in, out,
    rho0, val0, smo0, src0, res0, bx0, by0, bz0, dg0, idg0,
    rho1, val1, up1, src1, res1, bx1, by1, bz1, dg1, idg1,
    rho2, val2, up2, src2, res2, bx2, by2, bz2, dg2, idg2,
    rows_out, rows_in, message, inbox_dens, inbox_src, tile, wide_dens, wide_src,
    rho3, bx3, by3, bz3, dg3, dir3, res3, img3, cor3, pair_tmp,
    local_sem, send_sem, recv_sem,
):
    gz, gy = lax.axis_index("gz"), lax.axis_index("gy")
    nz, ny = 128, 4
    core, ypos, xpos, zhi = gz % 2, (gz // 2) % 4, (gz // 8) % 4, gz // 32
    zpos = zhi * 4 + gy

    def gz_of(zh, x, y, c):
        return ((zh * 4 + x) * 4 + y) * 2 + c

    up_z, down_z = (gz + 1) % nz, (gz + nz - 1) % nz
    up_y, down_y = (gy + 1) % ny, (gy + ny - 1) % ny
    column = []
    for d in range(16):
        for k in range(2):
            if d or k:
                z = (zpos + d) % 16
                column.append((gz_of(z // 4, xpos, ypos, (core + k) % 2), z % 4))
    layer = []
    for i in range(4):
        for j in range(4):
            if i or j:
                layer.append((gz_of(zhi, (xpos + i) % 4, (ypos + j) % 4, core), gy))
    faces = [(up_z, gy), (down_z, gy), (gz, up_y), (gz, down_y)]
    corners = [(up_z, up_y), (up_z, down_y), (down_z, up_y), (down_z, down_y)]
    greeted = faces + corners + column + layer

    barrier = pltpu.get_barrier_semaphore()
    for device in greeted:
        pl.semaphore_signal(barrier, inc=1, device_id=device, device_id_type=MESH)

    local = []
    for i, (source, target) in enumerate(
        ((dens_in, rho0.at[1:5, 8:40, :]), (guess_in, val0.at[1:5, 8:40, :]), (right_in, src0))
    ):
        copy = pltpu.make_async_copy(source, target, local_sem.at[i])
        copy.start()
        local.append(copy)

    count = [0]

    def send(source, target, device):
        i = count[0]
        count[0] = i + 1
        copy = pltpu.make_async_remote_copy(
            src_ref=source, dst_ref=target, send_sem=send_sem.at[i], recv_sem=recv_sem.at[i],
            device_id=device, device_id_type=MESH,
        )
        copy.start()
        return copy

    def wait_recv(copies):
        for copy in copies:
            copy.wait_recv()

    def wait_send(copies):
        for copy in copies:
            copy.wait_send()

    fine = Level((4, 32, 512), 8, rho0, bx0, by0, bz0, dg0, idg0)
    middle = Level((2, 16, 256), 16, rho1, bx1, by1, bz1, dg1, idg1)
    coarse = Level((1, 8, 128), 8, rho2, bx2, by2, bz2, dg2, idg2)

    z_low = jnp.where(gz > 0, 1.0, 0.0).astype(F32)
    z_high = jnp.where(gz < nz - 1, 1.0, 0.0).astype(F32)
    y_low = jnp.where(gy > 0, 1.0, 0.0).astype(F32)
    y_high = jnp.where(gy < ny - 1, 1.0, 0.0).astype(F32)

    pair_x0, pair_x1 = pair_matrix(512), pair_matrix(256)
    pair_y0 = jnp.where(iota((16, 32), 1) // 2 == iota((16, 32), 0), 0.125, 0.0).astype(F32)
    pair_y1 = jnp.where(iota((8, 16), 1) // 2 == iota((8, 16), 0), 0.125, 0.0).astype(F32)

    def restrict0(read):
        return [dot(pair_y0, dot(read(2 * k) + read(2 * k + 1), pair_x0)) for k in range(2)]

    def restrict1(read):
        return dot(pair_y1, dot(read(0) + read(1), pair_x1))

    half_rows, half_cols = iota((128, 256), 0), iota((128, 256), 1)
    to_halves = jnp.where((half_cols % 64 == half_rows // 2) & ((half_cols < 64) | (half_cols >= 192)), 0.125, 0.0).astype(F32)

    def pack_message(field, value):
        pair_tmp[...] = dot(value, to_halves)
        for r in range(2):
            t = 4 * r
            message[field, r : r + 1, :] = (
                pair_tmp[t : t + 1, 0:128] + pair_tmp[t + 1 : t + 2, 0:128]
                + pair_tmp[t + 2 : t + 3, 128:256] + pair_tmp[t + 3 : t + 4, 128:256]
            )

    def gather_column(field, inbox):
        inbox[zhi, core, gy] = message[field]
        return [send(message.at[field], inbox.at[zhi, core, gy], device) for device in column]

    def gather_layer(field, inbox, wide):
        for zh in range(4):
            for y in range(4):
                tile[field, zh, 2 * y : 2 * y + 2, :] = inbox[zh, 0, y] + inbox[zh, 1, y]
        slot = xpos * 4 + ypos
        wide[slot] = tile[field]
        return [send(tile.at[field], wide.at[slot], device) for device in layer]

    local[0].wait()
    own1 = restrict0(lambda k: rho0[k + 1, 8:40, :])
    for k in range(2):
        rho1[k + 1, 8:24, :] = own1[k]
    own2 = restrict1(lambda k: own1[k])
    rho2[1, 8:16, :] = own2
    pack_message(0, own2)
    local[1].wait()
    for k in range(4):
        for f, ref in ((0, rho0), (1, val0)):
            rows_out[0, f, k : k + 1, :] = ref[k + 1, 39:40, :]
            rows_out[1, f, k : k + 1, :] = ref[k + 1, 8:9, :]

    pl.semaphore_wait(barrier, len(greeted))

    z_dens = [
        send(rho0.at[4, 8:40, :], rho0.at[0, 8:40, :], faces[0]),
        send(rho0.at[1, 8:40, :], rho0.at[5, 8:40, :], faces[1]),
    ]
    z_vals = [
        send(val0.at[4, 8:40, :], val0.at[0, 8:40, :], faces[0]),
        send(val0.at[1, 8:40, :], val0.at[5, 8:40, :], faces[1]),
    ]
    y_both = [
        send(rows_out.at[0, 0:2], rows_in.at[0, 0:2], faces[2]),
        send(rows_out.at[1, 0:2], rows_in.at[1, 0:2], faces[3]),
    ]

    def trade(ref, planes, rows):
        top = PAD + rows
        return [
            send(ref.at[planes, 8:top, :], ref.at[0, 8:top, :], faces[0]),
            send(ref.at[1, 8:top, :], ref.at[planes + 1, 8:top, :], faces[1]),
            send(ref.at[1 : planes + 1, rows : rows + 8, :], ref.at[1 : planes + 1, 0:8, :], faces[2]),
            send(ref.at[1 : planes + 1, 8:16, :], ref.at[1 : planes + 1, top : top + 8, :], faces[3]),
        ]

    dens1_copies = trade(rho1, 2, 16)
    dens2_copies = trade(rho2, 1, 8)
    column_dens = gather_column(0, inbox_dens)

    def fill_y(ref, planes, rows):
        top = PAD + rows
        for k in range(1, planes + 1):
            ref[k, 7:8, :] = jnp.where(gy == 0, ref[k, 8:9, :], ref[k, 7:8, :])
            ref[k, top : top + 1, :] = jnp.where(gy == ny - 1, ref[k, top - 1 : top, :], ref[k, top : top + 1, :])

    def fill_z(ref, planes, rows):
        top = PAD + rows
        ref[0, 8:top, :] = jnp.where(gz == 0, ref[1, 8:top, :], ref[0, 8:top, :])
        ref[planes + 1, 8:top, :] = jnp.where(gz == nz - 1, ref[planes, 8:top, :], ref[planes + 1, 8:top, :])

    for k in range(4):
        fine.faces_x(k)
    for face in (1, 2, 3):
        fine.faces_z(face)
    wait_recv(y_both)
    for k in range(4):
        for f, ref in ((0, rho0), (1, val0)):
            ref[k + 1, 7:8, :] = rows_in[0, f, k : k + 1, :]
            ref[k + 1, 40:41, :] = rows_in[1, f, k : k + 1, :]
    fill_y(rho0, 4, 32)
    for k in range(4):
        fine.faces_y(k)
    local[2].wait()

    def smooth(plane):
        for r, m in fine.chunks():
            here, near = fine.neighbours(val0, plane, r, m)
            smo0[plane + 1, 8 + r : 8 + r + m, :] = (1.0 - OMEGA) * here + (
                src0[plane, r : r + m, :] + near
            ) * fine.idg[plane, r : r + m, :]

    for k in (1, 2):
        fine.diagonal(k)
        fine.mask_y(k, y_low, y_high)
        smooth(k)
    wait_recv(z_dens)
    fill_z(rho0, 4, 32)
    for face in (0, 4):
        fine.faces_z(face)
    for k in (0, 3):
        fine.diagonal(k)
        fine.mask_y(k, y_low, y_high)
    fine.mask_z(z_low, z_high)
    wait_recv(z_vals)
    smooth(3)
    z_smooth = [send(smo0.at[4, 8:40, :], smo0.at[0, 8:40, :], faces[0])]
    smooth(0)
    z_smooth.append(send(smo0.at[1, 8:40, :], smo0.at[5, 8:40, :], faces[1]))
    for k in range(4):
        rows_out[0, 2, k : k + 1, :] = smo0[k + 1, 39:40, :]
        rows_out[1, 2, k : k + 1, :] = smo0[k + 1, 8:9, :]
    y_smooth = [
        send(rows_out.at[0, 2], rows_in.at[0, 2], faces[2]),
        send(rows_out.at[1, 2], rows_in.at[1, 2], faces[3]),
    ]

    def coefficients(level, copies):
        wait_recv(copies)
        fill_y(level.rho, level.planes, level.rows)
        fill_z(level.rho, level.planes, level.rows)
        for k in range(level.planes):
            level.faces_x(k)
            level.faces_y(k)
        for k in range(level.planes + 1):
            level.faces_z(k)
        for k in range(level.planes):
            level.diagonal(k)
            level.mask_y(k, y_low, y_high)
        level.mask_z(z_low, z_high)

    wait_recv(column_dens)
    layer_dens = gather_layer(0, inbox_dens, wide_dens)
    coefficients(middle, dens1_copies)
    coefficients(coarse, dens2_copies)

    wait_recv(y_smooth)
    for k in range(4):
        smo0[k + 1, 7:8, :] = rows_in[0, 2, k : k + 1, :]
        smo0[k + 1, 40:41, :] = rows_in[1, 2, k : k + 1, :]

    def residual(plane):
        for r, m in fine.chunks():
            here, near = fine.neighbours(smo0, plane, r, m)
            res0[plane, r : r + m, :] = src0[plane, r : r + m, :] - fine.dg[plane, r : r + m, :] * here + near

    for k in (1, 2):
        residual(k)
    wait_recv(z_smooth)
    for k in (0, 3):
        residual(k)

    source1 = restrict0(lambda k: res0[k])
    for k in range(2):
        src1[k] = source1[k]
        val1[k + 1, 8:24, :] = 4.0 * source1[k] * middle.idg[k]
    copies1 = trade(val1, 2, 16)

    wait_recv(layer_dens)
    lane, sub = iota((8, 128), 1), iota((8, 128), 0)
    right_half = lane >= 64
    first_x, last_x = (lane % 64) == 0, (lane % 64) == 63
    first_y, last_y = (lane < 64) & (sub == 0), (lane >= 64) & (sub == 7)

    def lower_y(v):
        q = pltpu.roll(v, 64, 1)
        return jnp.where(right_half, q, pltpu.roll(q, 1, 0))

    def upper_y(v):
        q = pltpu.roll(v, 64, 1)
        return jnp.where(right_half, pltpu.roll(q, 7, 0), q)

    scale3 = 0.015625
    for zh in range(4):
        for s in range(16):
            rho3[1 + 16 * zh + s] = wide_dens[s, zh]
    rho3[0] = rho3[1]
    rho3[65] = rho3[64]

    def face3(k, _):
        bz3[k] = scale3 * twice_inverse(rho3[k] + rho3[k + 1])
        return 0

    lax.fori_loop(0, 65, face3, 0)

    def coef3(k, _):
        rho = rho3[k + 1]
        edge = twice_inverse(rho + rho)
        low = twice_inverse(rho + jnp.where(first_x, rho, pltpu.roll(rho, 1, 1)))
        total = low + jnp.where(last_x, edge, pltpu.roll(low, 127, 1))
        bx3[k] = jnp.where(first_x, 0.0, scale3 * low)
        low = twice_inverse(rho + jnp.where(first_y, rho, lower_y(rho)))
        total = total + low + jnp.where(last_y, edge, upper_y(low))
        by3[k] = jnp.where(first_y, 0.0, scale3 * low)
        dg3[k] = scale3 * total + bz3[k] + bz3[k + 1]
        return 0

    lax.fori_loop(0, 64, coef3, 0, unroll=4)

    wait_recv(copies1)

    def residual1(k):
        here, near = middle.neighbours(val1, k, 0, 16)
        return (1.0 - OMEGA) * src1[k] + 0.25 * near

    source2 = restrict1(residual1)
    src2[0] = source2
    val2[1, 8:16, :] = 16.0 * source2 * coarse.idg[0]
    copies2 = trade(val2, 1, 8)
    wait_recv(copies2)
    here, near = coarse.neighbours(val2, 0, 0, 8)
    pack_message(1, (1.0 - OMEGA) * source2 + 0.0625 * near)
    column_src = gather_column(1, inbox_src)
    wait_recv(column_src)
    layer_src = gather_layer(1, inbox_src, wide_src)
    wait_recv(layer_src)

    zero_plane = jnp.zeros((8, 128), F32)
    dir3[0] = zero_plane
    dir3[65] = zero_plane
    for k in (0, 1, 66, 67):
        cor3[k] = zero_plane
    total = zero_plane
    for zh in range(4):
        for s in range(16):
            v = wide_src[s, zh]
            k = 16 * zh + s
            dir3[k + 1] = v
            res3[k] = v
            cor3[k + 2] = zero_plane
            total = total + v * v

    def whole(v):
        return jnp.sum(jnp.sum(v, axis=0, keepdims=True), axis=1, keepdims=True)

    def sweep(step, norm):
        def apply(k, acc):
            v = dir3[k + 1]
            bx, by = bx3[k], by3[k]
            image = dg3[k] * v - bz3[k] * dir3[k] - bz3[k + 1] * dir3[k + 2]
            image = image - by * lower_y(v) - upper_y(by * v)
            image = image - bx * pltpu.roll(v, 1, 1) - pltpu.roll(bx * v, 127, 1)
            img3[k] = image
            return acc + v * image

        bottom = whole(lax.fori_loop(0, 64, apply, zero_plane, unroll=16))
        alpha = norm / bottom

        def advance(k, acc):
            cor3[k + 2] = cor3[k + 2] + alpha * dir3[k + 1]
            r = res3[k] - alpha * img3[k]
            res3[k] = r
            return acc + r * r

        norm_next = whole(lax.fori_loop(0, 64, advance, zero_plane, unroll=16))
        beta = norm_next / norm

        def turn(k, _):
            dir3[k + 1] = res3[k] + beta * dir3[k + 1]
            return 0

        lax.fori_loop(0, 64, turn, 0, unroll=16)
        return norm_next

    lax.fori_loop(0, SWEEPS, sweep, whole(total))

    spread_rows, spread_cols = iota((128, 256), 0), iota((128, 256), 1)
    fine_x = spread_cols % 128
    parent = fine_x // 2
    near = parent + 2 * (fine_x % 2) - 1
    half = spread_cols // 128
    inside = (near >= 0) & (near < 64)
    from_halves = (
        jnp.where(spread_rows == parent + 64 * half, 0.75, 0.0)
        + jnp.where((spread_rows == near + 64 * half) & inside, 0.25, 0.0)
    ).astype(F32)
    row_at, col_at = iota((24, 16), 0) + 8 * gy - 8, iota((24, 16), 1)
    coarse_y = 2 * (col_at % 8) + col_at // 8
    row_up = row_at + 8
    parent_y = row_up // 2 - 4
    near_y = parent_y + 2 * (row_up % 2) - 1
    rows_from = (
        jnp.where(coarse_y == parent_y, 0.75, 0.0) + jnp.where(coarse_y == near_y, 0.25, 0.0)
    ).astype(F32)
    wait_send(copies2)
    for d in (-1, 0, 1):
        plane = gz + d + 4
        index = plane // 2
        other = index + 2 * (plane % 2) - 1
        mixed = 0.75 * cor3[index] + 0.25 * cor3[other]
        x_done = dot(mixed, from_halves)
        stacked = jnp.concatenate([x_done[:, 0:128], x_done[:, 128:256]], axis=0)
        val2[d + 1] = val2[d + 1] + dot(rows_from, stacked)

    here, near = coarse.neighbours(val2, 0, 0, 8)
    up2[1, 8:16, :] = (1.0 - OMEGA) * here + (16.0 * src2[0] + near) * coarse.idg[0]

    def trade_all(ref, planes, rows):
        top = PAD + rows
        copies = trade(ref, planes, rows)
        lowest, highest = slice(8, 16), slice(rows, rows + 8)
        copies.append(send(ref.at[planes, highest, :], ref.at[0, 0:8, :], corners[0]))
        copies.append(send(ref.at[planes, lowest, :], ref.at[0, top : top + 8, :], corners[1]))
        copies.append(send(ref.at[1, highest, :], ref.at[planes + 1, 0:8, :], corners[2]))
        copies.append(send(ref.at[1, lowest, :], ref.at[planes + 1, top : top + 8, :], corners[3]))
        return copies

    def clear_outside(ref, planes, rows):
        top = PAD + rows
        for k in range(planes + 2):
            ref[k, 0:8, :] = ref[k, 0:8, :] * y_low
            ref[k, top : top + 8, :] = ref[k, top : top + 8, :] * y_high
        ref[0] = ref[0] * z_low
        ref[planes + 1] = ref[planes + 1] * z_high

    spread_x1, spread_x0 = spread_matrix(128), spread_matrix(256)
    spread_y1, spread_y0 = padded_spread_matrix(8), padded_spread_matrix(16)

    def prolong(ref, planes, target, spread_x, spread_y):
        wide = [dot(spread_y, dot(ref[k], spread_x)) for k in range(planes + 2)]
        for k in range(2 * planes + 2):
            parent_z = (k + 1) // 2
            near_z = parent_z + 1 if k % 2 == 0 else parent_z - 1
            target[k] = target[k] + 0.75 * wide[parent_z] + 0.25 * wide[near_z]

    up2_copies = trade_all(up2, 1, 8)
    wait_recv(up2_copies)
    clear_outside(up2, 1, 8)
    wait_send(copies1)
    prolong(up2, 1, val1, spread_x1, spread_y1)
    for k in range(2):
        here, near = middle.neighbours(val1, k, 0, 16)
        up1[k + 1, 8:24, :] = (1.0 - OMEGA) * here + (4.0 * src1[k] + near) * middle.idg[k]
    up1_copies = trade_all(up1, 2, 16)
    wait_recv(up1_copies)
    clear_outside(up1, 2, 16)
    wait_send(z_smooth)
    prolong(up1, 2, smo0, spread_x0, spread_y0)
    for k in range(4):
        for r, m in fine.chunks():
            here, near = fine.neighbours(smo0, k, r, m)
            out[k, r : r + m, :] = (1.0 - OMEGA) * here + (src0[k, r : r + m, :] + near) * fine.idg[k, r : r + m, :]

    wait_send(
        z_dens + z_vals + y_both + dens1_copies + dens2_copies + column_dens + y_smooth + layer_dens
        + column_src + layer_src + up2_copies + up1_copies
    )


def level_scratch(planes, rows, cols):
    padded = pltpu.VMEM((planes + 2, rows + 2 * PAD, cols), F32)
    own = pltpu.VMEM((planes, rows, cols), F32)
    return [
        padded, padded, padded, own, own,
        own, pltpu.VMEM((planes, rows + 8, cols), F32), pltpu.VMEM((planes + 1, rows, cols), F32), own, own,
    ]


COPIES = 6 + 8 + 4 + 4 + 4 + 62 + 30 + 16


def per_device(density, right_side, pressure_guess):
    coarsest = pltpu.VMEM((64, 8, 128), F32)
    return pl.pallas_call(
        kernel,
        out_shape=jax.ShapeDtypeStruct(density.shape, F32),
        in_specs=[pl.BlockSpec(memory_space=pl.ANY)] * 3,
        out_specs=pl.BlockSpec(memory_space=pltpu.VMEM),
        scratch_shapes=[
            *level_scratch(4, 32, 512),
            *level_scratch(2, 16, 256),
            *level_scratch(1, 8, 128),
            pltpu.VMEM((2, 3, 4, 512), F32),
            pltpu.VMEM((2, 3, 4, 512), F32),
            pltpu.VMEM((2, 2, 128), F32),
            pltpu.VMEM((4, 2, 4, 2, 128), F32),
            pltpu.VMEM((4, 2, 4, 2, 128), F32),
            pltpu.VMEM((2, 4, 8, 128), F32),
            pltpu.VMEM((16, 4, 8, 128), F32),
            pltpu.VMEM((16, 4, 8, 128), F32),
            pltpu.VMEM((66, 8, 128), F32),
            coarsest, coarsest, pltpu.VMEM((65, 8, 128), F32), coarsest,
            pltpu.VMEM((66, 8, 128), F32), coarsest, coarsest, pltpu.VMEM((68, 8, 128), F32),
            pltpu.VMEM((8, 256), F32),
            pltpu.SemaphoreType.DMA((3,)),
            pltpu.SemaphoreType.DMA((COPIES,)),
            pltpu.SemaphoreType.DMA((COPIES,)),
        ],
        compiler_params=pltpu.CompilerParams(
            collective_id=0, has_side_effects=True, vmem_limit_bytes=32 * 1024 * 1024
        ),
        cost_estimate=pl.CostEstimate(flops=20_000_000, bytes_accessed=1 << 20, transcendentals=0),
    )(density, right_side, pressure_guess)


def solution(mesh):
    spec = P("gz", "gy", None)
    return jax.shard_map(per_device, mesh=mesh, in_specs=(spec, spec, spec), out_specs=spec, check_vma=False)
```

time: 849 us -> 94.6 us (0.11)
  the two profiles are of different devices: /device:TPU:448 before, /device:TPU:1 now
where the time goes in v1:
time: 94.6 us; the launch traced here: 93.2 us
  Pallas kernels  89.6 us (95%)
  local copies, waits for them, and re-layouts  3.55 us (4%)
    pallas_call x1, Pallas kernels, per_device(): pl.pallas_call(kernel, out_shape=jax.ShapeDtypeStruct(density.shape, F32)...  89.6 us
    unnamed x7, local copies, waits for them, and re-layouts  3.55 us

profile of v1, /device:TPU:1, one launch (start us, length us, event | category | flops | bytes accessed | tf_op | source)
XLA Modules:
  0.0 93.2 jit_solution(10482987612607758046)
XLA Ops:
  0.0 0.0 copy-start
  0.0 0.9 %copy-done = f32[4,32,512]{2,1,0:T(8,128)S(1)} copy-done((f32[4,32,512]{2,1,0:T(8,128)S(1)}, f32[4,32,512]{2,1,0:T(8,128)}, u32[]{:S(2)}) %copy-start) | copy-done | bytes 262168
  1.0 0.0 copy-start.1
  1.0 0.9 %copy-done.1 = f32[4,32,512]{2,1,0:T(8,128)S(1)} copy-done((f32[4,32,512]{2,1,0:T(8,128)S(1)}, f32[4,32,512]{2,1,0:T(8,128)}, u32[]{:S(2)}) %copy-start.1) | copy-done | bytes 262168
  1.9 0.0 copy-start.2
  1.9 0.9 %copy-done.2 = f32[4,32,512]{2,1,0:T(8,128)S(1)} copy-done((f32[4,32,512]{2,1,0:T(8,128)S(1)}, f32[4,32,512]{2,1,0:T(8,128)}, u32[]{:S(2)}) %copy-start.2) | copy-done | bytes 262168
  2.9 89.6 %shard_map.37 = f32[4,32,512]{2,1,0:T(8,128)S(1)} custom-call(f32[4,32,512]{2,1,0:T(8,128)S(1)} %copy-done, f32[4,32,512]{2,1,0:T(8,128)S(1)} %copy-done.1, f32[4,32,512]{2,1,0:T(8,128)S(1)} %copy-done.2), custom_call_target="tpu_custom_call" | custom-call | flops 20000000 | bytes 1048576 | tf_op jit(solution)/shard_map/pallas_call | solution.py:568
  92.5 0.7 copy.5
Async XLA Ops:
  0.0 0.9 %copy-start = (f32[4,32,512]{2,1,0:T(8,128)S(1)}, f32[4,32,512]{2,1,0:T(8,128)}, u32[]{:S(2)}) copy-start(f32[4,32,512]{2,1,0:T(8,128)} %dens_in.1) | copy-start | bytes 786436
  1.0 0.9 %copy-start.1 = (f32[4,32,512]{2,1,0:T(8,128)S(1)}, f32[4,32,512]{2,1,0:T(8,128)}, u32[]{:S(2)}) copy-start(f32[4,32,512]{2,1,0:T(8,128)} %right_in.1) | copy-start | bytes 786436
  1.9 0.9 %copy-start.2 = (f32[4,32,512]{2,1,0:T(8,128)S(1)}, f32[4,32,512]{2,1,0:T(8,128)}, u32[]{:S(2)}) copy-start(f32[4,32,512]{2,1,0:T(8,128)} %guess_in.1) | copy-start | bytes 786436

commit v2 on v1

--- a/solution.py
+++ b/solution.py
@@ -90,13 +90,13 @@
             self.dg[plane, r : r + m, :] = total
             self.idg[plane, r : r + m, :] = (0.5 * OMEGA) * twice_inverse(total)
 
-    def mask_y(self, plane, low, high):
-        self.by[plane, 0:1, :] = self.by[plane, 0:1, :] * low
-        self.by[plane, self.rows : self.rows + 1, :] = self.by[plane, self.rows : self.rows + 1, :] * high
-
-    def mask_z(self, low, high):
-        self.bz[0] = self.bz[0] * low
-        self.bz[self.planes] = self.bz[self.planes] * high
+    def mask_y(self, plane, faces):
+        for row, factor in faces:
+            self.by[plane, row : row + 1, :] = self.by[plane, row : row + 1, :] * factor
+
+    def mask_z(self, faces):
+        for face, factor in faces:
+            self.bz[face] = self.bz[face] * factor
 
     def neighbours(self, val, plane, r, m):
         n = self.cols
@@ -115,8 +115,8 @@
 def kernel(
     dens_in, right_in, guess_in, out,
     rho0, val0, smo0, src0, res0, bx0, by0, bz0, dg0, idg0,
-    rho1, val1, up1, src1, res1, bx1, by1, bz1, dg1, idg1,
-    rho2, val2, up2, src2, res2, bx2, by2, bz2, dg2, idg2,
+    rho1, pair1, bx1, by1, bz1, dg1, idg1,
+    rho2, pair2, bx2, by2, bz2, dg2, idg2,
     rows_out, rows_in, message, inbox_dens, inbox_src, tile, wide_dens, wide_src,
     rho3, bx3, by3, bz3, dg3, dir3, res3, img3, cor3, pair_tmp,
     local_sem, send_sem, recv_sem,
@@ -143,8 +143,12 @@
             if i or j:
                 layer.append((gz_of(zhi, (xpos + i) % 4, (ypos + j) % 4, core), gy))
     faces = [(up_z, gy), (down_z, gy), (gz, up_y), (gz, down_y)]
-    corners = [(up_z, up_y), (up_z, down_y), (down_z, up_y), (down_z, down_y)]
-    greeted = faces + corners + column + layer
+    around = []
+    for dz in (1, -1, 2, -2, 3, -3):
+        for dy in (0, 1, -1):
+            around.append((dz, dy, ((gz + dz + nz) % nz, (gy + dy + ny) % ny)))
+    corners = [(dz, dy, device) for dz, dy, device in around if abs(dz) == 1 and dy]
+    greeted = faces[2:] + [device for _, _, device in around] + column + layer
 
     barrier = pltpu.get_barrier_semaphore()
     for device in greeted:
@@ -179,8 +183,9 @@
             copy.wait_send()
 
     fine = Level((4, 32, 512), 8, rho0, bx0, by0, bz0, dg0, idg0)
-    middle = Level((2, 16, 256), 16, rho1, bx1, by1, bz1, dg1, idg1)
-    coarse = Level((1, 8, 128), 8, rho2, bx2, by2, bz2, dg2, idg2)
+    middle = Level((4, 32, 256), 16, rho1, bx1, by1, bz1, dg1, idg1)
+    coarse = Level((5, 24, 128), 24, rho2, bx2, by2, bz2, dg2, idg2)
+    val1, src1, val2, src2 = pair1.at[0], pair1.at[1], pair2.at[0], pair2.at[1]
 
     z_low = jnp.where(gz > 0, 1.0, 0.0).astype(F32)
     z_high = jnp.where(gz < nz - 1, 1.0, 0.0).astype(F32)
@@ -224,9 +229,9 @@
     local[0].wait()
     own1 = restrict0(lambda k: rho0[k + 1, 8:40, :])
     for k in range(2):
-        rho1[k + 1, 8:24, :] = own1[k]
+        rho1[k + 2, 16:32, :] = own1[k]
     own2 = restrict1(lambda k: own1[k])
-    rho2[1, 8:16, :] = own2
+    rho2[3, 16:24, :] = own2
     pack_message(0, own2)
     local[1].wait()
     for k in range(4):
@@ -249,29 +254,38 @@
         send(rows_out.at[1, 0:2], rows_in.at[1, 0:2], faces[3]),
     ]
 
-    def trade(ref, planes, rows):
-        top = PAD + rows
-        return [
-            send(ref.at[planes, 8:top, :], ref.at[0, 8:top, :], faces[0]),
-            send(ref.at[1, 8:top, :], ref.at[planes + 1, 8:top, :], faces[1]),
-            send(ref.at[1 : planes + 1, rows : rows + 8, :], ref.at[1 : planes + 1, 0:8, :], faces[2]),
-            send(ref.at[1 : planes + 1, 8:16, :], ref.at[1 : planes + 1, top : top + 8, :], faces[3]),
-        ]
-
-    dens1_copies = trade(rho1, 2, 16)
-    dens2_copies = trade(rho2, 1, 8)
+    rows1 = {0: (slice(16, 32), slice(16, 32)), 1: (slice(24, 32), slice(8, 16)), -1: (slice(16, 24), slice(32, 40))}
+    rows2 = {dy: (slice(16, 24), slice(16 - 8 * dy, 24 - 8 * dy)) for dy in (0, 1, -1)}
+    y_ways = ((1, faces[2]), (-1, faces[3]))
+    z_ways = ((1, faces[0]), (-1, faces[1]))
+
+    def planes1(dz):
+        return slice(2 - 2 * dz, 4 - 2 * dz)
+
+    dens1_copies = [
+        send(rho1.at[2:4, 16:32, :], rho1.at[planes1(dz), 16:32, :], device) for dz, device in z_ways
+    ]
+    for dy, device in y_ways:
+        source, target = rows1[dy]
+        dens1_copies.append(send(rho1.at[2:4, source, :], rho1.at[2:4, target, :], device))
+    for dz, dy, device in corners:
+        source, target = rows1[dy]
+        dens1_copies.append(send(rho1.at[2:4, source, :], rho1.at[planes1(dz), target, :], device))
     column_dens = gather_column(0, inbox_dens)
 
-    def fill_y(ref, planes, rows):
-        top = PAD + rows
-        for k in range(1, planes + 1):
-            ref[k, 7:8, :] = jnp.where(gy == 0, ref[k, 8:9, :], ref[k, 7:8, :])
-            ref[k, top : top + 1, :] = jnp.where(gy == ny - 1, ref[k, top - 1 : top, :], ref[k, top : top + 1, :])
-
-    def fill_z(ref, planes, rows):
-        top = PAD + rows
-        ref[0, 8:top, :] = jnp.where(gz == 0, ref[1, 8:top, :], ref[0, 8:top, :])
-        ref[planes + 1, 8:top, :] = jnp.where(gz == nz - 1, ref[planes, 8:top, :], ref[planes + 1, 8:top, :])
+    def fill_y(ref, planes, rows, first):
+        last = first + rows - 1
+        for k in planes:
+            ref[k, first - 1 : first, :] = jnp.where(gy == 0, ref[k, first : first + 1, :], ref[k, first - 1 : first, :])
+            ref[k, last + 1 : last + 2, :] = jnp.where(
+                gy == ny - 1, ref[k, last : last + 1, :], ref[k, last + 1 : last + 2, :]
+            )
+
+    def fill_z(ref, own, planes, rows, reach):
+        for i in range(reach):
+            low, high = own - 1 - i * planes, own + planes + i * planes
+            ref[low, rows, :] = jnp.where(gz == i, ref[low + 1, rows, :], ref[low, rows, :])
+            ref[high, rows, :] = jnp.where(gz == nz - 1 - i, ref[high - 1, rows, :], ref[high, rows, :])
 
     for k in range(4):
         fine.faces_x(k)
@@ -282,7 +296,7 @@
         for f, ref in ((0, rho0), (1, val0)):
             ref[k + 1, 7:8, :] = rows_in[0, f, k : k + 1, :]
             ref[k + 1, 40:41, :] = rows_in[1, f, k : k + 1, :]
-    fill_y(rho0, 4, 32)
+    fill_y(rho0, range(1, 5), 32, 8)
     for k in range(4):
         fine.faces_y(k)
     local[2].wait()
@@ -296,16 +310,16 @@
 
     for k in (1, 2):
         fine.diagonal(k)
-        fine.mask_y(k, y_low, y_high)
+        fine.mask_y(k, ((0, y_low), (32, y_high)))
         smooth(k)
     wait_recv(z_dens)
-    fill_z(rho0, 4, 32)
+    fill_z(rho0, 1, 4, slice(8, 40), 1)
     for face in (0, 4):
         fine.faces_z(face)
     for k in (0, 3):
         fine.diagonal(k)
-        fine.mask_y(k, y_low, y_high)
-    fine.mask_z(z_low, z_high)
+        fine.mask_y(k, ((0, y_low), (32, y_high)))
+    fine.mask_z(((0, z_low), (4, z_high)))
     wait_recv(z_vals)
     smooth(3)
     z_smooth = [send(smo0.at[4, 8:40, :], smo0.at[0, 8:40, :], faces[0])]
@@ -319,10 +333,13 @@
         send(rows_out.at[1, 2], rows_in.at[1, 2], faces[3]),
     ]
 
-    def coefficients(level, copies):
-        wait_recv(copies)
-        fill_y(level.rho, level.planes, level.rows)
-        fill_z(level.rho, level.planes, level.rows)
+    dens2_copies = [
+        send(rho2.at[3, 16:24, :], rho2.at[3, rows2[dy][1], :], device) for dy, device in y_ways
+    ]
+    for dz, dy, device in around:
+        dens2_copies.append(send(rho2.at[3, 16:24, :], rho2.at[3 - dz, rows2[dy][1], :], device))
+
+    def coefficients(level, z_faces):
         for k in range(level.planes):
             level.faces_x(k)
             level.faces_y(k)
@@ -330,13 +347,15 @@
             level.faces_z(k)
         for k in range(level.planes):
             level.diagonal(k)
-            level.mask_y(k, y_low, y_high)
-        level.mask_z(z_low, z_high)
-
+            level.mask_y(k, ((8, y_low), (level.rows - 8, y_high)))
+        level.mask_z(z_faces)
+
+    wait_recv(dens1_copies)
+    fill_y(rho1, range(6), 16, 16)
+    fill_z(rho1, 2, 2, slice(8, 40), 1)
+    coefficients(middle, ((1, z_low), (3, z_high)))
     wait_recv(column_dens)
     layer_dens = gather_layer(0, inbox_dens, wide_dens)
-    coefficients(middle, dens1_copies)
-    coefficients(coarse, dens2_copies)
 
     wait_recv(y_smooth)
     for k in range(4):
@@ -356,9 +375,25 @@
 
     source1 = restrict0(lambda k: res0[k])
     for k in range(2):
-        src1[k] = source1[k]
-        val1[k + 1, 8:24, :] = 4.0 * source1[k] * middle.idg[k]
-    copies1 = trade(val1, 2, 16)
+        src1[k + 2, 16:32, :] = source1[k]
+        val1[k + 2, 16:32, :] = 4.0 * source1[k] * idg1[k + 1, 8:24, :]
+    copies1 = [
+        send(val1.at[3, 16:32, :], val1.at[1, 16:32, :], faces[0]),
+        send(val1.at[2, 16:32, :], val1.at[4, 16:32, :], faces[1]),
+    ]
+    for dy, device in y_ways:
+        source, target = rows1[dy]
+        copies1.append(send(val1.at[2:4, source, :], val1.at[2:4, target, :], device))
+
+    wait_recv(dens2_copies)
+    fill_y(rho2, range(7), 8, 16)
+    fill_z(rho2, 3, 1, slice(8, 32), 3)
+
+    def inside_z(face):
+        at = gz + face - 2
+        return jnp.where((at > 0) & (at < nz), 1.0, 0.0).astype(F32)
+
+    coefficients(coarse, [(face, inside_z(face)) for face in range(6)])
 
     wait_recv(layer_dens)
     lane, sub = iota((8, 128), 1), iota((8, 128), 0)
@@ -404,17 +439,39 @@
     wait_recv(copies1)
 
     def residual1(k):
-        here, near = middle.neighbours(val1, k, 0, 16)
-        return (1.0 - OMEGA) * src1[k] + 0.25 * near
+        here, near = middle.neighbours(val1, k + 1, 8, 16)
+        return (1.0 - OMEGA) * source1[k] + 0.25 * near
 
     source2 = restrict1(residual1)
-    src2[0] = source2
-    val2[1, 8:16, :] = 16.0 * source2 * coarse.idg[0]
-    copies2 = trade(val2, 1, 8)
+    src2[3, 16:24, :] = source2
+    val2[3, 16:24, :] = 16.0 * source2 * idg2[2, 8:16, :]
+    copies2 = [send(val2.at[3, 16:24, :], val2.at[3, rows2[dy][1], :], device) for dy, device in y_ways]
+    for dz, device in z_ways:
+        copies2.append(send(val2.at[3, 16:24, :], val2.at[3 - dz, 16:24, :], device))
     wait_recv(copies2)
-    here, near = coarse.neighbours(val2, 0, 0, 8)
+    here, near = coarse.neighbours(val2, 2, 8, 8)
     pack_message(1, (1.0 - OMEGA) * source2 + 0.0625 * near)
     column_src = gather_column(1, inbox_src)
+
+    more1 = [
+        send(val1.at[2, 16:32, :], val1.at[0, 16:32, :], faces[0]),
+        send(val1.at[3, 16:32, :], val1.at[5, 16:32, :], faces[1]),
+    ]
+    for dz, device in z_ways:
+        more1.append(send(src1.at[2:4, 16:32, :], src1.at[planes1(dz), 16:32, :], device))
+    for dy, device in y_ways:
+        source, target = rows1[dy]
+        more1.append(send(src1.at[2:4, source, :], src1.at[2:4, target, :], device))
+    for dz, dy, device in corners:
+        source, target = rows1[dy]
+        more1.append(send(pair1.at[:, 2:4, source, :], pair1.at[:, planes1(dz), target, :], device))
+    more2 = [send(src2.at[3, 16:24, :], src2.at[3, rows2[dy][1], :], device) for dy, device in y_ways]
+    for dz, dy, device in around:
+        if abs(dz) == 1 and dy == 0:
+            more2.append(send(src2.at[3, 16:24, :], src2.at[3 - dz, 16:24, :], device))
+        else:
+            more2.append(send(pair2.at[:, 3, 16:24, :], pair2.at[:, 3 - dz, rows2[dy][1], :], device))
+
     wait_recv(column_src)
     layer_src = gather_layer(1, inbox_src, wide_src)
     wait_recv(layer_src)
@@ -486,60 +543,55 @@
     rows_from = (
         jnp.where(coarse_y == parent_y, 0.75, 0.0) + jnp.where(coarse_y == near_y, 0.25, 0.0)
     ).astype(F32)
-    wait_send(copies2)
-    for d in (-1, 0, 1):
+    mixed = []
+    for d in range(-3, 4):
         plane = gz + d + 4
         index = plane // 2
         other = index + 2 * (plane % 2) - 1
-        mixed = 0.75 * cor3[index] + 0.25 * cor3[other]
-        x_done = dot(mixed, from_halves)
-        stacked = jnp.concatenate([x_done[:, 0:128], x_done[:, 128:256]], axis=0)
-        val2[d + 1] = val2[d + 1] + dot(rows_from, stacked)
-
-    here, near = coarse.neighbours(val2, 0, 0, 8)
-    up2[1, 8:16, :] = (1.0 - OMEGA) * here + (16.0 * src2[0] + near) * coarse.idg[0]
-
-    def trade_all(ref, planes, rows):
-        top = PAD + rows
-        copies = trade(ref, planes, rows)
-        lowest, highest = slice(8, 16), slice(rows, rows + 8)
-        copies.append(send(ref.at[planes, highest, :], ref.at[0, 0:8, :], corners[0]))
-        copies.append(send(ref.at[planes, lowest, :], ref.at[0, top : top + 8, :], corners[1]))
-        copies.append(send(ref.at[1, highest, :], ref.at[planes + 1, 0:8, :], corners[2]))
-        copies.append(send(ref.at[1, lowest, :], ref.at[planes + 1, top : top + 8, :], corners[3]))
-        return copies
-
-    def clear_outside(ref, planes, rows):
-        top = PAD + rows
-        for k in range(planes + 2):
-            ref[k, 0:8, :] = ref[k, 0:8, :] * y_low
-            ref[k, top : top + 8, :] = ref[k, top : top + 8, :] * y_high
-        ref[0] = ref[0] * z_low
-        ref[planes + 1] = ref[planes + 1] * z_high
+        mixed.append(0.75 * cor3[index] + 0.25 * cor3[other])
+    x_done = dot(jnp.concatenate(mixed, axis=0), from_halves)
+    wait_recv(more1 + more2)
+    wait_send(copies1 + copies2 + more1 + more2 + z_smooth)
+    for k in range(7):
+        own = x_done[8 * k : 8 * k + 8]
+        stacked = jnp.concatenate([own[:, 0:128], own[:, 128:256]], axis=0)
+        val2[k, 8:32, :] = val2[k, 8:32, :] + dot(rows_from, stacked)
+
+    def in_grid(shape, first_row, rows, plane, planes):
+        row = iota(shape, 0)
+        at = row + first_row
+        good = (row > 0) & (row < shape[0] - 1) & (at >= 0) & (at < rows)
+        return good & (plane >= 0) & (plane < planes)
+
+    ups = []
+    for k in range(5):
+        here, near = coarse.neighbours(val2, k, 0, 24)
+        up = (1.0 - OMEGA) * here + (16.0 * src2[k + 1, 8:32, :] + near) * idg2[k]
+        ups.append(jnp.where(in_grid((24, 128), 8 * gy - 8, 8 * ny, gz + k - 2, nz), up, 0.0))
 
     spread_x1, spread_x0 = spread_matrix(128), spread_matrix(256)
     spread_y1, spread_y0 = padded_spread_matrix(8), padded_spread_matrix(16)
 
-    def prolong(ref, planes, target, spread_x, spread_y):
-        wide = [dot(spread_y, dot(ref[k], spread_x)) for k in range(planes + 2)]
-        for k in range(2 * planes + 2):
-            parent_z = (k + 1) // 2
-            near_z = parent_z + 1 if k % 2 == 0 else parent_z - 1
-            target[k] = target[k] + 0.75 * wide[parent_z] + 0.25 * wide[near_z]
-
-    up2_copies = trade_all(up2, 1, 8)
-    wait_recv(up2_copies)
-    clear_outside(up2, 1, 8)
-    wait_send(copies1)
-    prolong(up2, 1, val1, spread_x1, spread_y1)
-    for k in range(2):
-        here, near = middle.neighbours(val1, k, 0, 16)
-        up1[k + 1, 8:24, :] = (1.0 - OMEGA) * here + (4.0 * src1[k] + near) * middle.idg[k]
-    up1_copies = trade_all(up1, 2, 16)
-    wait_recv(up1_copies)
-    clear_outside(up1, 2, 16)
-    wait_send(z_smooth)
-    prolong(up1, 2, smo0, spread_x0, spread_y0)
+    def prolong(ups, target, first, rows, spread_x, spread_y):
+        height = ups[0].shape[0]
+        x_done = dot(jnp.concatenate(ups, axis=0), spread_x)
+        wide = [dot(spread_y, x_done[height * k : height * (k + 1)]) for k in range(len(ups))]
+        for k in range(6):
+            parent_z = (k + first) // 2
+            near_z = parent_z + 2 * ((k + first) % 2) - 1
+            target[k, rows, :] = target[k, rows, :] + 0.75 * wide[parent_z] + 0.25 * wide[near_z]
+
+    prolong(ups, val1, 2, slice(8, 40), spread_x1, spread_y1)
+    ups = []
+    for k in range(4):
+        parts = []
+        for r, m in middle.chunks():
+            here, near = middle.neighbours(val1, k, r, m)
+            source = src1[k + 1, 8 + r : 8 + r + m, :]
+            parts.append((1.0 - OMEGA) * here + (4.0 * source + near) * idg1[k, r : r + m, :])
+        up = jnp.concatenate(parts, axis=0)
+        ups.append(jnp.where(in_grid((32, 256), 16 * gy - 8, 16 * ny, 2 * gz + k - 1, 2 * nz), up, 0.0))
+    prolong(ups, smo0, 1, slice(0, 48), spread_x0, spread_y0)
     for k in range(4):
         for r, m in fine.chunks():
             here, near = fine.neighbours(smo0, k, r, m)
@@ -547,20 +599,16 @@
 
     wait_send(
         z_dens + z_vals + y_both + dens1_copies + dens2_copies + column_dens + y_smooth + layer_dens
-        + column_src + layer_src + up2_copies + up1_copies
+        + column_src + layer_src
     )
 
 
-def level_scratch(planes, rows, cols):
-    padded = pltpu.VMEM((planes + 2, rows + 2 * PAD, cols), F32)
+def coefficient_scratch(planes, rows, cols):
     own = pltpu.VMEM((planes, rows, cols), F32)
-    return [
-        padded, padded, padded, own, own,
-        own, pltpu.VMEM((planes, rows + 8, cols), F32), pltpu.VMEM((planes + 1, rows, cols), F32), own, own,
-    ]
-
-
-COPIES = 6 + 8 + 4 + 4 + 4 + 62 + 30 + 16
+    return [own, pltpu.VMEM((planes, rows + 8, cols), F32), pltpu.VMEM((planes + 1, rows, cols), F32), own, own]
+
+
+COPIES = 6 + 8 + 20 + 4 + 14 + 24 + 62 + 30
 
 
 def per_device(density, right_side, pressure_guess):
@@ -571,9 +619,15 @@
         in_specs=[pl.BlockSpec(memory_space=pl.ANY)] * 3,
         out_specs=pl.BlockSpec(memory_space=pltpu.VMEM),
         scratch_shapes=[
-            *level_scratch(4, 32, 512),
-            *level_scratch(2, 16, 256),
-            *level_scratch(1, 8, 128),
+            *[pltpu.VMEM((6, 48, 512), F32)] * 3,
+            *[pltpu.VMEM((4, 32, 512), F32)] * 2,
+            *coefficient_scratch(4, 32, 512),
+            pltpu.VMEM((6, 48, 256), F32),
+            pltpu.VMEM((2, 6, 48, 256), F32),
+            *coefficient_scratch(4, 32, 256),
+            pltpu.VMEM((7, 40, 128), F32),
+            pltpu.VMEM((2, 7, 40, 128), F32),
+            *coefficient_scratch(5, 24, 128),
             pltpu.VMEM((2, 3, 4, 512), F32),
             pltpu.VMEM((2, 3, 4, 512), F32),
             pltpu.VMEM((2, 2, 128), F32),

time: 94.6 us -> 84.3 us (0.89); the launches traced: 93.2 us -> 84.1 us
  Pallas kernels: 89.6 us -> 80.5 us
    pallas_call x1, Pallas kernels: 89.6 us -> 80.5 us  [per_device(): pl.pallas_call(kernel, out_shape=jax.ShapeDtypeStruct(density.shape, F32)...]
where the time goes in v2:
time: 84.3 us; the launch traced here: 84.1 us
  Pallas kernels  80.5 us (95%)
  local copies, waits for them, and re-layouts  3.55 us (4%)
    pallas_call x1, Pallas kernels, per_device(): pl.pallas_call(kernel, out_shape=jax.ShapeDtypeStruct(density.shape, F32)...  80.5 us
    unnamed x7, local copies, waits for them, and re-layouts  3.55 us

profile of v2, /device:TPU:1, one launch (start us, length us, event | category | flops | bytes accessed | tf_op | source)
XLA Modules:
  0.0 84.1 jit_solution(14552960639707308296)
XLA Ops:
  0.0 0.0 copy-start
  0.0 0.9 %copy-done = f32[4,32,512]{2,1,0:T(8,128)S(1)} copy-done((f32[4,32,512]{2,1,0:T(8,128)S(1)}, f32[4,32,512]{2,1,0:T(8,128)}, u32[]{:S(2)}) %copy-start) | copy-done | bytes 262168
  1.0 0.0 copy-start.1
  1.0 0.9 %copy-done.1 = f32[4,32,512]{2,1,0:T(8,128)S(1)} copy-done((f32[4,32,512]{2,1,0:T(8,128)S(1)}, f32[4,32,512]{2,1,0:T(8,128)}, u32[]{:S(2)}) %copy-start.1) | copy-done | bytes 262168
  1.9 0.0 copy-start.2
  1.9 0.9 %copy-done.2 = f32[4,32,512]{2,1,0:T(8,128)S(1)} copy-done((f32[4,32,512]{2,1,0:T(8,128)S(1)}, f32[4,32,512]{2,1,0:T(8,128)}, u32[]{:S(2)}) %copy-start.2) | copy-done | bytes 262168
  2.9 80.5 %shard_map.37 = f32[4,32,512]{2,1,0:T(8,128)S(1)} custom-call(f32[4,32,512]{2,1,0:T(8,128)S(1)} %copy-done, f32[4,32,512]{2,1,0:T(8,128)S(1)} %copy-done.1, f32[4,32,512]{2,1,0:T(8,128)S(1)} %copy-done.2), custom_call_target="tpu_custom_call" | custom-call | flops 20000000 | bytes 1048576 | tf_op jit(solution)/shard_map/pallas_call | solution.py:616
  83.4 0.7 copy.5
Async XLA Ops:
  0.0 0.9 %copy-start = (f32[4,32,512]{2,1,0:T(8,128)S(1)}, f32[4,32,512]{2,1,0:T(8,128)}, u32[]{:S(2)}) copy-start(f32[4,32,512]{2,1,0:T(8,128)} %dens_in.1) | copy-start | bytes 786436
  1.0 0.9 %copy-start.1 = (f32[4,32,512]{2,1,0:T(8,128)S(1)}, f32[4,32,512]{2,1,0:T(8,128)}, u32[]{:S(2)}) copy-start(f32[4,32,512]{2,1,0:T(8,128)} %right_in.1) | copy-start | bytes 786436
  1.9 0.9 %copy-start.2 = (f32[4,32,512]{2,1,0:T(8,128)S(1)}, f32[4,32,512]{2,1,0:T(8,128)}, u32[]{:S(2)}) copy-start(f32[4,32,512]{2,1,0:T(8,128)} %guess_in.1) | copy-start | bytes 786436

commit v3 on v2

--- a/solution.py
+++ b/solution.py
@@ -14,8 +14,17 @@
 PAD = 8
 
 
-def dot(a, b):
-    return jnp.dot(a, b, precision=lax.Precision.HIGHEST, preferred_element_type=F32)
+def dot(values, weights):
+    rows = values.shape[0]
+    if rows % 16:
+        values = jnp.concatenate([values, jnp.zeros((16 - rows % 16, values.shape[1]), F32)], axis=0)
+    total = values.shape[0]
+    first = values.astype(jnp.bfloat16).astype(F32)
+    rest = values - first
+    second = rest.astype(jnp.bfloat16).astype(F32)
+    parts = jnp.concatenate([first, second, rest - second], axis=0).astype(jnp.bfloat16)
+    out = jnp.dot(parts, weights, preferred_element_type=F32)
+    return (out[0:total] + out[total : 2 * total] + out[2 * total :])[0:rows]
 
 
 def twice_inverse(total):
@@ -27,24 +36,16 @@
     return lax.broadcasted_iota(jnp.int32, shape, axis)
 
 
-def pair_matrix(fine):
-    rows, cols = iota((fine, fine // 2), 0), iota((fine, fine // 2), 1)
-    return jnp.where(rows // 2 == cols, 1.0, 0.0).astype(F32)
+def pair_matrix():
+    rows, cols = iota((256, 128), 0), iota((256, 128), 1)
+    return jnp.where(rows // 2 == cols, 0.125, 0.0).astype(jnp.bfloat16)
 
 
 def spread_matrix(coarse):
     rows, cols = iota((coarse, 2 * coarse), 0), iota((coarse, 2 * coarse), 1)
     parent = cols // 2
     near = parent + 2 * (cols % 2) - 1
-    return (jnp.where(rows == parent, 0.75, 0.0) + jnp.where(rows == near, 0.25, 0.0)).astype(F32)
-
-
-def padded_spread_matrix(coarse):
-    shape = (2 * coarse + 2 * PAD, coarse + 2 * PAD)
-    rows, cols = iota(shape, 0), iota(shape, 1)
-    parent = rows // 2 + PAD // 2
-    near = parent + 2 * (rows % 2) - 1
-    return (jnp.where(cols == parent, 0.75, 0.0) + jnp.where(cols == near, 0.25, 0.0)).astype(F32)
+    return (jnp.where(rows == parent, 0.75, 0.0) + jnp.where(rows == near, 0.25, 0.0)).astype(jnp.bfloat16)
 
 
 class Level:
@@ -115,11 +116,11 @@
 def kernel(
     dens_in, right_in, guess_in, out,
     rho0, val0, smo0, src0, res0, bx0, by0, bz0, dg0, idg0,
-    rho1, pair1, bx1, by1, bz1, dg1, idg1,
+    rho1, pair1, near1, bx1, by1, bz1, dg1, idg1,
     rho2, pair2, bx2, by2, bz2, dg2, idg2,
     rows_out, rows_in, message, inbox_dens, inbox_src, tile, wide_dens, wide_src,
-    rho3, bx3, by3, bz3, dg3, dir3, res3, img3, cor3, pair_tmp,
-    local_sem, send_sem, recv_sem,
+    rho3, bx3, by3, bz3, dg3, dir3, res3, img3, cor3, pair_tmp, pair_rows, fine_rows, result,
+    far_smooth, face_rows, z_out, z_in, y_out, y_in, d_out, d_in, local_sem, out_sem, send_sem, recv_sem,
 ):
     gz, gy = lax.axis_index("gz"), lax.axis_index("gy")
     nz, ny = 128, 4
@@ -192,18 +193,34 @@
     y_low = jnp.where(gy > 0, 1.0, 0.0).astype(F32)
     y_high = jnp.where(gy < ny - 1, 1.0, 0.0).astype(F32)
 
-    pair_x0, pair_x1 = pair_matrix(512), pair_matrix(256)
-    pair_y0 = jnp.where(iota((16, 32), 1) // 2 == iota((16, 32), 0), 0.125, 0.0).astype(F32)
-    pair_y1 = jnp.where(iota((8, 16), 1) // 2 == iota((8, 16), 0), 0.125, 0.0).astype(F32)
-
-    def restrict0(read):
-        return [dot(pair_y0, dot(read(2 * k) + read(2 * k + 1), pair_x0)) for k in range(2)]
+    pair_x = pair_matrix()
+
+    def halve_x(blocks):
+        rows = sum(block.shape[0] for block in blocks)
+        summed = dot(jnp.concatenate([b[:, 0:256] for b in blocks] + [b[:, 256:512] for b in blocks], axis=0), pair_x)
+        out, at = [], 0
+        for block in blocks:
+            n = block.shape[0]
+            out.append((summed[at : at + n], summed[rows + at : rows + at + n]))
+            at += n
+        return out
+
+    def halve_y(slot, value):
+        n = value.shape[0]
+        pair_rows[slot, 0:n, :] = value
+        return pair_rows[slot, pl.ds(0, n // 2, stride=2), :] + pair_rows[slot, pl.ds(1, n // 2, stride=2), :]
+
+    def halve_xy(blocks):
+        return [
+            jnp.concatenate([halve_y(2 * i, left), halve_y(2 * i + 1, right)], axis=1)
+            for i, (left, right) in enumerate(halve_x(blocks))
+        ]
 
     def restrict1(read):
-        return dot(pair_y1, dot(read(0) + read(1), pair_x1))
+        return halve_y(0, dot(read(0) + read(1), pair_x))
 
     half_rows, half_cols = iota((128, 256), 0), iota((128, 256), 1)
-    to_halves = jnp.where((half_cols % 64 == half_rows // 2) & ((half_cols < 64) | (half_cols >= 192)), 0.125, 0.0).astype(F32)
+    to_halves = jnp.where((half_cols % 64 == half_rows // 2) & ((half_cols < 64) | (half_cols >= 192)), 0.125, 0.0).astype(jnp.bfloat16)
 
     def pack_message(field, value):
         pair_tmp[...] = dot(value, to_halves)
@@ -227,7 +244,7 @@
         return [send(tile.at[field], wide.at[slot], device) for device in layer]
 
     local[0].wait()
-    own1 = restrict0(lambda k: rho0[k + 1, 8:40, :])
+    own1 = halve_xy([rho0[2 * k + 1, 8:40, :] + rho0[2 * k + 2, 8:40, :] for k in range(2)])
     for k in range(2):
         rho1[k + 2, 16:32, :] = own1[k]
     own2 = restrict1(lambda k: own1[k])
@@ -238,6 +255,12 @@
         for f, ref in ((0, rho0), (1, val0)):
             rows_out[0, f, k : k + 1, :] = ref[k + 1, 39:40, :]
             rows_out[1, f, k : k + 1, :] = ref[k + 1, 8:9, :]
+
+    for k in (0, 5):
+        smo0[k, 8:40, :] = jnp.zeros((32, 512), F32)
+    for k in range(1, 5):
+        smo0[k, 7:8, :] = jnp.zeros((1, 512), F32)
+        smo0[k, 40:41, :] = jnp.zeros((1, 512), F32)
 
     pl.semaphore_wait(barrier, len(greeted))
 
@@ -322,17 +345,52 @@
     fine.mask_z(((0, z_low), (4, z_high)))
     wait_recv(z_vals)
     smooth(3)
-    z_smooth = [send(smo0.at[4, 8:40, :], smo0.at[0, 8:40, :], faces[0])]
     smooth(0)
-    z_smooth.append(send(smo0.at[1, 8:40, :], smo0.at[5, 8:40, :], faces[1]))
+
+    for plane in range(4):
+        for r, m in fine.chunks():
+            here, near = fine.neighbours(smo0, plane, r, m)
+            res0[plane, r : r + m, :] = src0[plane, r : r + m, :] - dg0[plane, r : r + m, :] * here + near
+    for way, (row, cell) in enumerate(((32, 39), (0, 8))):
+        for k in range(2):
+            lower = by0[2 * k, row : row + 1, :] * smo0[2 * k + 1, cell : cell + 1, :]
+            upper = by0[2 * k + 1, row : row + 1, :] * smo0[2 * k + 2, cell : cell + 1, :]
+            face_rows[2 * way + k : 2 * way + k + 1, :] = lower + upper
+    blocks = halve_x(
+        [res0[0] + res0[1], res0[2] + res0[3], bz0[4] * smo0[4, 8:40, :], bz0[0] * smo0[1, 8:40, :], face_rows[...]]
+    )
+    part0, part1, give_up, give_down = [
+        jnp.concatenate([halve_y(2 * i, left), halve_y(2 * i + 1, right)], axis=1)
+        for i, (left, right) in enumerate(blocks[:4])
+    ]
+    give_rows = jnp.concatenate(blocks[4], axis=1)
+    parts = (part0, part1)
+    z_out[0, 0] = give_up
+    z_out[0, 1] = part1
+    z_out[1, 0] = give_down
+    z_out[1, 1] = part0
+    swap_z = [send(z_out.at[way], z_in.at[way], faces[way]) for way in range(2)]
+    for way, row in ((0, 15), (1, 0)):
+        for k in range(2):
+            y_out[way, k : k + 1, :] = parts[k][row : row + 1]
+            y_out[way, 2 + k : 3 + k, :] = give_rows[2 * way + k : 2 * way + k + 1]
+    swap_y = [send(y_out.at[way], y_in.at[way], faces[2 + way]) for way in range(2)]
+    slot_of, swap_d = {}, []
+    for i, (dz, dy, device) in enumerate(corners):
+        slot_of[dz, dy] = i
+        way = (1 - dy) // 2
+        plane = (1 + dz) // 2
+        give, row = (give_up if dz == 1 else give_down), (15 if dy == 1 else 0)
+        d_out[i, 0:1, :] = give_rows[2 * way + plane : 2 * way + plane + 1]
+        d_out[i, 1:2, :] = give[row : row + 1]
+        swap_d.append(send(d_out.at[i], d_in.at[i], device))
+    z_smooth = [
+        send(smo0.at[4, 8:40, :], far_smooth.at[0], faces[0]), send(smo0.at[1, 8:40, :], far_smooth.at[1], faces[1])
+    ]
     for k in range(4):
         rows_out[0, 2, k : k + 1, :] = smo0[k + 1, 39:40, :]
         rows_out[1, 2, k : k + 1, :] = smo0[k + 1, 8:9, :]
-    y_smooth = [
-        send(rows_out.at[0, 2], rows_in.at[0, 2], faces[2]),
-        send(rows_out.at[1, 2], rows_in.at[1, 2], faces[3]),
-    ]
-
+    y_smooth = [send(rows_out.at[way, 2], rows_in.at[way, 2], faces[2 + way]) for way in range(2)]
     dens2_copies = [
         send(rho2.at[3, 16:24, :], rho2.at[3, rows2[dy][1], :], device) for dy, device in y_ways
     ]
@@ -357,34 +415,6 @@
     wait_recv(column_dens)
     layer_dens = gather_layer(0, inbox_dens, wide_dens)
 
-    wait_recv(y_smooth)
-    for k in range(4):
-        smo0[k + 1, 7:8, :] = rows_in[0, 2, k : k + 1, :]
-        smo0[k + 1, 40:41, :] = rows_in[1, 2, k : k + 1, :]
-
-    def residual(plane):
-        for r, m in fine.chunks():
-            here, near = fine.neighbours(smo0, plane, r, m)
-            res0[plane, r : r + m, :] = src0[plane, r : r + m, :] - fine.dg[plane, r : r + m, :] * here + near
-
-    for k in (1, 2):
-        residual(k)
-    wait_recv(z_smooth)
-    for k in (0, 3):
-        residual(k)
-
-    source1 = restrict0(lambda k: res0[k])
-    for k in range(2):
-        src1[k + 2, 16:32, :] = source1[k]
-        val1[k + 2, 16:32, :] = 4.0 * source1[k] * idg1[k + 1, 8:24, :]
-    copies1 = [
-        send(val1.at[3, 16:32, :], val1.at[1, 16:32, :], faces[0]),
-        send(val1.at[2, 16:32, :], val1.at[4, 16:32, :], faces[1]),
-    ]
-    for dy, device in y_ways:
-        source, target = rows1[dy]
-        copies1.append(send(val1.at[2:4, source, :], val1.at[2:4, target, :], device))
-
     wait_recv(dens2_copies)
     fill_y(rho2, range(7), 8, 16)
     fill_z(rho2, 3, 1, slice(8, 32), 3)
@@ -394,6 +424,41 @@
         return jnp.where((at > 0) & (at < nz), 1.0, 0.0).astype(F32)
 
     coefficients(coarse, [(face, inside_z(face)) for face in range(6)])
+
+    wait_recv(swap_z + swap_y + swap_d)
+    source1 = []
+    for k in range(2):
+        src1[k + 2, 16:32, :] = parts[k] + z_in[k, 0]
+        src1[k + 2, 16:17, :] = src1[k + 2, 16:17, :] + y_in[0, 2 + k : 3 + k, :]
+        src1[k + 2, 31:32, :] = src1[k + 2, 31:32, :] + y_in[1, 2 + k : 3 + k, :]
+        source1.append(src1[k + 2, 16:32, :])
+        corr = 4.0 * source1[k] * idg1[k + 1, 8:24, :]
+        val1[k + 2, 16:32, :] = corr
+        near1[k + 2, 16:32, :] = corr
+    for dz, plane, theirs, mine in ((1, 4, z_in[1, 1], give_up), (-1, 1, z_in[0, 1], give_down)):
+        near1[plane, 16:32, :] = theirs + mine
+        low, high = slot_of[-dz, 1], slot_of[-dz, -1]
+        near1[plane, 16:17, :] = near1[plane, 16:17, :] + d_in[low, 0:1, :]
+        near1[plane, 31:32, :] = near1[plane, 31:32, :] + d_in[high, 0:1, :]
+        near1[plane, 16:32, :] = 4.0 * near1[plane, 16:32, :] * idg1[plane - 1, 8:24, :]
+    for dy, row in ((1, 32), (-1, 15)):
+        way = (1 - dy) // 2
+        for k, dz in ((0, -1), (1, 1)):
+            total = y_in[1 - way, k : k + 1, :] + give_rows[2 * way + k : 2 * way + k + 1]
+            corner = slot_of[-dz, -dy]
+            total = total + d_in[corner, 1:2, :]
+            near1[k + 2, row : row + 1, :] = 4.0 * total * idg1[k + 1, row - 8 : row - 7, :]
+
+    def residual1(k):
+        here, near = middle.neighbours(near1, k + 1, 8, 16)
+        return (1.0 - OMEGA) * source1[k] + 0.25 * near
+
+    source2 = restrict1(residual1)
+    src2[3, 16:24, :] = source2
+    val2[3, 16:24, :] = 16.0 * source2 * idg2[2, 8:16, :]
+    copies2 = [send(val2.at[3, 16:24, :], val2.at[3, rows2[dy][1], :], device) for dy, device in y_ways]
+    for dz, device in z_ways:
+        copies2.append(send(val2.at[3, 16:24, :], val2.at[3 - dz, 16:24, :], device))
 
     wait_recv(layer_dens)
     lane, sub = iota((8, 128), 1), iota((8, 128), 0)
@@ -436,32 +501,15 @@
 
     lax.fori_loop(0, 64, coef3, 0, unroll=4)
 
-    wait_recv(copies1)
-
-    def residual1(k):
-        here, near = middle.neighbours(val1, k + 1, 8, 16)
-        return (1.0 - OMEGA) * source1[k] + 0.25 * near
-
-    source2 = restrict1(residual1)
-    src2[3, 16:24, :] = source2
-    val2[3, 16:24, :] = 16.0 * source2 * idg2[2, 8:16, :]
-    copies2 = [send(val2.at[3, 16:24, :], val2.at[3, rows2[dy][1], :], device) for dy, device in y_ways]
-    for dz, device in z_ways:
-        copies2.append(send(val2.at[3, 16:24, :], val2.at[3 - dz, 16:24, :], device))
     wait_recv(copies2)
     here, near = coarse.neighbours(val2, 2, 8, 8)
     pack_message(1, (1.0 - OMEGA) * source2 + 0.0625 * near)
     column_src = gather_column(1, inbox_src)
 
-    more1 = [
-        send(val1.at[2, 16:32, :], val1.at[0, 16:32, :], faces[0]),
-        send(val1.at[3, 16:32, :], val1.at[5, 16:32, :], faces[1]),
-    ]
-    for dz, device in z_ways:
-        more1.append(send(src1.at[2:4, 16:32, :], src1.at[planes1(dz), 16:32, :], device))
+    more1 = [send(pair1.at[:, 2:4, 16:32, :], pair1.at[:, planes1(dz), 16:32, :], device) for dz, device in z_ways]
     for dy, device in y_ways:
         source, target = rows1[dy]
-        more1.append(send(src1.at[2:4, source, :], src1.at[2:4, target, :], device))
+        more1.append(send(pair1.at[:, 2:4, source, :], pair1.at[:, 2:4, target, :], device))
     for dz, dy, device in corners:
         source, target = rows1[dy]
         more1.append(send(pair1.at[:, 2:4, source, :], pair1.at[:, planes1(dz), target, :], device))
@@ -534,15 +582,7 @@
     from_halves = (
         jnp.where(spread_rows == parent + 64 * half, 0.75, 0.0)
         + jnp.where((spread_rows == near + 64 * half) & inside, 0.25, 0.0)
-    ).astype(F32)
-    row_at, col_at = iota((24, 16), 0) + 8 * gy - 8, iota((24, 16), 1)
-    coarse_y = 2 * (col_at % 8) + col_at // 8
-    row_up = row_at + 8
-    parent_y = row_up // 2 - 4
-    near_y = parent_y + 2 * (row_up % 2) - 1
-    rows_from = (
-        jnp.where(coarse_y == parent_y, 0.75, 0.0) + jnp.where(coarse_y == near_y, 0.25, 0.0)
-    ).astype(F32)
+    ).astype(jnp.bfloat16)
     mixed = []
     for d in range(-3, 4):
         plane = gz + d + 4
@@ -550,12 +590,21 @@
         other = index + 2 * (plane % 2) - 1
         mixed.append(0.75 * cor3[index] + 0.25 * cor3[other])
     x_done = dot(jnp.concatenate(mixed, axis=0), from_halves)
-    wait_recv(more1 + more2)
-    wait_send(copies1 + copies2 + more1 + more2 + z_smooth)
+    wait_recv(more1 + more2 + z_smooth + y_smooth)
+    wait_send(copies2 + more1 + more2 + z_smooth)
+    first_row, last_row = iota((8, 128), 0) == 0, iota((8, 128), 0) == 7
+    window = pl.ds(pl.multiple_of(8 * gy, 8), 24)
     for k in range(7):
-        own = x_done[8 * k : 8 * k + 8]
-        stacked = jnp.concatenate([own[:, 0:128], own[:, 128:256]], axis=0)
-        val2[k, 8:32, :] = val2[k, 8:32, :] + dot(rows_from, stacked)
+        even, odd = x_done[8 * k : 8 * k + 8, 0:128], x_done[8 * k : 8 * k + 8, 128:256]
+        fine_rows[k, 0:8, :] = zero_plane
+        fine_rows[k, 40:48, :] = zero_plane
+        below = jnp.where(first_row, 0.0, pltpu.roll(odd, 1, 0))
+        above = jnp.where(last_row, 0.0, pltpu.roll(even, 7, 0))
+        fine_rows[k, pl.ds(8, 8, stride=4), :] = 0.75 * even + 0.25 * below
+        fine_rows[k, pl.ds(9, 8, stride=4), :] = 0.75 * even + 0.25 * odd
+        fine_rows[k, pl.ds(10, 8, stride=4), :] = 0.75 * odd + 0.25 * even
+        fine_rows[k, pl.ds(11, 8, stride=4), :] = 0.75 * odd + 0.25 * above
+        val2[k, 8:32, :] = val2[k, 8:32, :] + fine_rows[k, window, :]
 
     def in_grid(shape, first_row, rows, plane, planes):
         row = iota(shape, 0)
@@ -570,18 +619,28 @@
         ups.append(jnp.where(in_grid((24, 128), 8 * gy - 8, 8 * ny, gz + k - 2, nz), up, 0.0))
 
     spread_x1, spread_x0 = spread_matrix(128), spread_matrix(256)
-    spread_y1, spread_y0 = padded_spread_matrix(8), padded_spread_matrix(16)
-
-    def prolong(ups, target, first, rows, spread_x, spread_y):
+
+    def prolong(ups, target, first, rows, spread_x):
         height = ups[0].shape[0]
+        tall = 2 * height - 16
+        n = height - 8
         x_done = dot(jnp.concatenate(ups, axis=0), spread_x)
-        wide = [dot(spread_y, x_done[height * k : height * (k + 1)]) for k in range(len(ups))]
-        for k in range(6):
-            parent_z = (k + first) // 2
-            near_z = parent_z + 2 * ((k + first) % 2) - 1
-            target[k, rows, :] = target[k, rows, :] + 0.75 * wide[parent_z] + 0.25 * wide[near_z]
-
-    prolong(ups, val1, 2, slice(8, 40), spread_x1, spread_y1)
+        tiles = x_done.shape[1] // 128
+        for t in range(tiles):
+            for k in range(len(ups)):
+                pair_rows[t, 0:height, :] = x_done[height * k : height * (k + 1), 128 * t : 128 * (t + 1)]
+                here = 0.75 * pair_rows[t, 4 : 4 + n, :]
+                fine_rows[k, pl.ds(0, n, stride=2), :] = here + 0.25 * pair_rows[t, 3 : 3 + n, :]
+                fine_rows[k, pl.ds(1, n, stride=2), :] = here + 0.25 * pair_rows[t, 5 : 5 + n, :]
+            cols = slice(128 * t, 128 * (t + 1))
+            for k in range(6):
+                parent_z = (k + first) // 2
+                near_z = parent_z + 2 * ((k + first) % 2) - 1
+                target[k, rows, cols] = (
+                    target[k, rows, cols] + 0.75 * fine_rows[parent_z, 0:tall, :] + 0.25 * fine_rows[near_z, 0:tall, :]
+                )
+
+    prolong(ups, val1, 2, slice(8, 40), spread_x1)
     ups = []
     for k in range(4):
         parts = []
@@ -591,16 +650,27 @@
             parts.append((1.0 - OMEGA) * here + (4.0 * source + near) * idg1[k, r : r + m, :])
         up = jnp.concatenate(parts, axis=0)
         ups.append(jnp.where(in_grid((32, 256), 16 * gy - 8, 16 * ny, 2 * gz + k - 1, 2 * nz), up, 0.0))
-    prolong(ups, smo0, 1, slice(0, 48), spread_x0, spread_y0)
+    for k, plane in ((0, 0), (1, 5)):
+        smo0[plane, 8:40, :] = far_smooth[k]
+    for k in range(4):
+        smo0[k + 1, 7:8, :] = rows_in[0, 2, k : k + 1, :]
+        smo0[k + 1, 40:41, :] = rows_in[1, 2, k : k + 1, :]
+    prolong(ups, smo0, 1, slice(0, 48), spread_x0)
+    outgoing = []
     for k in range(4):
         for r, m in fine.chunks():
             here, near = fine.neighbours(smo0, k, r, m)
-            out[k, r : r + m, :] = (1.0 - OMEGA) * here + (src0[k, r : r + m, :] + near) * fine.idg[k, r : r + m, :]
+            result[k, r : r + m, :] = (1.0 - OMEGA) * here + (src0[k, r : r + m, :] + near) * fine.idg[k, r : r + m, :]
+        copy = pltpu.make_async_copy(result.at[k], out.at[k], out_sem.at[k])
+        copy.start()
+        outgoing.append(copy)
 
     wait_send(
         z_dens + z_vals + y_both + dens1_copies + dens2_copies + column_dens + y_smooth + layer_dens
-        + column_src + layer_src
+        + column_src + layer_src + swap_z + swap_y + swap_d
     )
+    for copy in outgoing:
+        copy.wait()
 
 
 def coefficient_scratch(planes, rows, cols):
@@ -608,7 +678,7 @@
     return [own, pltpu.VMEM((planes, rows + 8, cols), F32), pltpu.VMEM((planes + 1, rows, cols), F32), own, own]
 
 
-COPIES = 6 + 8 + 20 + 4 + 14 + 24 + 62 + 30
+COPIES = 6 + 8 + 20 + 8 + 4 + 4 + 8 + 20 + 62 + 30
 
 
 def per_device(density, right_side, pressure_guess):
@@ -616,14 +686,15 @@
     return pl.pallas_call(
         kernel,
         out_shape=jax.ShapeDtypeStruct(density.shape, F32),
-        in_specs=[pl.BlockSpec(memory_space=pl.ANY)] * 3,
-        out_specs=pl.BlockSpec(memory_space=pltpu.VMEM),
+        in_specs=[pl.BlockSpec(memory_space=pltpu.HBM)] * 3,
+        out_specs=pl.BlockSpec(memory_space=pltpu.HBM),
         scratch_shapes=[
             *[pltpu.VMEM((6, 48, 512), F32)] * 3,
             *[pltpu.VMEM((4, 32, 512), F32)] * 2,
             *coefficient_scratch(4, 32, 512),
             pltpu.VMEM((6, 48, 256), F32),
             pltpu.VMEM((2, 6, 48, 256), F32),
+            pltpu.VMEM((6, 48, 256), F32),
             *coefficient_scratch(4, 32, 256),
             pltpu.VMEM((7, 40, 128), F32),
             pltpu.VMEM((2, 7, 40, 128), F32),
@@ -640,7 +711,16 @@
             coarsest, coarsest, pltpu.VMEM((65, 8, 128), F32), coarsest,
             pltpu.VMEM((66, 8, 128), F32), coarsest, coarsest, pltpu.VMEM((68, 8, 128), F32),
             pltpu.VMEM((8, 256), F32),
+            pltpu.VMEM((8, 32, 128), F32),
+            pltpu.VMEM((7, 48, 128), F32),
+            pltpu.VMEM((4, 32, 512), F32),
+            pltpu.VMEM((2, 32, 512), F32),
+            pltpu.VMEM((8, 512), F32),
+            *[pltpu.VMEM((2, 2, 16, 256), F32)] * 2,
+            *[pltpu.VMEM((2, 4, 256), F32)] * 2,
+            *[pltpu.VMEM((4, 2, 256), F32)] * 2,
             pltpu.SemaphoreType.DMA((3,)),
+            pltpu.SemaphoreType.DMA((4,)),
             pltpu.SemaphoreType.DMA((COPIES,)),
             pltpu.SemaphoreType.DMA((COPIES,)),
         ],

time: 84.3 us -> 79.7 us (0.945)
  Pallas kernels: 80.5 us -> 75.9 us
    pallas_call x1, Pallas kernels: 80.5 us -> 75.9 us  [per_device(): pl.pallas_call(kernel, out_shape=jax.ShapeDtypeStruct(density.shape, F32)...]
where the time goes in v3:
time: 79.7 us; the launch traced here: 79.5 us
  Pallas kernels  75.9 us (95%)
  local copies, waits for them, and re-layouts  3.55 us (4%)
    pallas_call x1, Pallas kernels, per_device(): pl.pallas_call(kernel, out_shape=jax.ShapeDtypeStruct(density.shape, F32)...  75.9 us
    unnamed x7, local copies, waits for them, and re-layouts  3.55 us

profile of v3, /device:TPU:1, one launch (start us, length us, event | category | flops | bytes accessed | tf_op | source)
XLA Modules:
  0.0 79.5 jit_solution(15680918721446351949)
XLA Ops:
  0.0 0.0 copy-start
  0.0 0.9 %copy-done = f32[4,32,512]{2,1,0:T(8,128)S(1)} copy-done((f32[4,32,512]{2,1,0:T(8,128)S(1)}, f32[4,32,512]{2,1,0:T(8,128)}, u32[]{:S(2)}) %copy-start) | copy-done | bytes 262168
  1.0 0.0 copy-start.1
  1.0 0.9 %copy-done.1 = f32[4,32,512]{2,1,0:T(8,128)S(1)} copy-done((f32[4,32,512]{2,1,0:T(8,128)S(1)}, f32[4,32,512]{2,1,0:T(8,128)}, u32[]{:S(2)}) %copy-start.1) | copy-done | bytes 262168
  1.9 0.0 copy-start.2
  1.9 0.9 %copy-done.2 = f32[4,32,512]{2,1,0:T(8,128)S(1)} copy-done((f32[4,32,512]{2,1,0:T(8,128)S(1)}, f32[4,32,512]{2,1,0:T(8,128)}, u32[]{:S(2)}) %copy-start.2) | copy-done | bytes 262168
  2.9 75.9 %shard_map.37 = f32[4,32,512]{2,1,0:T(8,128)S(1)} custom-call(f32[4,32,512]{2,1,0:T(8,128)S(1)} %copy-done, f32[4,32,512]{2,1,0:T(8,128)S(1)} %copy-done.1, f32[4,32,512]{2,1,0:T(8,128)S(1)} %copy-done.2), custom_call_target="tpu_custom_call" | custom-call | flops 20000000 | bytes 1048576 | tf_op jit(solution)/shard_map/pallas_call | solution.py:686
  78.8 0.7 copy.5
Async XLA Ops:
  0.0 0.9 %copy-start = (f32[4,32,512]{2,1,0:T(8,128)S(1)}, f32[4,32,512]{2,1,0:T(8,128)}, u32[]{:S(2)}) copy-start(f32[4,32,512]{2,1,0:T(8,128)} %dens_in.1) | copy-start | bytes 786436
  1.0 0.9 %copy-start.1 = (f32[4,32,512]{2,1,0:T(8,128)S(1)}, f32[4,32,512]{2,1,0:T(8,128)}, u32[]{:S(2)}) copy-start(f32[4,32,512]{2,1,0:T(8,128)} %right_in.1) | copy-start | bytes 786436
  1.9 0.9 %copy-start.2 = (f32[4,32,512]{2,1,0:T(8,128)S(1)}, f32[4,32,512]{2,1,0:T(8,128)}, u32[]{:S(2)}) copy-start(f32[4,32,512]{2,1,0:T(8,128)} %guess_in.1) | copy-start | bytes 786436

commit v4 on v3

--- a/solution.py
+++ b/solution.py
@@ -54,8 +54,10 @@
         self.chunk = chunk
         self.rho, self.bx, self.by, self.bz, self.dg, self.idg = rho, bx, by, bz, dg, idg
 
+        self.span = (0, self.rows)
+
     def chunks(self):
-        return [(r, self.chunk) for r in range(0, self.rows, self.chunk)]
+        return [(r, self.chunk) for r in range(*self.span, self.chunk)]
 
     def faces_x(self, plane):
         n = self.cols
@@ -72,10 +74,10 @@
             low = self.rho[plane + 1, PAD - 1 + r : PAD - 1 + r + m, :]
             high = self.rho[plane + 1, PAD + r : PAD + r + m, :]
             self.by[plane, r : r + m, :] = twice_inverse(low + high)
-        end = PAD + self.rows
-        low = self.rho[plane + 1, end - 1 : end, :]
-        high = self.rho[plane + 1, end : end + 1, :]
-        self.by[plane, self.rows : self.rows + 1, :] = twice_inverse(low + high)
+        last = self.span[1]
+        low = self.rho[plane + 1, PAD - 1 + last : PAD + last, :]
+        high = self.rho[plane + 1, PAD + last : PAD + last + 1, :]
+        self.by[plane, last : last + 1, :] = twice_inverse(low + high)
 
     def faces_z(self, face):
         for r, m in self.chunks():
@@ -116,11 +118,11 @@
 def kernel(
     dens_in, right_in, guess_in, out,
     rho0, val0, smo0, src0, res0, bx0, by0, bz0, dg0, idg0,
-    rho1, pair1, near1, bx1, by1, bz1, dg1, idg1,
+    rho1, pair1, bx1, by1, bz1, dg1, idg1,
     rho2, pair2, bx2, by2, bz2, dg2, idg2,
     rows_out, rows_in, message, inbox_dens, inbox_src, tile, wide_dens, wide_src,
-    rho3, bx3, by3, bz3, dg3, dir3, res3, img3, cor3, pair_tmp, pair_rows, fine_rows, result,
-    far_smooth, face_rows, z_out, z_in, y_out, y_in, d_out, d_in, local_sem, out_sem, send_sem, recv_sem,
+    rho3, bx3, by3, bz3, dg3, dir3, res3, img3, mul3, cor3, pair_tmp, pair_rows, fine_rows, result,
+    far_smooth, face_rows, z_out, z_in, y_out, y_in, d_out, d_in, wide_y_out, wide_y_in, wide_d_out, wide_d_in, local_sem, out_sem, send_sem, recv_sem,
 ):
     gz, gy = lax.axis_index("gz"), lax.axis_index("gy")
     nz, ny = 128, 4
@@ -133,7 +135,7 @@
     up_z, down_z = (gz + 1) % nz, (gz + nz - 1) % nz
     up_y, down_y = (gy + 1) % ny, (gy + ny - 1) % ny
     column = []
-    for d in range(16):
+    for d in (8, 7, 9, 6, 10, 5, 11, 4, 12, 3, 13, 2, 14, 1, 15, 0):
         for k in range(2):
             if d or k:
                 z = (zpos + d) % 16
@@ -149,7 +151,7 @@
         for dy in (0, 1, -1):
             around.append((dz, dy, ((gz + dz + nz) % nz, (gy + dy + ny) % ny)))
     corners = [(dz, dy, device) for dz, dy, device in around if abs(dz) == 1 and dy]
-    greeted = faces[2:] + [device for _, _, device in around] + column + layer
+    greeted = column + [device for _, _, device in around] + faces[2:] + layer
 
     barrier = pltpu.get_barrier_semaphore()
     for device in greeted:
@@ -185,7 +187,7 @@
 
     fine = Level((4, 32, 512), 8, rho0, bx0, by0, bz0, dg0, idg0)
     middle = Level((4, 32, 256), 16, rho1, bx1, by1, bz1, dg1, idg1)
-    coarse = Level((5, 24, 128), 24, rho2, bx2, by2, bz2, dg2, idg2)
+    coarse = Level((5, 24, 128), 8, rho2, bx2, by2, bz2, dg2, idg2)
     val1, src1, val2, src2 = pair1.at[0], pair1.at[1], pair2.at[0], pair2.at[1]
 
     z_low = jnp.where(gz > 0, 1.0, 0.0).astype(F32)
@@ -284,17 +286,6 @@
 
     def planes1(dz):
         return slice(2 - 2 * dz, 4 - 2 * dz)
-
-    dens1_copies = [
-        send(rho1.at[2:4, 16:32, :], rho1.at[planes1(dz), 16:32, :], device) for dz, device in z_ways
-    ]
-    for dy, device in y_ways:
-        source, target = rows1[dy]
-        dens1_copies.append(send(rho1.at[2:4, source, :], rho1.at[2:4, target, :], device))
-    for dz, dy, device in corners:
-        source, target = rows1[dy]
-        dens1_copies.append(send(rho1.at[2:4, source, :], rho1.at[planes1(dz), target, :], device))
-    column_dens = gather_column(0, inbox_dens)
 
     def fill_y(ref, planes, rows, first):
         last = first + rows - 1
@@ -344,6 +335,15 @@
         fine.mask_y(k, ((0, y_low), (32, y_high)))
     fine.mask_z(((0, z_low), (4, z_high)))
     wait_recv(z_vals)
+    dens1_copies = [
+        send(rho1.at[2:4, 16:32, :], rho1.at[planes1(dz), 16:32, :], device) for dz, device in z_ways
+    ]
+    for dy, device in y_ways:
+        source, target = rows1[dy]
+        dens1_copies.append(send(rho1.at[2:4, source, :], rho1.at[2:4, target, :], device))
+    for dz, dy, device in corners:
+        source, target = rows1[dy]
+        dens1_copies.append(send(rho1.at[2:4, source, :], rho1.at[planes1(dz), target, :], device))
     smooth(3)
     smooth(0)
 
@@ -384,6 +384,65 @@
         d_out[i, 0:1, :] = give_rows[2 * way + plane : 2 * way + plane + 1]
         d_out[i, 1:2, :] = give[row : row + 1]
         swap_d.append(send(d_out.at[i], d_in.at[i], device))
+    column_dens = gather_column(0, inbox_dens)
+    dens2_near = [send(rho2.at[3, 16:24, :], rho2.at[3, rows2[dy][1], :], device) for dy, device in y_ways]
+    dens2_near += [send(rho2.at[3, 16:24, :], rho2.at[3 - dz, 16:24, :], device) for dz, device in z_ways]
+
+    def coefficients(level, planes, z_faces):
+        for k in planes:
+            level.faces_x(k)
+            level.faces_y(k)
+        for k in range(planes[0], planes[-1] + 2):
+            level.faces_z(k)
+        for k in planes:
+            level.diagonal(k)
+            level.mask_y(k, ((8, y_low), (level.rows - 8, y_high)))
+        level.mask_z(z_faces)
+
+    wait_recv(dens1_copies)
+    fill_y(rho1, range(6), 16, 16)
+    fill_z(rho1, 2, 2, slice(8, 40), 1)
+    coefficients(middle, range(4), ((1, z_low), (3, z_high)))
+    wait_recv(dens2_near)
+    fill_y(rho2, (3,), 8, 16)
+    fill_z(rho2, 3, 1, slice(16, 24), 1)
+    coarse.span = (8, 16)
+    coefficients(coarse, (2,), ((2, z_low), (3, z_high)))
+    coarse.span = (0, 24)
+
+    wait_recv(swap_z + swap_y + swap_d)
+    source1 = []
+    for k in range(2):
+        src1[k + 2, 16:32, :] = parts[k] + z_in[k, 0]
+        src1[k + 2, 16:17, :] = src1[k + 2, 16:17, :] + y_in[0, 2 + k : 3 + k, :]
+        src1[k + 2, 31:32, :] = src1[k + 2, 31:32, :] + y_in[1, 2 + k : 3 + k, :]
+        source1.append(src1[k + 2, 16:32, :])
+        val1[k + 2, 16:32, :] = 4.0 * source1[k] * idg1[k + 1, 8:24, :]
+    for dz, plane, theirs, mine in ((1, 4, z_in[1, 1], give_up), (-1, 1, z_in[0, 1], give_down)):
+        src1[plane, 16:32, :] = theirs + mine
+        low, high = slot_of[-dz, 1], slot_of[-dz, -1]
+        src1[plane, 16:17, :] = src1[plane, 16:17, :] + d_in[low, 0:1, :]
+        src1[plane, 31:32, :] = src1[plane, 31:32, :] + d_in[high, 0:1, :]
+        val1[plane, 16:32, :] = 4.0 * src1[plane, 16:32, :] * idg1[plane - 1, 8:24, :]
+    for dy, row in ((1, 32), (-1, 15)):
+        way = (1 - dy) // 2
+        for k, dz in ((0, -1), (1, 1)):
+            total = y_in[1 - way, k : k + 1, :] + give_rows[2 * way + k : 2 * way + k + 1]
+            total = total + d_in[slot_of[-dz, -dy], 1:2, :]
+            src1[k + 2, row : row + 1, :] = total
+            val1[k + 2, row : row + 1, :] = 4.0 * total * idg1[k + 1, row - 8 : row - 7, :]
+
+    def residual1(k):
+        here, near = middle.neighbours(val1, k + 1, 8, 16)
+        return (1.0 - OMEGA) * source1[k] + 0.25 * near
+
+    source2 = restrict1(residual1)
+    src2[3, 16:24, :] = source2
+    val2[3, 16:24, :] = 16.0 * source2 * idg2[2, 8:16, :]
+    copies2 = [send(val2.at[3, 16:24, :], val2.at[3, rows2[dy][1], :], device) for dy, device in y_ways]
+    for dz, device in z_ways:
+        copies2.append(send(val2.at[3, 16:24, :], val2.at[3 - dz, 16:24, :], device))
+
     z_smooth = [
         send(smo0.at[4, 8:40, :], far_smooth.at[0], faces[0]), send(smo0.at[1, 8:40, :], far_smooth.at[1], faces[1])
     ]
@@ -391,74 +450,16 @@
         rows_out[0, 2, k : k + 1, :] = smo0[k + 1, 39:40, :]
         rows_out[1, 2, k : k + 1, :] = smo0[k + 1, 8:9, :]
     y_smooth = [send(rows_out.at[way, 2], rows_in.at[way, 2], faces[2 + way]) for way in range(2)]
-    dens2_copies = [
-        send(rho2.at[3, 16:24, :], rho2.at[3, rows2[dy][1], :], device) for dy, device in y_ways
+    dens2_far = [
+        send(rho2.at[3, 16:24, :], rho2.at[3 - dz, rows2[dy][1], :], device)
+        for dz, dy, device in around if abs(dz) > 1 or dy
     ]
-    for dz, dy, device in around:
-        dens2_copies.append(send(rho2.at[3, 16:24, :], rho2.at[3 - dz, rows2[dy][1], :], device))
-
-    def coefficients(level, z_faces):
-        for k in range(level.planes):
-            level.faces_x(k)
-            level.faces_y(k)
-        for k in range(level.planes + 1):
-            level.faces_z(k)
-        for k in range(level.planes):
-            level.diagonal(k)
-            level.mask_y(k, ((8, y_low), (level.rows - 8, y_high)))
-        level.mask_z(z_faces)
-
-    wait_recv(dens1_copies)
-    fill_y(rho1, range(6), 16, 16)
-    fill_z(rho1, 2, 2, slice(8, 40), 1)
-    coefficients(middle, ((1, z_low), (3, z_high)))
     wait_recv(column_dens)
     layer_dens = gather_layer(0, inbox_dens, wide_dens)
-
-    wait_recv(dens2_copies)
-    fill_y(rho2, range(7), 8, 16)
-    fill_z(rho2, 3, 1, slice(8, 32), 3)
-
-    def inside_z(face):
-        at = gz + face - 2
-        return jnp.where((at > 0) & (at < nz), 1.0, 0.0).astype(F32)
-
-    coefficients(coarse, [(face, inside_z(face)) for face in range(6)])
-
-    wait_recv(swap_z + swap_y + swap_d)
-    source1 = []
-    for k in range(2):
-        src1[k + 2, 16:32, :] = parts[k] + z_in[k, 0]
-        src1[k + 2, 16:17, :] = src1[k + 2, 16:17, :] + y_in[0, 2 + k : 3 + k, :]
-        src1[k + 2, 31:32, :] = src1[k + 2, 31:32, :] + y_in[1, 2 + k : 3 + k, :]
-        source1.append(src1[k + 2, 16:32, :])
-        corr = 4.0 * source1[k] * idg1[k + 1, 8:24, :]
-        val1[k + 2, 16:32, :] = corr
-        near1[k + 2, 16:32, :] = corr
-    for dz, plane, theirs, mine in ((1, 4, z_in[1, 1], give_up), (-1, 1, z_in[0, 1], give_down)):
-        near1[plane, 16:32, :] = theirs + mine
-        low, high = slot_of[-dz, 1], slot_of[-dz, -1]
-        near1[plane, 16:17, :] = near1[plane, 16:17, :] + d_in[low, 0:1, :]
-        near1[plane, 31:32, :] = near1[plane, 31:32, :] + d_in[high, 0:1, :]
-        near1[plane, 16:32, :] = 4.0 * near1[plane, 16:32, :] * idg1[plane - 1, 8:24, :]
-    for dy, row in ((1, 32), (-1, 15)):
-        way = (1 - dy) // 2
-        for k, dz in ((0, -1), (1, 1)):
-            total = y_in[1 - way, k : k + 1, :] + give_rows[2 * way + k : 2 * way + k + 1]
-            corner = slot_of[-dz, -dy]
-            total = total + d_in[corner, 1:2, :]
-            near1[k + 2, row : row + 1, :] = 4.0 * total * idg1[k + 1, row - 8 : row - 7, :]
-
-    def residual1(k):
-        here, near = middle.neighbours(near1, k + 1, 8, 16)
-        return (1.0 - OMEGA) * source1[k] + 0.25 * near
-
-    source2 = restrict1(residual1)
-    src2[3, 16:24, :] = source2
-    val2[3, 16:24, :] = 16.0 * source2 * idg2[2, 8:16, :]
-    copies2 = [send(val2.at[3, 16:24, :], val2.at[3, rows2[dy][1], :], device) for dy, device in y_ways]
-    for dz, device in z_ways:
-        copies2.append(send(val2.at[3, 16:24, :], val2.at[3 - dz, 16:24, :], device))
+    wait_recv(copies2)
+    here, near = coarse.neighbours(val2, 2, 8, 8)
+    pack_message(1, (1.0 - OMEGA) * source2 + 0.0625 * near)
+    column_src = gather_column(1, inbox_src)
 
     wait_recv(layer_dens)
     lane, sub = iota((8, 128), 1), iota((8, 128), 0)
@@ -501,77 +502,109 @@
 
     lax.fori_loop(0, 64, coef3, 0, unroll=4)
 
-    wait_recv(copies2)
-    here, near = coarse.neighbours(val2, 2, 8, 8)
-    pack_message(1, (1.0 - OMEGA) * source2 + 0.0625 * near)
-    column_src = gather_column(1, inbox_src)
-
-    more1 = [send(pair1.at[:, 2:4, 16:32, :], pair1.at[:, planes1(dz), 16:32, :], device) for dz, device in z_ways]
-    for dy, device in y_ways:
-        source, target = rows1[dy]
-        more1.append(send(pair1.at[:, 2:4, source, :], pair1.at[:, 2:4, target, :], device))
-    for dz, dy, device in corners:
-        source, target = rows1[dy]
-        more1.append(send(pair1.at[:, 2:4, source, :], pair1.at[:, planes1(dz), target, :], device))
+    wait_recv(dens2_far)
+
+    def inside_z(face):
+        at = gz + face - 2
+        return jnp.where((at > 0) & (at < nz), 1.0, 0.0).astype(F32)
+
+    fill_y(rho2, range(7), 8, 16)
+    fill_z(rho2, 3, 1, slice(8, 32), 3)
+    coefficients(coarse, range(5), [(face, inside_z(face)) for face in range(6)])
+
+    zero_plane = jnp.zeros((8, 128), F32)
+    for k in (0, 1, 66, 67):
+        cor3[k] = zero_plane
+
+    def clear3(k, _):
+        dir3[k] = zero_plane
+        mul3[k] = zero_plane
+        cor3[k + 2] = zero_plane
+        return 0
+
+    lax.fori_loop(0, 64, clear3, 0, unroll=8)
+    for ref in (dir3, mul3, res3, img3):
+        ref[64] = zero_plane
+
+    wait_recv(column_src)
+    layer_src = gather_layer(1, inbox_src, wide_src)
+
+    more1 = [
+        send(val1.at[2, 16:32, :], val1.at[0, 16:32, :], faces[0]),
+        send(val1.at[3, 16:32, :], val1.at[5, 16:32, :], faces[1]),
+    ]
+    for way, row in ((0, 30), (1, 17)):
+        for k in range(2):
+            wide_y_out[way, k : k + 1, :] = val1[k + 2, row : row + 1, :]
+        more1.append(send(wide_y_out.at[way], wide_y_in.at[way], faces[2 + way]))
+    for i, (dz, dy, device) in enumerate(corners):
+        plane, far_plane = (3, 2) if dz == 1 else (2, 3)
+        row, far_row = (31, 30) if dy == 1 else (16, 17)
+        wide_d_out[i, 0:1, :] = val1[plane, row : row + 1, :]
+        wide_d_out[i, 1:2, :] = val1[plane, far_row : far_row + 1, :]
+        wide_d_out[i, 2:3, :] = val1[far_plane, row : row + 1, :]
+        wide_d_out[i, 3:4, :] = src1[plane, row : row + 1, :]
+        more1.append(send(wide_d_out.at[i], wide_d_in.at[i], device))
     more2 = [send(src2.at[3, 16:24, :], src2.at[3, rows2[dy][1], :], device) for dy, device in y_ways]
     for dz, dy, device in around:
+        target = rows2[dy][1]
         if abs(dz) == 1 and dy == 0:
-            more2.append(send(src2.at[3, 16:24, :], src2.at[3 - dz, 16:24, :], device))
+            more2.append(send(src2.at[3, 16:24, :], src2.at[3 - dz, target, :], device))
+        elif abs(dz) == 3:
+            more2.append(send(val2.at[3, 16:24, :], val2.at[3 - dz, target, :], device))
         else:
-            more2.append(send(pair2.at[:, 3, 16:24, :], pair2.at[:, 3 - dz, rows2[dy][1], :], device))
-
-    wait_recv(column_src)
-    layer_src = gather_layer(1, inbox_src, wide_src)
+            more2.append(send(pair2.at[:, 3, 16:24, :], pair2.at[:, 3 - dz, target, :], device))
     wait_recv(layer_src)
 
-    zero_plane = jnp.zeros((8, 128), F32)
-    dir3[0] = zero_plane
-    dir3[65] = zero_plane
-    for k in (0, 1, 66, 67):
-        cor3[k] = zero_plane
-    total = zero_plane
     for zh in range(4):
-        for s in range(16):
-            v = wide_src[s, zh]
-            k = 16 * zh + s
-            dir3[k + 1] = v
-            res3[k] = v
-            cor3[k + 2] = zero_plane
-            total = total + v * v
+        for k in range(16):
+            res3[16 * zh + k] = wide_src[k, zh]
 
     def whole(v):
-        return jnp.sum(jnp.sum(v, axis=0, keepdims=True), axis=1, keepdims=True)
-
-    def sweep(step, norm):
-        def apply(k, acc):
-            v = dir3[k + 1]
-            bx, by = bx3[k], by3[k]
-            image = dg3[k] * v - bz3[k] * dir3[k] - bz3[k + 1] * dir3[k + 2]
-            image = image - by * lower_y(v) - upper_y(by * v)
-            image = image - bx * pltpu.roll(v, 1, 1) - pltpu.roll(bx * v, 127, 1)
-            img3[k] = image
-            return acc + v * image
-
-        bottom = whole(lax.fori_loop(0, 64, apply, zero_plane, unroll=16))
-        alpha = norm / bottom
-
-        def advance(k, acc):
-            cor3[k + 2] = cor3[k + 2] + alpha * dir3[k + 1]
-            r = res3[k] - alpha * img3[k]
-            res3[k] = r
-            return acc + r * r
-
-        norm_next = whole(lax.fori_loop(0, 64, advance, zero_plane, unroll=16))
+        return jnp.sum(jnp.sum(v, axis=1, keepdims=True), axis=0, keepdims=True)
+
+    def apply(k, prev, here, later):
+        bx, by = bx3[k], by3[k]
+        image = (dg3[k] * here - bz3[k] * prev) - (bz3[k + 1] * later + by * lower_y(here))
+        image = image - ((bx * pltpu.roll(here, 1, 1) + upper_y(by * here)) + pltpu.roll(bx * here, 127, 1))
+        img3[k] = image
+        return image
+
+    def advance(k, alpha, beta):
+        direction = res3[k] + beta * dir3[k]
+        dir3[k] = direction
+        cor3[k + 2] = cor3[k + 2] + alpha * direction
+        image = img3[k] + beta * mul3[k]
+        mul3[k] = image
+        resid = res3[k] - alpha * image
+        res3[k] = resid
+        return resid
+
+    def totals(first, next_resid):
+        def plane(k, carry):
+            norm, power, prev, here = carry
+            later = next_resid(k + 1)
+            image = apply(k, prev, here, later)
+            return norm + here * here, power + here * image, here, later
+
+        norm, power, _, _ = lax.fori_loop(0, 64, plane, (zero_plane, zero_plane, zero_plane, first), unroll=64)
+        return whole(norm), whole(power)
+
+    norm, power = totals(res3[0], lambda k: res3[k])
+
+    def sweep(step, carry):
+        alpha, beta, norm = carry
+        norm_next, power = totals(advance(0, alpha, beta), lambda k: advance(k, alpha, beta))
         beta = norm_next / norm
-
-        def turn(k, _):
-            dir3[k + 1] = res3[k] + beta * dir3[k + 1]
-            return 0
-
-        lax.fori_loop(0, 64, turn, 0, unroll=16)
-        return norm_next
-
-    lax.fori_loop(0, SWEEPS, sweep, whole(total))
+        return norm_next / (power - beta * norm_next / alpha), beta, norm_next
+
+    alpha, beta, _ = lax.fori_loop(0, SWEEPS - 1, sweep, (norm / power, jnp.zeros((1, 1), F32), norm))
+
+    def finish(k, _):
+        cor3[k + 2] = cor3[k + 2] + alpha * (res3[k] + beta * dir3[k])
+        return 0
+
+    lax.fori_loop(0, 64, finish, 0, unroll=16)
 
     spread_rows, spread_cols = iota((128, 256), 0), iota((128, 256), 1)
     fine_x = spread_cols % 128
@@ -592,6 +625,16 @@
     x_done = dot(jnp.concatenate(mixed, axis=0), from_halves)
     wait_recv(more1 + more2 + z_smooth + y_smooth)
     wait_send(copies2 + more1 + more2 + z_smooth)
+    for way, row in ((0, 14), (1, 33)):
+        for k in range(2):
+            val1[k + 2, row : row + 1, :] = wide_y_in[way, k : k + 1, :]
+    for i, (dz, dy, _) in enumerate(corners):
+        plane, far_plane = (1, 0) if dz == 1 else (4, 5)
+        row, far_row = (15, 14) if dy == 1 else (32, 33)
+        val1[plane, row : row + 1, :] = wide_d_in[i, 0:1, :]
+        val1[plane, far_row : far_row + 1, :] = wide_d_in[i, 1:2, :]
+        val1[far_plane, row : row + 1, :] = wide_d_in[i, 2:3, :]
+        src1[plane, row : row + 1, :] = wide_d_in[i, 3:4, :]
     first_row, last_row = iota((8, 128), 0) == 0, iota((8, 128), 0) == 7
     window = pl.ds(pl.multiple_of(8 * gy, 8), 24)
     for k in range(7):
@@ -606,17 +649,17 @@
         fine_rows[k, pl.ds(11, 8, stride=4), :] = 0.75 * odd + 0.25 * above
         val2[k, 8:32, :] = val2[k, 8:32, :] + fine_rows[k, window, :]
 
-    def in_grid(shape, first_row, rows, plane, planes):
+    def in_grid(shape, margin, first_row, rows, plane, planes):
         row = iota(shape, 0)
         at = row + first_row
-        good = (row > 0) & (row < shape[0] - 1) & (at >= 0) & (at < rows)
+        good = (row >= margin) & (row < shape[0] - margin) & (at >= 0) & (at < rows)
         return good & (plane >= 0) & (plane < planes)
 
     ups = []
     for k in range(5):
         here, near = coarse.neighbours(val2, k, 0, 24)
         up = (1.0 - OMEGA) * here + (16.0 * src2[k + 1, 8:32, :] + near) * idg2[k]
-        ups.append(jnp.where(in_grid((24, 128), 8 * gy - 8, 8 * ny, gz + k - 2, nz), up, 0.0))
+        ups.append(jnp.where(in_grid((24, 128), 1, 8 * gy - 8, 8 * ny, gz + k - 2, nz), up, 0.0))
 
     spread_x1, spread_x0 = spread_matrix(128), spread_matrix(256)
 
@@ -649,7 +692,7 @@
             source = src1[k + 1, 8 + r : 8 + r + m, :]
             parts.append((1.0 - OMEGA) * here + (4.0 * source + near) * idg1[k, r : r + m, :])
         up = jnp.concatenate(parts, axis=0)
-        ups.append(jnp.where(in_grid((32, 256), 16 * gy - 8, 16 * ny, 2 * gz + k - 1, 2 * nz), up, 0.0))
+        ups.append(jnp.where(in_grid((32, 256), 7, 16 * gy - 8, 16 * ny, 2 * gz + k - 1, 2 * nz), up, 0.0))
     for k, plane in ((0, 0), (1, 5)):
         smo0[plane, 8:40, :] = far_smooth[k]
     for k in range(4):
@@ -666,7 +709,7 @@
         outgoing.append(copy)
 
     wait_send(
-        z_dens + z_vals + y_both + dens1_copies + dens2_copies + column_dens + y_smooth + layer_dens
+        z_dens + z_vals + y_both + dens1_copies + dens2_near + dens2_far + column_dens + y_smooth + layer_dens
         + column_src + layer_src + swap_z + swap_y + swap_d
     )
     for copy in outgoing:
@@ -678,11 +721,11 @@
     return [own, pltpu.VMEM((planes, rows + 8, cols), F32), pltpu.VMEM((planes + 1, rows, cols), F32), own, own]
 
 
-COPIES = 6 + 8 + 20 + 8 + 4 + 4 + 8 + 20 + 62 + 30
+COPIES = 6 + 8 + 8 + 4 + 16 + 4 + 4 + 8 + 20 + 62 + 30
 
 
 def per_device(density, right_side, pressure_guess):
-    coarsest = pltpu.VMEM((64, 8, 128), F32)
+    coarsest, longer = pltpu.VMEM((64, 8, 128), F32), pltpu.VMEM((65, 8, 128), F32)
     return pl.pallas_call(
         kernel,
         out_shape=jax.ShapeDtypeStruct(density.shape, F32),
@@ -694,7 +737,6 @@
             *coefficient_scratch(4, 32, 512),
             pltpu.VMEM((6, 48, 256), F32),
             pltpu.VMEM((2, 6, 48, 256), F32),
-            pltpu.VMEM((6, 48, 256), F32),
             *coefficient_scratch(4, 32, 256),
             pltpu.VMEM((7, 40, 128), F32),
             pltpu.VMEM((2, 7, 40, 128), F32),
@@ -708,8 +750,8 @@
             pltpu.VMEM((16, 4, 8, 128), F32),
             pltpu.VMEM((16, 4, 8, 128), F32),
             pltpu.VMEM((66, 8, 128), F32),
-            coarsest, coarsest, pltpu.VMEM((65, 8, 128), F32), coarsest,
-            pltpu.VMEM((66, 8, 128), F32), coarsest, coarsest, pltpu.VMEM((68, 8, 128), F32),
+            coarsest, coarsest, longer, coarsest,
+            longer, longer, longer, longer, pltpu.VMEM((68, 8, 128), F32),
             pltpu.VMEM((8, 256), F32),
             pltpu.VMEM((8, 32, 128), F32),
             pltpu.VMEM((7, 48, 128), F32),
@@ -719,6 +761,8 @@
             *[pltpu.VMEM((2, 2, 16, 256), F32)] * 2,
             *[pltpu.VMEM((2, 4, 256), F32)] * 2,
             *[pltpu.VMEM((4, 2, 256), F32)] * 2,
+            *[pltpu.VMEM((2, 2, 256), F32)] * 2,
+            *[pltpu.VMEM((4, 4, 256), F32)] * 2,
             pltpu.SemaphoreType.DMA((3,)),
             pltpu.SemaphoreType.DMA((4,)),
             pltpu.SemaphoreType.DMA((COPIES,)),

time: 79.7 us -> 76.3 us (0.957)
  Pallas kernels: 75.9 us -> 72.5 us
    pallas_call x1, Pallas kernels: 75.9 us -> 72.5 us  [per_device(): pl.pallas_call(kernel, out_shape=jax.ShapeDtypeStruct(density.shape, F32)...]
where the time goes in v4:
time: 76.3 us; the launch traced here: 76.1 us
  Pallas kernels  72.5 us (95%)
  local copies, waits for them, and re-layouts  3.55 us (5%)
    pallas_call x1, Pallas kernels, per_device(): pl.pallas_call(kernel, out_shape=jax.ShapeDtypeStruct(density.shape, F32)...  72.5 us
    unnamed x7, local copies, waits for them, and re-layouts  3.55 us

profile of v4, /device:TPU:1, one launch (start us, length us, event | category | flops | bytes accessed | tf_op | source)
XLA Modules:
  0.0 76.1 jit_solution(12188021292180369860)
XLA Ops:
  0.0 0.0 copy-start
  0.0 0.9 %copy-done = f32[4,32,512]{2,1,0:T(8,128)S(1)} copy-done((f32[4,32,512]{2,1,0:T(8,128)S(1)}, f32[4,32,512]{2,1,0:T(8,128)}, u32[]{:S(2)}) %copy-start) | copy-done | bytes 262168
  1.0 0.0 copy-start.1
  1.0 0.9 %copy-done.1 = f32[4,32,512]{2,1,0:T(8,128)S(1)} copy-done((f32[4,32,512]{2,1,0:T(8,128)S(1)}, f32[4,32,512]{2,1,0:T(8,128)}, u32[]{:S(2)}) %copy-start.1) | copy-done | bytes 262168
  1.9 0.0 copy-start.2
  1.9 0.9 %copy-done.2 = f32[4,32,512]{2,1,0:T(8,128)S(1)} copy-done((f32[4,32,512]{2,1,0:T(8,128)S(1)}, f32[4,32,512]{2,1,0:T(8,128)}, u32[]{:S(2)}) %copy-start.2) | copy-done | bytes 262168
  2.9 72.5 %shard_map.37 = f32[4,32,512]{2,1,0:T(8,128)S(1)} custom-call(f32[4,32,512]{2,1,0:T(8,128)S(1)} %copy-done, f32[4,32,512]{2,1,0:T(8,128)S(1)} %copy-done.1, f32[4,32,512]{2,1,0:T(8,128)S(1)} %copy-done.2), custom_call_target="tpu_custom_call" | custom-call | flops 20000000 | bytes 1048576 | tf_op jit(solution)/shard_map/pallas_call | solution.py:729
  75.4 0.7 copy.5
Async XLA Ops:
  0.0 0.9 %copy-start = (f32[4,32,512]{2,1,0:T(8,128)S(1)}, f32[4,32,512]{2,1,0:T(8,128)}, u32[]{:S(2)}) copy-start(f32[4,32,512]{2,1,0:T(8,128)} %dens_in.1) | copy-start | bytes 786436
  1.0 0.9 %copy-start.1 = (f32[4,32,512]{2,1,0:T(8,128)S(1)}, f32[4,32,512]{2,1,0:T(8,128)}, u32[]{:S(2)}) copy-start(f32[4,32,512]{2,1,0:T(8,128)} %right_in.1) | copy-start | bytes 786436
  1.9 0.9 %copy-start.2 = (f32[4,32,512]{2,1,0:T(8,128)S(1)}, f32[4,32,512]{2,1,0:T(8,128)}, u32[]{:S(2)}) copy-start(f32[4,32,512]{2,1,0:T(8,128)} %guess_in.1) | copy-start | bytes 786436

commit v5 on v4

--- a/solution.py
+++ b/solution.py
@@ -122,7 +122,8 @@
     rho2, pair2, bx2, by2, bz2, dg2, idg2,
     rows_out, rows_in, message, inbox_dens, inbox_src, tile, wide_dens, wide_src,
     rho3, bx3, by3, bz3, dg3, dir3, res3, img3, mul3, cor3, pair_tmp, pair_rows, fine_rows, result,
-    far_smooth, face_rows, z_out, z_in, y_out, y_in, d_out, d_in, wide_y_out, wide_y_in, wide_d_out, wide_d_in, local_sem, out_sem, send_sem, recv_sem,
+    far_smooth, face_rows, z_out, z_in, y_out, y_in, d_out, d_in, wide_y_out, wide_y_in, wide_d_out, wide_d_in,
+    dens_y_out, dens_y_in, dens_d_out, dens_d_in, local_sem, out_sem, send_sem, recv_sem,
 ):
     gz, gy = lax.axis_index("gz"), lax.axis_index("gy")
     nz, ny = 128, 4
@@ -258,6 +259,15 @@
             rows_out[0, f, k : k + 1, :] = ref[k + 1, 39:40, :]
             rows_out[1, f, k : k + 1, :] = ref[k + 1, 8:9, :]
 
+    for way, (row, second) in enumerate(((31, 30), (16, 17))):
+        for k in range(2):
+            dens_y_out[way, 2 * k : 2 * k + 1, :] = rho1[k + 2, row : row + 1, :]
+            dens_y_out[way, 2 * k + 1 : 2 * k + 2, :] = rho1[k + 2, second : second + 1, :]
+    for i, (dz, dy, device) in enumerate(corners):
+        plane, far_plane = (3, 2) if dz == 1 else (2, 3)
+        row, second = (31, 30) if dy == 1 else (16, 17)
+        for at, (p, r) in enumerate(((plane, row), (plane, second), (far_plane, row), (far_plane, second))):
+            dens_d_out[i, at : at + 1, :] = rho1[p, r : r + 1, :]
     for k in (0, 5):
         smo0[k, 8:40, :] = jnp.zeros((32, 512), F32)
     for k in range(1, 5):
@@ -279,13 +289,18 @@
         send(rows_out.at[1, 0:2], rows_in.at[1, 0:2], faces[3]),
     ]
 
-    rows1 = {0: (slice(16, 32), slice(16, 32)), 1: (slice(24, 32), slice(8, 16)), -1: (slice(16, 24), slice(32, 40))}
+    dens1_copies = [
+        send(rho1.at[2:4, 16:32, :], rho1.at[0:2, 16:32, :], faces[0]),
+        send(rho1.at[2:4, 16:32, :], rho1.at[4:6, 16:32, :], faces[1]),
+        send(dens_y_out.at[0], dens_y_in.at[0], faces[2]),
+        send(dens_y_out.at[1], dens_y_in.at[1], faces[3]),
+    ]
+    for i, (dz, dy, device) in enumerate(corners):
+        dens1_copies.append(send(dens_d_out.at[i], dens_d_in.at[i], device))
+
     rows2 = {dy: (slice(16, 24), slice(16 - 8 * dy, 24 - 8 * dy)) for dy in (0, 1, -1)}
     y_ways = ((1, faces[2]), (-1, faces[3]))
     z_ways = ((1, faces[0]), (-1, faces[1]))
-
-    def planes1(dz):
-        return slice(2 - 2 * dz, 4 - 2 * dz)
 
     def fill_y(ref, planes, rows, first):
         last = first + rows - 1
@@ -335,15 +350,6 @@
         fine.mask_y(k, ((0, y_low), (32, y_high)))
     fine.mask_z(((0, z_low), (4, z_high)))
     wait_recv(z_vals)
-    dens1_copies = [
-        send(rho1.at[2:4, 16:32, :], rho1.at[planes1(dz), 16:32, :], device) for dz, device in z_ways
-    ]
-    for dy, device in y_ways:
-        source, target = rows1[dy]
-        dens1_copies.append(send(rho1.at[2:4, source, :], rho1.at[2:4, target, :], device))
-    for dz, dy, device in corners:
-        source, target = rows1[dy]
-        dens1_copies.append(send(rho1.at[2:4, source, :], rho1.at[planes1(dz), target, :], device))
     smooth(3)
     smooth(0)
 
@@ -400,6 +406,15 @@
         level.mask_z(z_faces)
 
     wait_recv(dens1_copies)
+    for way, (row, second) in enumerate(((15, 14), (32, 33))):
+        for k in range(2):
+            rho1[k + 2, row : row + 1, :] = dens_y_in[way, 2 * k : 2 * k + 1, :]
+            rho1[k + 2, second : second + 1, :] = dens_y_in[way, 2 * k + 1 : 2 * k + 2, :]
+    for i, (dz, dy, device) in enumerate(corners):
+        plane, far_plane = (1, 0) if dz == 1 else (4, 5)
+        row, second = (15, 14) if dy == 1 else (32, 33)
+        for at, (p, r) in enumerate(((plane, row), (plane, second), (far_plane, row), (far_plane, second))):
+            rho1[p, r : r + 1, :] = dens_d_in[i, at : at + 1, :]
     fill_y(rho1, range(6), 16, 16)
     fill_z(rho1, 2, 2, slice(8, 40), 1)
     coefficients(middle, range(4), ((1, z_low), (3, z_high)))
@@ -443,92 +458,10 @@
     for dz, device in z_ways:
         copies2.append(send(val2.at[3, 16:24, :], val2.at[3 - dz, 16:24, :], device))
 
-    z_smooth = [
-        send(smo0.at[4, 8:40, :], far_smooth.at[0], faces[0]), send(smo0.at[1, 8:40, :], far_smooth.at[1], faces[1])
-    ]
-    for k in range(4):
-        rows_out[0, 2, k : k + 1, :] = smo0[k + 1, 39:40, :]
-        rows_out[1, 2, k : k + 1, :] = smo0[k + 1, 8:9, :]
-    y_smooth = [send(rows_out.at[way, 2], rows_in.at[way, 2], faces[2 + way]) for way in range(2)]
     dens2_far = [
         send(rho2.at[3, 16:24, :], rho2.at[3 - dz, rows2[dy][1], :], device)
         for dz, dy, device in around if abs(dz) > 1 or dy
     ]
-    wait_recv(column_dens)
-    layer_dens = gather_layer(0, inbox_dens, wide_dens)
-    wait_recv(copies2)
-    here, near = coarse.neighbours(val2, 2, 8, 8)
-    pack_message(1, (1.0 - OMEGA) * source2 + 0.0625 * near)
-    column_src = gather_column(1, inbox_src)
-
-    wait_recv(layer_dens)
-    lane, sub = iota((8, 128), 1), iota((8, 128), 0)
-    right_half = lane >= 64
-    first_x, last_x = (lane % 64) == 0, (lane % 64) == 63
-    first_y, last_y = (lane < 64) & (sub == 0), (lane >= 64) & (sub == 7)
-
-    def lower_y(v):
-        q = pltpu.roll(v, 64, 1)
-        return jnp.where(right_half, q, pltpu.roll(q, 1, 0))
-
-    def upper_y(v):
-        q = pltpu.roll(v, 64, 1)
-        return jnp.where(right_half, pltpu.roll(q, 7, 0), q)
-
-    scale3 = 0.015625
-    for zh in range(4):
-        for s in range(16):
-            rho3[1 + 16 * zh + s] = wide_dens[s, zh]
-    rho3[0] = rho3[1]
-    rho3[65] = rho3[64]
-
-    def face3(k, _):
-        bz3[k] = scale3 * twice_inverse(rho3[k] + rho3[k + 1])
-        return 0
-
-    lax.fori_loop(0, 65, face3, 0)
-
-    def coef3(k, _):
-        rho = rho3[k + 1]
-        edge = twice_inverse(rho + rho)
-        low = twice_inverse(rho + jnp.where(first_x, rho, pltpu.roll(rho, 1, 1)))
-        total = low + jnp.where(last_x, edge, pltpu.roll(low, 127, 1))
-        bx3[k] = jnp.where(first_x, 0.0, scale3 * low)
-        low = twice_inverse(rho + jnp.where(first_y, rho, lower_y(rho)))
-        total = total + low + jnp.where(last_y, edge, upper_y(low))
-        by3[k] = jnp.where(first_y, 0.0, scale3 * low)
-        dg3[k] = scale3 * total + bz3[k] + bz3[k + 1]
-        return 0
-
-    lax.fori_loop(0, 64, coef3, 0, unroll=4)
-
-    wait_recv(dens2_far)
-
-    def inside_z(face):
-        at = gz + face - 2
-        return jnp.where((at > 0) & (at < nz), 1.0, 0.0).astype(F32)
-
-    fill_y(rho2, range(7), 8, 16)
-    fill_z(rho2, 3, 1, slice(8, 32), 3)
-    coefficients(coarse, range(5), [(face, inside_z(face)) for face in range(6)])
-
-    zero_plane = jnp.zeros((8, 128), F32)
-    for k in (0, 1, 66, 67):
-        cor3[k] = zero_plane
-
-    def clear3(k, _):
-        dir3[k] = zero_plane
-        mul3[k] = zero_plane
-        cor3[k + 2] = zero_plane
-        return 0
-
-    lax.fori_loop(0, 64, clear3, 0, unroll=8)
-    for ref in (dir3, mul3, res3, img3):
-        ref[64] = zero_plane
-
-    wait_recv(column_src)
-    layer_src = gather_layer(1, inbox_src, wide_src)
-
     more1 = [
         send(val1.at[2, 16:32, :], val1.at[0, 16:32, :], faces[0]),
         send(val1.at[3, 16:32, :], val1.at[5, 16:32, :], faces[1]),
@@ -554,6 +487,88 @@
             more2.append(send(val2.at[3, 16:24, :], val2.at[3 - dz, target, :], device))
         else:
             more2.append(send(pair2.at[:, 3, 16:24, :], pair2.at[:, 3 - dz, target, :], device))
+    wait_recv(column_dens)
+    layer_dens = gather_layer(0, inbox_dens, wide_dens)
+    wait_recv(copies2)
+    here, near = coarse.neighbours(val2, 2, 8, 8)
+    pack_message(1, (1.0 - OMEGA) * source2 + 0.0625 * near)
+    column_src = gather_column(1, inbox_src)
+
+    wait_recv(layer_dens)
+    lane, sub = iota((8, 128), 1), iota((8, 128), 0)
+    right_half = lane >= 64
+    first_x, last_x = (lane % 64) == 0, (lane % 64) == 63
+    first_y, last_y = (lane < 64) & (sub == 0), (lane >= 64) & (sub == 7)
+
+    def lower_y(v):
+        q = pltpu.roll(v, 64, 1)
+        return jnp.where(right_half, q, pltpu.roll(q, 1, 0))
+
+    def upper_y(v):
+        q = pltpu.roll(v, 64, 1)
+        return jnp.where(right_half, pltpu.roll(q, 7, 0), q)
+
+    scale3 = 0.015625
+    for zh in range(4):
+        for s in range(16):
+            rho3[1 + 16 * zh + s] = wide_dens[s, zh]
+    rho3[0] = rho3[1]
+    rho3[65] = rho3[64]
+
+    def face3(k, _):
+        bz3[k] = scale3 * twice_inverse(rho3[k] + rho3[k + 1])
+        return 0
+
+    lax.fori_loop(0, 65, face3, 0)
+
+    def coef3(k, _):
+        rho = rho3[k + 1]
+        edge = twice_inverse(rho + rho)
+        low = twice_inverse(rho + jnp.where(first_x, rho, pltpu.roll(rho, 1, 1)))
+        total = low + jnp.where(last_x, edge, pltpu.roll(low, 127, 1))
+        bx3[k] = jnp.where(first_x, 0.0, scale3 * low)
+        low = twice_inverse(rho + jnp.where(first_y, rho, lower_y(rho)))
+        total = total + low + jnp.where(last_y, edge, upper_y(low))
+        by3[k] = jnp.where(first_y, 0.0, scale3 * low)
+        dg3[k] = scale3 * total + bz3[k] + bz3[k + 1]
+        return 0
+
+    lax.fori_loop(0, 64, coef3, 0, unroll=4)
+
+    wait_recv(dens2_far)
+
+    def inside_z(face):
+        at = gz + face - 2
+        return jnp.where((at > 0) & (at < nz), 1.0, 0.0).astype(F32)
+
+    fill_y(rho2, range(7), 8, 16)
+    fill_z(rho2, 3, 1, slice(8, 32), 3)
+    coefficients(coarse, range(5), [(face, inside_z(face)) for face in range(6)])
+
+    zero_plane = jnp.zeros((8, 128), F32)
+    for k in (0, 1, 66, 67):
+        cor3[k] = zero_plane
+
+    def clear3(k, _):
+        dir3[k] = zero_plane
+        mul3[k] = zero_plane
+        cor3[k + 2] = zero_plane
+        return 0
+
+    lax.fori_loop(0, 64, clear3, 0, unroll=8)
+    for ref in (dir3, mul3, res3, img3):
+        ref[64] = zero_plane
+
+    wait_recv(column_src)
+    layer_src = gather_layer(1, inbox_src, wide_src)
+
+    z_smooth = [
+        send(smo0.at[4, 8:40, :], far_smooth.at[0], faces[0]), send(smo0.at[1, 8:40, :], far_smooth.at[1], faces[1])
+    ]
+    for k in range(4):
+        rows_out[0, 2, k : k + 1, :] = smo0[k + 1, 39:40, :]
+        rows_out[1, 2, k : k + 1, :] = smo0[k + 1, 8:9, :]
+    y_smooth = [send(rows_out.at[way, 2], rows_in.at[way, 2], faces[2 + way]) for way in range(2)]
     wait_recv(layer_src)
 
     for zh in range(4):
@@ -763,13 +778,15 @@
             *[pltpu.VMEM((4, 2, 256), F32)] * 2,
             *[pltpu.VMEM((2, 2, 256), F32)] * 2,
             *[pltpu.VMEM((4, 4, 256), F32)] * 2,
+            *[pltpu.VMEM((2, 4, 256), F32)] * 2,
+            *[pltpu.VMEM((4, 4, 256), F32)] * 2,
             pltpu.SemaphoreType.DMA((3,)),
             pltpu.SemaphoreType.DMA((4,)),
             pltpu.SemaphoreType.DMA((COPIES,)),
             pltpu.SemaphoreType.DMA((COPIES,)),
         ],
         compiler_params=pltpu.CompilerParams(
-            collective_id=0, has_side_effects=True, vmem_limit_bytes=32 * 1024 * 1024
+            collective_id=0, has_side_effects=True, vmem_limit_bytes=63 * 1024 * 1024
         ),
         cost_estimate=pl.CostEstimate(flops=20_000_000, bytes_accessed=1 << 20, transcendentals=0),
     )(density, right_side, pressure_guess)

time: 76.3 us -> 69.4 us (0.910)
  Pallas kernels: 72.5 us -> 67.5 us
  local copies, waits for them, and re-layouts: 3.55 us -> 1.67 us
    pallas_call x1, Pallas kernels: 72.5 us -> 67.5 us  [per_device(): pl.pallas_call(kernel, out_shape=jax.ShapeDtypeStruct(density.shape, F32)...]
    unnamed x7 -> x1, local copies, waits for them, and re-layouts: 3.55 us -> 1.67 us
where the time goes in v5:
time: 69.4 us; the launch traced here: 69.2 us
  Pallas kernels  67.5 us (97%)
  local copies, waits for them, and re-layouts  1.67 us (2%)
    pallas_call x1, Pallas kernels, per_device(): pl.pallas_call(kernel, out_shape=jax.ShapeDtypeStruct(density.shape, F32)...  67.5 us
    unnamed x1, local copies, waits for them, and re-layouts  1.67 us

profile of v5, /device:TPU:1, one launch (start us, length us, event | category | flops | bytes accessed | tf_op | source)
XLA Modules:
  0.0 69.2 jit_solution(9342491780239219350)
XLA Ops:
  0.0 67.5 %shard_map.37 = f32[4,32,512]{2,1,0:T(8,128)} custom-call(f32[4,32,512]{2,1,0:T(8,128)} %dens_in.1, f32[4,32,512]{2,1,0:T(8,128)} %right_in.1, f32[4,32,512]{2,1,0:T(8,128)} %guess_in.1), custom_call_target="tpu_custom_call" | custom-call | flops 20000000 | bytes 1048576 | tf_op jit(solution)/shard_map/pallas_call | solution.py:744
  67.5 1.7 %copy.5 = f32[4,32,512]{2,1,0:T(8,128)} copy(f32[4,32,512]{2,1,0:T(8,128)} %shard_map.37) | data formatting | bytes 524288

commit v6 on v5

--- a/solution.py
+++ b/solution.py
@@ -118,8 +118,8 @@
 def kernel(
     dens_in, right_in, guess_in, out,
     rho0, val0, smo0, src0, res0, bx0, by0, bz0, dg0, idg0,
-    rho1, pair1, bx1, by1, bz1, dg1, idg1,
-    rho2, pair2, bx2, by2, bz2, dg2, idg2,
+    rho1, val1, src1, base1, up1, bx1, by1, bz1, dg1, idg1,
+    rho2, val2, base2, up2, bx2, by2, bz2, dg2, idg2,
     rows_out, rows_in, message, inbox_dens, inbox_src, tile, wide_dens, wide_src,
     rho3, bx3, by3, bz3, dg3, dir3, res3, img3, mul3, cor3, pair_tmp, pair_rows, fine_rows, result,
     far_smooth, face_rows, z_out, z_in, y_out, y_in, d_out, d_in, wide_y_out, wide_y_in, wide_d_out, wide_d_in,
@@ -148,10 +148,10 @@
                 layer.append((gz_of(zhi, (xpos + i) % 4, (ypos + j) % 4, core), gy))
     faces = [(up_z, gy), (down_z, gy), (gz, up_y), (gz, down_y)]
     around = []
-    for dz in (1, -1, 2, -2, 3, -3):
+    for dz in (1, -1):
         for dy in (0, 1, -1):
             around.append((dz, dy, ((gz + dz + nz) % nz, (gy + dy + ny) % ny)))
-    corners = [(dz, dy, device) for dz, dy, device in around if abs(dz) == 1 and dy]
+    corners = [(dz, dy, device) for dz, dy, device in around if dy]
     greeted = column + [device for _, _, device in around] + faces[2:] + layer
 
     barrier = pltpu.get_barrier_semaphore()
@@ -189,7 +189,6 @@
     fine = Level((4, 32, 512), 8, rho0, bx0, by0, bz0, dg0, idg0)
     middle = Level((4, 32, 256), 16, rho1, bx1, by1, bz1, dg1, idg1)
     coarse = Level((5, 24, 128), 8, rho2, bx2, by2, bz2, dg2, idg2)
-    val1, src1, val2, src2 = pair1.at[0], pair1.at[1], pair2.at[0], pair2.at[1]
 
     z_low = jnp.where(gz > 0, 1.0, 0.0).astype(F32)
     z_high = jnp.where(gz < nz - 1, 1.0, 0.0).astype(F32)
@@ -392,7 +391,9 @@
         swap_d.append(send(d_out.at[i], d_in.at[i], device))
     column_dens = gather_column(0, inbox_dens)
     dens2_near = [send(rho2.at[3, 16:24, :], rho2.at[3, rows2[dy][1], :], device) for dy, device in y_ways]
-    dens2_near += [send(rho2.at[3, 16:24, :], rho2.at[3 - dz, 16:24, :], device) for dz, device in z_ways]
+    dens2_near += [
+        send(rho2.at[3, 16:24, :], rho2.at[3 - dz, rows2[dy][1], :], device) for dz, dy, device in around
+    ]
 
     def coefficients(level, planes, z_faces):
         for k in planes:
@@ -449,50 +450,45 @@
 
     def residual1(k):
         here, near = middle.neighbours(val1, k + 1, 8, 16)
+        base1[k + 2, 16:32, :] = (1.0 - OMEGA) * here + (4.0 * source1[k] + near) * idg1[k + 1, 8:24, :]
         return (1.0 - OMEGA) * source1[k] + 0.25 * near
 
     source2 = restrict1(residual1)
-    src2[3, 16:24, :] = source2
     val2[3, 16:24, :] = 16.0 * source2 * idg2[2, 8:16, :]
     copies2 = [send(val2.at[3, 16:24, :], val2.at[3, rows2[dy][1], :], device) for dy, device in y_ways]
     for dz, device in z_ways:
         copies2.append(send(val2.at[3, 16:24, :], val2.at[3 - dz, 16:24, :], device))
 
-    dens2_far = [
-        send(rho2.at[3, 16:24, :], rho2.at[3 - dz, rows2[dy][1], :], device)
-        for dz, dy, device in around if abs(dz) > 1 or dy
+    def pass_on(ref, reach):
+        return [
+            send(ref.at[4 - reach, 8:32, :], ref.at[3 - reach, 8:32, :], faces[0]),
+            send(ref.at[2 + reach, 8:32, :], ref.at[3 + reach, 8:32, :], faces[1]),
+        ]
+
+    dens2_far = pass_on(rho2, 2)
+    more1 = [
+        send(base1.at[3, 16:32, :], base1.at[1, 16:32, :], faces[0]),
+        send(base1.at[2, 16:32, :], base1.at[4, 16:32, :], faces[1]),
     ]
-    more1 = [
-        send(val1.at[2, 16:32, :], val1.at[0, 16:32, :], faces[0]),
-        send(val1.at[3, 16:32, :], val1.at[5, 16:32, :], faces[1]),
-    ]
-    for way, row in ((0, 30), (1, 17)):
+    for way, row in ((0, 31), (1, 16)):
         for k in range(2):
-            wide_y_out[way, k : k + 1, :] = val1[k + 2, row : row + 1, :]
+            wide_y_out[way, k : k + 1, :] = base1[k + 2, row : row + 1, :]
         more1.append(send(wide_y_out.at[way], wide_y_in.at[way], faces[2 + way]))
     for i, (dz, dy, device) in enumerate(corners):
-        plane, far_plane = (3, 2) if dz == 1 else (2, 3)
-        row, far_row = (31, 30) if dy == 1 else (16, 17)
-        wide_d_out[i, 0:1, :] = val1[plane, row : row + 1, :]
-        wide_d_out[i, 1:2, :] = val1[plane, far_row : far_row + 1, :]
-        wide_d_out[i, 2:3, :] = val1[far_plane, row : row + 1, :]
-        wide_d_out[i, 3:4, :] = src1[plane, row : row + 1, :]
+        plane, row = (3 if dz == 1 else 2), (31 if dy == 1 else 16)
+        wide_d_out[i] = base1[plane, row : row + 1, :]
         more1.append(send(wide_d_out.at[i], wide_d_in.at[i], device))
-    more2 = [send(src2.at[3, 16:24, :], src2.at[3, rows2[dy][1], :], device) for dy, device in y_ways]
-    for dz, dy, device in around:
-        target = rows2[dy][1]
-        if abs(dz) == 1 and dy == 0:
-            more2.append(send(src2.at[3, 16:24, :], src2.at[3 - dz, target, :], device))
-        elif abs(dz) == 3:
-            more2.append(send(val2.at[3, 16:24, :], val2.at[3 - dz, target, :], device))
-        else:
-            more2.append(send(pair2.at[:, 3, 16:24, :], pair2.at[:, 3 - dz, target, :], device))
     wait_recv(column_dens)
     layer_dens = gather_layer(0, inbox_dens, wide_dens)
     wait_recv(copies2)
     here, near = coarse.neighbours(val2, 2, 8, 8)
     pack_message(1, (1.0 - OMEGA) * source2 + 0.0625 * near)
+    base2[3, 16:24, :] = (1.0 - OMEGA) * here + (16.0 * source2 + near) * idg2[2, 8:16, :]
     column_src = gather_column(1, inbox_src)
+    more2 = [send(base2.at[3, 16:24, :], base2.at[3, rows2[dy][1], :], device) for dy, device in y_ways]
+    more2 += [send(base2.at[3, 16:24, :], base2.at[3 - dz, rows2[dy][1], :], device) for dz, dy, device in around]
+    wait_recv(dens2_far)
+    dens2_last = pass_on(rho2, 3)
 
     wait_recv(layer_dens)
     lane, sub = iota((8, 128), 1), iota((8, 128), 0)
@@ -535,16 +531,6 @@
 
     lax.fori_loop(0, 64, coef3, 0, unroll=4)
 
-    wait_recv(dens2_far)
-
-    def inside_z(face):
-        at = gz + face - 2
-        return jnp.where((at > 0) & (at < nz), 1.0, 0.0).astype(F32)
-
-    fill_y(rho2, range(7), 8, 16)
-    fill_z(rho2, 3, 1, slice(8, 32), 3)
-    coefficients(coarse, range(5), [(face, inside_z(face)) for face in range(6)])
-
     zero_plane = jnp.zeros((8, 128), F32)
     for k in (0, 1, 66, 67):
         cor3[k] = zero_plane
@@ -569,6 +555,20 @@
         rows_out[0, 2, k : k + 1, :] = smo0[k + 1, 39:40, :]
         rows_out[1, 2, k : k + 1, :] = smo0[k + 1, 8:9, :]
     y_smooth = [send(rows_out.at[way, 2], rows_in.at[way, 2], faces[2 + way]) for way in range(2)]
+    wait_recv(more2)
+    base2_far = pass_on(base2, 2)
+
+    wait_recv(dens2_last)
+    wait_send(dens2_near + dens2_far + dens2_last)
+
+    def inside_z(face):
+        at = gz + face - 2
+        return jnp.where((at > 0) & (at < nz), 1.0, 0.0).astype(F32)
+
+    fill_y(rho2, range(7), 8, 16)
+    fill_z(rho2, 3, 1, slice(8, 32), 3)
+    coefficients(coarse, range(5), [(face, inside_z(face)) for face in range(6)])
+
     wait_recv(layer_src)
 
     for zh in range(4):
@@ -638,18 +638,14 @@
         other = index + 2 * (plane % 2) - 1
         mixed.append(0.75 * cor3[index] + 0.25 * cor3[other])
     x_done = dot(jnp.concatenate(mixed, axis=0), from_halves)
-    wait_recv(more1 + more2 + z_smooth + y_smooth)
-    wait_send(copies2 + more1 + more2 + z_smooth)
-    for way, row in ((0, 14), (1, 33)):
+    wait_recv(more1 + base2_far + z_smooth + y_smooth)
+    wait_send(more1 + more2 + base2_far + z_smooth)
+    for way, row in ((0, 15), (1, 32)):
         for k in range(2):
-            val1[k + 2, row : row + 1, :] = wide_y_in[way, k : k + 1, :]
+            base1[k + 2, row : row + 1, :] = wide_y_in[way, k : k + 1, :]
     for i, (dz, dy, _) in enumerate(corners):
-        plane, far_plane = (1, 0) if dz == 1 else (4, 5)
-        row, far_row = (15, 14) if dy == 1 else (32, 33)
-        val1[plane, row : row + 1, :] = wide_d_in[i, 0:1, :]
-        val1[plane, far_row : far_row + 1, :] = wide_d_in[i, 1:2, :]
-        val1[far_plane, row : row + 1, :] = wide_d_in[i, 2:3, :]
-        src1[plane, row : row + 1, :] = wide_d_in[i, 3:4, :]
+        plane, row = (1 if dz == 1 else 4), (15 if dy == 1 else 32)
+        base1[plane, row : row + 1, :] = wide_d_in[i]
     first_row, last_row = iota((8, 128), 0) == 0, iota((8, 128), 0) == 7
     window = pl.ds(pl.multiple_of(8 * gy, 8), 24)
     for k in range(7):
@@ -662,7 +658,7 @@
         fine_rows[k, pl.ds(9, 8, stride=4), :] = 0.75 * even + 0.25 * odd
         fine_rows[k, pl.ds(10, 8, stride=4), :] = 0.75 * odd + 0.25 * even
         fine_rows[k, pl.ds(11, 8, stride=4), :] = 0.75 * odd + 0.25 * above
-        val2[k, 8:32, :] = val2[k, 8:32, :] + fine_rows[k, window, :]
+        up2[k, 8:32, :] = fine_rows[k, window, :]
 
     def in_grid(shape, margin, first_row, rows, plane, planes):
         row = iota(shape, 0)
@@ -672,13 +668,13 @@
 
     ups = []
     for k in range(5):
-        here, near = coarse.neighbours(val2, k, 0, 24)
-        up = (1.0 - OMEGA) * here + (16.0 * src2[k + 1, 8:32, :] + near) * idg2[k]
+        here, near = coarse.neighbours(up2, k, 0, 24)
+        up = base2[k + 1, 8:32, :] + (1.0 - OMEGA) * here + near * idg2[k]
         ups.append(jnp.where(in_grid((24, 128), 1, 8 * gy - 8, 8 * ny, gz + k - 2, nz), up, 0.0))
 
     spread_x1, spread_x0 = spread_matrix(128), spread_matrix(256)
 
-    def prolong(ups, target, first, rows, spread_x):
+    def prolong(ups, target, first, rows, spread_x, add):
         height = ups[0].shape[0]
         tall = 2 * height - 16
         n = height - 8
@@ -694,18 +690,17 @@
             for k in range(6):
                 parent_z = (k + first) // 2
                 near_z = parent_z + 2 * ((k + first) % 2) - 1
-                target[k, rows, cols] = (
-                    target[k, rows, cols] + 0.75 * fine_rows[parent_z, 0:tall, :] + 0.25 * fine_rows[near_z, 0:tall, :]
-                )
-
-    prolong(ups, val1, 2, slice(8, 40), spread_x1)
+                value = 0.75 * fine_rows[parent_z, 0:tall, :] + 0.25 * fine_rows[near_z, 0:tall, :]
+                target[k, rows, cols] = target[k, rows, cols] + value if add else value
+
+    prolong(ups, up1, 2, slice(8, 40), spread_x1, False)
     ups = []
     for k in range(4):
         parts = []
         for r, m in middle.chunks():
-            here, near = middle.neighbours(val1, k, r, m)
-            source = src1[k + 1, 8 + r : 8 + r + m, :]
-            parts.append((1.0 - OMEGA) * here + (4.0 * source + near) * idg1[k, r : r + m, :])
+            here, near = middle.neighbours(up1, k, r, m)
+            base = base1[k + 1, 8 + r : 8 + r + m, :]
+            parts.append(base + (1.0 - OMEGA) * here + near * idg1[k, r : r + m, :])
         up = jnp.concatenate(parts, axis=0)
         ups.append(jnp.where(in_grid((32, 256), 7, 16 * gy - 8, 16 * ny, 2 * gz + k - 1, 2 * nz), up, 0.0))
     for k, plane in ((0, 0), (1, 5)):
@@ -713,7 +708,7 @@
     for k in range(4):
         smo0[k + 1, 7:8, :] = rows_in[0, 2, k : k + 1, :]
         smo0[k + 1, 40:41, :] = rows_in[1, 2, k : k + 1, :]
-    prolong(ups, smo0, 1, slice(0, 48), spread_x0)
+    prolong(ups, smo0, 1, slice(0, 48), spread_x0, True)
     outgoing = []
     for k in range(4):
         for r, m in fine.chunks():
@@ -724,7 +719,7 @@
         outgoing.append(copy)
 
     wait_send(
-        z_dens + z_vals + y_both + dens1_copies + dens2_near + dens2_far + column_dens + y_smooth + layer_dens
+        z_dens + z_vals + y_both + dens1_copies + copies2 + column_dens + y_smooth + layer_dens
         + column_src + layer_src + swap_z + swap_y + swap_d
     )
     for copy in outgoing:
@@ -736,7 +731,7 @@
     return [own, pltpu.VMEM((planes, rows + 8, cols), F32), pltpu.VMEM((planes + 1, rows, cols), F32), own, own]
 
 
-COPIES = 6 + 8 + 8 + 4 + 16 + 4 + 4 + 8 + 20 + 62 + 30
+COPIES = 6 + 8 + 8 + 8 + 2 + 2 + 4 + 4 + 8 + 8 + 2 + 62 + 30
 
 
 def per_device(density, right_side, pressure_guess):
@@ -751,10 +746,10 @@
             *[pltpu.VMEM((4, 32, 512), F32)] * 2,
             *coefficient_scratch(4, 32, 512),
             pltpu.VMEM((6, 48, 256), F32),
-            pltpu.VMEM((2, 6, 48, 256), F32),
+            *[pltpu.VMEM((6, 48, 256), F32)] * 4,
             *coefficient_scratch(4, 32, 256),
             pltpu.VMEM((7, 40, 128), F32),
-            pltpu.VMEM((2, 7, 40, 128), F32),
+            *[pltpu.VMEM((7, 40, 128), F32)] * 3,
             *coefficient_scratch(5, 24, 128),
             pltpu.VMEM((2, 3, 4, 512), F32),
             pltpu.VMEM((2, 3, 4, 512), F32),
@@ -777,7 +772,7 @@
             *[pltpu.VMEM((2, 4, 256), F32)] * 2,
             *[pltpu.VMEM((4, 2, 256), F32)] * 2,
             *[pltpu.VMEM((2, 2, 256), F32)] * 2,
-            *[pltpu.VMEM((4, 4, 256), F32)] * 2,
+            *[pltpu.VMEM((4, 1, 256), F32)] * 2,
             *[pltpu.VMEM((2, 4, 256), F32)] * 2,
             *[pltpu.VMEM((4, 4, 256), F32)] * 2,
             pltpu.SemaphoreType.DMA((3,)),
@@ -786,10 +781,10 @@
             pltpu.SemaphoreType.DMA((COPIES,)),
         ],
         compiler_params=pltpu.CompilerParams(
-            collective_id=0, has_side_effects=True, vmem_limit_bytes=63 * 1024 * 1024
+            collective_id=0, has_side_effects=True, vmem_limit_bytes=32 * 1024 * 1024
         ),
         cost_estimate=pl.CostEstimate(flops=20_000_000, bytes_accessed=1 << 20, transcendentals=0),
-    )(density, right_side, pressure_guess)
+    )(*[pltpu.with_memory_space_constraint(a, pltpu.HBM) for a in (density, right_side, pressure_guess)])
 
 
 def solution(mesh):

time: 69.4 us -> 66.5 us (0.958); the launches traced: 69.2 us -> 65.3 us
  Pallas kernels: 67.5 us -> 64.6 us
  local copies, waits for them, and re-layouts: 1.67 us -> 0.71 us
    pallas_call x1, Pallas kernels: 67.5 us -> 64.6 us  [per_device(): pl.pallas_call(kernel, out_shape=jax.ShapeDtypeStruct(density.shape, F32)...]
    unnamed x1, local copies, waits for them, and re-layouts: 1.67 us -> 0.71 us
where the time goes in v6:
time: 66.5 us; the launch traced here: 65.3 us
  Pallas kernels  64.6 us (97%)
  local copies, waits for them, and re-layouts  0.71 us (1%)
    pallas_call x1, Pallas kernels, per_device(): pl.pallas_call(kernel, out_shape=jax.ShapeDtypeStruct(density.shape, F32)...  64.6 us

profile of v6, /device:TPU:1, one launch (start us, length us, event | category | flops | bytes accessed | tf_op | source)
XLA Modules:
  0.0 65.3 jit_solution(15031829979520990435)
XLA Ops:
  0.0 64.6 %shard_map.37 = f32[4,32,512]{2,1,0:T(8,128)S(1)} custom-call(f32[4,32,512]{2,1,0:T(8,128)} %dens_in.1, f32[4,32,512]{2,1,0:T(8,128)} %right_in.1, f32[4,32,512]{2,1,0:T(8,128)} %guess_in.1), custom_call_target="tpu_custom_call" | custom-call | flops 20000000 | bytes 1048576 | tf_op jit(solution)/shard_map/pallas_call | solution.py:739
  64.6 0.7 %copy.5 = f32[4,32,512]{2,1,0:T(8,128)} copy(f32[4,32,512]{2,1,0:T(8,128)S(1)} %shard_map.37) | data formatting | bytes 524288

commit v7 on v6

--- a/solution.py
+++ b/solution.py
@@ -121,9 +121,9 @@
     rho1, val1, src1, base1, up1, bx1, by1, bz1, dg1, idg1,
     rho2, val2, base2, up2, bx2, by2, bz2, dg2, idg2,
     rows_out, rows_in, message, inbox_dens, inbox_src, tile, wide_dens, wide_src,
-    rho3, bx3, by3, bz3, dg3, dir3, res3, img3, mul3, cor3, pair_tmp, pair_rows, fine_rows, result,
+    rho3, bx3, by3, bz3, dg3, dir3, res3, img3, mul3, cor3, pair_tmp, pair_rows, fine_rows,
     far_smooth, face_rows, z_out, z_in, y_out, y_in, d_out, d_in, wide_y_out, wide_y_in, wide_d_out, wide_d_in,
-    dens_y_out, dens_y_in, dens_d_out, dens_d_in, local_sem, out_sem, send_sem, recv_sem,
+    dens_y_out, dens_y_in, dens_d_out, dens_d_in, local_sem, send_sem, recv_sem,
 ):
     gz, gy = lax.axis_index("gz"), lax.axis_index("gy")
     nz, ny = 128, 4
@@ -142,8 +142,8 @@
                 z = (zpos + d) % 16
                 column.append((gz_of(z // 4, xpos, ypos, (core + k) % 2), z % 4))
     layer = []
-    for i in range(4):
-        for j in range(4):
+    for i in (2, 1, 3, 0):
+        for j in (2, 1, 3, 0):
             if i or j:
                 layer.append((gz_of(zhi, (xpos + i) % 4, (ypos + j) % 4, core), gy))
     faces = [(up_z, gy), (down_z, gy), (gz, up_y), (gz, down_y)]
@@ -532,18 +532,20 @@
     lax.fori_loop(0, 64, coef3, 0, unroll=4)
 
     zero_plane = jnp.zeros((8, 128), F32)
-    for k in (0, 1, 66, 67):
-        cor3[k] = zero_plane
+    lowest = (gz + 1) // 2 - 1
+    cor3[...] = jnp.zeros((6, 8, 128), F32)
+    for k in (0, 1, 2, 67, 68, 69):
+        dir3[k] = zero_plane
+        res3[k] = zero_plane
+    mul3[64] = zero_plane
+    img3[64] = zero_plane
 
     def clear3(k, _):
-        dir3[k] = zero_plane
+        dir3[k + 3] = zero_plane
         mul3[k] = zero_plane
-        cor3[k + 2] = zero_plane
         return 0
 
     lax.fori_loop(0, 64, clear3, 0, unroll=8)
-    for ref in (dir3, mul3, res3, img3):
-        ref[64] = zero_plane
 
     wait_recv(column_src)
     layer_src = gather_layer(1, inbox_src, wide_src)
@@ -573,7 +575,7 @@
 
     for zh in range(4):
         for k in range(16):
-            res3[16 * zh + k] = wide_src[k, zh]
+            res3[16 * zh + k + 3] = wide_src[k, zh]
 
     def whole(v):
         return jnp.sum(jnp.sum(v, axis=1, keepdims=True), axis=0, keepdims=True)
@@ -586,13 +588,11 @@
         return image
 
     def advance(k, alpha, beta):
-        direction = res3[k] + beta * dir3[k]
-        dir3[k] = direction
-        cor3[k + 2] = cor3[k + 2] + alpha * direction
+        dir3[k + 3] = res3[k + 3] + beta * dir3[k + 3]
         image = img3[k] + beta * mul3[k]
         mul3[k] = image
-        resid = res3[k] - alpha * image
-        res3[k] = resid
+        resid = res3[k + 3] - alpha * image
+        res3[k + 3] = resid
         return resid
 
     def totals(first, next_resid):
@@ -605,21 +605,19 @@
         norm, power, _, _ = lax.fori_loop(0, 64, plane, (zero_plane, zero_plane, zero_plane, first), unroll=64)
         return whole(norm), whole(power)
 
-    norm, power = totals(res3[0], lambda k: res3[k])
+    norm, power = totals(res3[3], lambda k: res3[k + 3])
 
     def sweep(step, carry):
         alpha, beta, norm = carry
         norm_next, power = totals(advance(0, alpha, beta), lambda k: advance(k, alpha, beta))
+        cor3[...] = cor3[...] + alpha * dir3[pl.ds(lowest + 1, 6)]
         beta = norm_next / norm
         return norm_next / (power - beta * norm_next / alpha), beta, norm_next
 
     alpha, beta, _ = lax.fori_loop(0, SWEEPS - 1, sweep, (norm / power, jnp.zeros((1, 1), F32), norm))
 
-    def finish(k, _):
-        cor3[k + 2] = cor3[k + 2] + alpha * (res3[k] + beta * dir3[k])
-        return 0
-
-    lax.fori_loop(0, 64, finish, 0, unroll=16)
+    window = pl.ds(lowest + 1, 6)
+    cor3[...] = cor3[...] + alpha * (res3[window] + beta * dir3[window])
 
     spread_rows, spread_cols = iota((128, 256), 0), iota((128, 256), 1)
     fine_x = spread_cols % 128
@@ -634,7 +632,7 @@
     mixed = []
     for d in range(-3, 4):
         plane = gz + d + 4
-        index = plane // 2
+        index = plane // 2 - lowest
         other = index + 2 * (plane % 2) - 1
         mixed.append(0.75 * cor3[index] + 0.25 * cor3[other])
     x_done = dot(jnp.concatenate(mixed, axis=0), from_halves)
@@ -709,21 +707,15 @@
         smo0[k + 1, 7:8, :] = rows_in[0, 2, k : k + 1, :]
         smo0[k + 1, 40:41, :] = rows_in[1, 2, k : k + 1, :]
     prolong(ups, smo0, 1, slice(0, 48), spread_x0, True)
-    outgoing = []
     for k in range(4):
         for r, m in fine.chunks():
             here, near = fine.neighbours(smo0, k, r, m)
-            result[k, r : r + m, :] = (1.0 - OMEGA) * here + (src0[k, r : r + m, :] + near) * fine.idg[k, r : r + m, :]
-        copy = pltpu.make_async_copy(result.at[k], out.at[k], out_sem.at[k])
-        copy.start()
-        outgoing.append(copy)
+            out[k, r : r + m, :] = (1.0 - OMEGA) * here + (src0[k, r : r + m, :] + near) * fine.idg[k, r : r + m, :]
 
     wait_send(
         z_dens + z_vals + y_both + dens1_copies + copies2 + column_dens + y_smooth + layer_dens
         + column_src + layer_src + swap_z + swap_y + swap_d
     )
-    for copy in outgoing:
-        copy.wait()
 
 
 def coefficient_scratch(planes, rows, cols):
@@ -736,11 +728,12 @@
 
 def per_device(density, right_side, pressure_guess):
     coarsest, longer = pltpu.VMEM((64, 8, 128), F32), pltpu.VMEM((65, 8, 128), F32)
+    padded = pltpu.VMEM((70, 8, 128), F32)
     return pl.pallas_call(
         kernel,
         out_shape=jax.ShapeDtypeStruct(density.shape, F32),
         in_specs=[pl.BlockSpec(memory_space=pltpu.HBM)] * 3,
-        out_specs=pl.BlockSpec(memory_space=pltpu.HBM),
+        out_specs=pl.BlockSpec(memory_space=pltpu.VMEM),
         scratch_shapes=[
             *[pltpu.VMEM((6, 48, 512), F32)] * 3,
             *[pltpu.VMEM((4, 32, 512), F32)] * 2,
@@ -761,11 +754,10 @@
             pltpu.VMEM((16, 4, 8, 128), F32),
             pltpu.VMEM((66, 8, 128), F32),
             coarsest, coarsest, longer, coarsest,
-            longer, longer, longer, longer, pltpu.VMEM((68, 8, 128), F32),
+            padded, padded, longer, longer, pltpu.VMEM((6, 8, 128), F32),
             pltpu.VMEM((8, 256), F32),
             pltpu.VMEM((8, 32, 128), F32),
             pltpu.VMEM((7, 48, 128), F32),
-            pltpu.VMEM((4, 32, 512), F32),
             pltpu.VMEM((2, 32, 512), F32),
             pltpu.VMEM((8, 512), F32),
             *[pltpu.VMEM((2, 2, 16, 256), F32)] * 2,
@@ -776,7 +768,6 @@
             *[pltpu.VMEM((2, 4, 256), F32)] * 2,
             *[pltpu.VMEM((4, 4, 256), F32)] * 2,
             pltpu.SemaphoreType.DMA((3,)),
-            pltpu.SemaphoreType.DMA((4,)),
             pltpu.SemaphoreType.DMA((COPIES,)),
             pltpu.SemaphoreType.DMA((COPIES,)),
         ],

time: 66.5 us -> 66.3 us (level)
  the two profiles are of different devices: /device:TPU:1 before, /device:TPU:2 now
where the time goes in v7:
time: 66.3 us; the launch traced here: 66.2 us
  Pallas kernels  65.4 us (99%)
  local copies, waits for them, and re-layouts  0.71 us (1%)
    pallas_call x1, Pallas kernels, per_device(): pl.pallas_call(kernel, out_shape=jax.ShapeDtypeStruct(density.shape, F32)...  65.4 us

profile of v7, /device:TPU:2, one launch (start us, length us, event | category | flops | bytes accessed | tf_op | source)
XLA Modules:
  0.0 66.2 jit_solution(11909489197675029275)
XLA Ops:
  0.0 65.4 %shard_map.37 = f32[4,32,512]{2,1,0:T(8,128)S(1)} custom-call(f32[4,32,512]{2,1,0:T(8,128)} %dens_in.1, f32[4,32,512]{2,1,0:T(8,128)} %right_in.1, f32[4,32,512]{2,1,0:T(8,128)} %guess_in.1), custom_call_target="tpu_custom_call" | custom-call | flops 20000000 | bytes 1048576 | tf_op jit(solution)/shard_map/pallas_call | solution.py:732
  65.5 0.7 %copy.5 = f32[4,32,512]{2,1,0:T(8,128)} copy(f32[4,32,512]{2,1,0:T(8,128)S(1)} %shard_map.37) | data formatting | bytes 524288

commit v8 on v7

--- a/solution.py
+++ b/solution.py
@@ -288,6 +288,29 @@
         send(rows_out.at[1, 0:2], rows_in.at[1, 0:2], faces[3]),
     ]
 
+    rows2 = {dy: (slice(16, 24), slice(16 - 8 * dy, 24 - 8 * dy)) for dy in (0, 1, -1)}
+    y_ways = ((1, faces[2]), (-1, faces[3]))
+    z_ways = ((1, faces[0]), (-1, faces[1]))
+
+    def fill_y(ref, planes, rows, first):
+        last = first + rows - 1
+        for k in planes:
+            ref[k, first - 1 : first, :] = jnp.where(gy == 0, ref[k, first : first + 1, :], ref[k, first - 1 : first, :])
+            ref[k, last + 1 : last + 2, :] = jnp.where(
+                gy == ny - 1, ref[k, last : last + 1, :], ref[k, last + 1 : last + 2, :]
+            )
+
+    def fill_z(ref, own, planes, rows, reach):
+        for i in range(reach):
+            low, high = own - 1 - i * planes, own + planes + i * planes
+            ref[low, rows, :] = jnp.where(gz == i, ref[low + 1, rows, :], ref[low, rows, :])
+            ref[high, rows, :] = jnp.where(gz == nz - 1 - i, ref[high - 1, rows, :], ref[high, rows, :])
+
+    for k in range(4):
+        fine.faces_x(k)
+    for face in (1, 2, 3):
+        fine.faces_z(face)
+    wait_recv(y_both)
     dens1_copies = [
         send(rho1.at[2:4, 16:32, :], rho1.at[0:2, 16:32, :], faces[0]),
         send(rho1.at[2:4, 16:32, :], rho1.at[4:6, 16:32, :], faces[1]),
@@ -296,30 +319,6 @@
     ]
     for i, (dz, dy, device) in enumerate(corners):
         dens1_copies.append(send(dens_d_out.at[i], dens_d_in.at[i], device))
-
-    rows2 = {dy: (slice(16, 24), slice(16 - 8 * dy, 24 - 8 * dy)) for dy in (0, 1, -1)}
-    y_ways = ((1, faces[2]), (-1, faces[3]))
-    z_ways = ((1, faces[0]), (-1, faces[1]))
-
-    def fill_y(ref, planes, rows, first):
-        last = first + rows - 1
-        for k in planes:
-            ref[k, first - 1 : first, :] = jnp.where(gy == 0, ref[k, first : first + 1, :], ref[k, first - 1 : first, :])
-            ref[k, last + 1 : last + 2, :] = jnp.where(
-                gy == ny - 1, ref[k, last : last + 1, :], ref[k, last + 1 : last + 2, :]
-            )
-
-    def fill_z(ref, own, planes, rows, reach):
-        for i in range(reach):
-            low, high = own - 1 - i * planes, own + planes + i * planes
-            ref[low, rows, :] = jnp.where(gz == i, ref[low + 1, rows, :], ref[low, rows, :])
-            ref[high, rows, :] = jnp.where(gz == nz - 1 - i, ref[high - 1, rows, :], ref[high, rows, :])
-
-    for k in range(4):
-        fine.faces_x(k)
-    for face in (1, 2, 3):
-        fine.faces_z(face)
-    wait_recv(y_both)
     for k in range(4):
         for f, ref in ((0, rho0), (1, val0)):
             ref[k + 1, 7:8, :] = rows_in[0, f, k : k + 1, :]

time: 66.3 us -> 66.8 us (level)
  no operation moved by 1% of the time
where the time goes in v8:
time: 66.8 us; the launch traced here: 66.7 us
  Pallas kernels  65.9 us (99%)
  local copies, waits for them, and re-layouts  0.71 us (1%)
    pallas_call x1, Pallas kernels, per_device(): pl.pallas_call(kernel, out_shape=jax.ShapeDtypeStruct(density.shape, F32)...  65.9 us

profile of v8, /device:TPU:2, one launch (start us, length us, event | category | flops | bytes accessed | tf_op | source)
XLA Modules:
  0.0 66.7 jit_solution(3094135759818843323)
XLA Ops:
  0.0 65.9 %shard_map.37 = f32[4,32,512]{2,1,0:T(8,128)S(1)} custom-call(f32[4,32,512]{2,1,0:T(8,128)} %dens_in.1, f32[4,32,512]{2,1,0:T(8,128)} %right_in.1, f32[4,32,512]{2,1,0:T(8,128)} %guess_in.1), custom_call_target="tpu_custom_call" | custom-call | flops 20000000 | bytes 1048576 | tf_op jit(solution)/shard_map/pallas_call | solution.py:731
  66.0 0.7 %copy.5 = f32[4,32,512]{2,1,0:T(8,128)} copy(f32[4,32,512]{2,1,0:T(8,128)S(1)} %shard_map.37) | data formatting | bytes 524288

commit v9 on v7

--- a/solution.py
+++ b/solution.py
@@ -121,7 +121,7 @@
     rho1, val1, src1, base1, up1, bx1, by1, bz1, dg1, idg1,
     rho2, val2, base2, up2, bx2, by2, bz2, dg2, idg2,
     rows_out, rows_in, message, inbox_dens, inbox_src, tile, wide_dens, wide_src,
-    rho3, bx3, by3, bz3, dg3, dir3, res3, img3, mul3, cor3, pair_tmp, pair_rows, fine_rows,
+    rho3, bx3, by3, by3_up, bz3, dg3, dir3, res3, img3, mul3, cor3, pair_tmp, pair_rows, fine_rows,
     far_smooth, face_rows, z_out, z_in, y_out, y_in, d_out, d_in, wide_y_out, wide_y_in, wide_d_out, wide_d_in,
     dens_y_out, dens_y_in, dens_d_out, dens_d_in, local_sem, send_sem, recv_sem,
 ):
@@ -524,7 +524,9 @@
         total = low + jnp.where(last_x, edge, pltpu.roll(low, 127, 1))
         bx3[k] = jnp.where(first_x, 0.0, scale3 * low)
         low = twice_inverse(rho + jnp.where(first_y, rho, lower_y(rho)))
-        total = total + low + jnp.where(last_y, edge, upper_y(low))
+        high = upper_y(low)
+        total = total + low + jnp.where(last_y, edge, high)
+        by3_up[k] = jnp.where(last_y, 0.0, scale3 * high)
         by3[k] = jnp.where(first_y, 0.0, scale3 * low)
         dg3[k] = scale3 * total + bz3[k] + bz3[k + 1]
         return 0
@@ -547,6 +549,9 @@
 
     lax.fori_loop(0, 64, clear3, 0, unroll=8)
 
+    wait_send(
+        z_dens + z_vals + y_both + dens1_copies + swap_z + swap_y + swap_d + column_dens + layer_dens + copies2
+    )
     wait_recv(column_src)
     layer_src = gather_layer(1, inbox_src, wide_src)
 
@@ -561,7 +566,7 @@
     base2_far = pass_on(base2, 2)
 
     wait_recv(dens2_last)
-    wait_send(dens2_near + dens2_far + dens2_last)
+    wait_send(dens2_near + dens2_far + dens2_last + more1 + more2 + column_src)
 
     def inside_z(face):
         at = gz + face - 2
@@ -581,9 +586,12 @@
         return jnp.sum(jnp.sum(v, axis=1, keepdims=True), axis=0, keepdims=True)
 
     def apply(k, prev, here, later):
-        bx, by = bx3[k], by3[k]
-        image = (dg3[k] * here - bz3[k] * prev) - (bz3[k + 1] * later + by * lower_y(here))
-        image = image - ((bx * pltpu.roll(here, 1, 1) + upper_y(by * here)) + pltpu.roll(bx * here, 127, 1))
+        bx = bx3[k]
+        swapped = pltpu.roll(here, 64, 1)
+        below = jnp.where(right_half, swapped, pltpu.roll(swapped, 1, 0))
+        above = jnp.where(right_half, pltpu.roll(swapped, 7, 0), swapped)
+        image = (dg3[k] * here - bz3[k] * prev) - (bz3[k + 1] * later + by3[k] * below)
+        image = image - ((bx * pltpu.roll(here, 1, 1) + by3_up[k] * above) + pltpu.roll(bx * here, 127, 1))
         img3[k] = image
         return image
 
@@ -637,7 +645,7 @@
         mixed.append(0.75 * cor3[index] + 0.25 * cor3[other])
     x_done = dot(jnp.concatenate(mixed, axis=0), from_halves)
     wait_recv(more1 + base2_far + z_smooth + y_smooth)
-    wait_send(more1 + more2 + base2_far + z_smooth)
+    wait_send(z_smooth)
     for way, row in ((0, 15), (1, 32)):
         for k in range(2):
             base1[k + 2, row : row + 1, :] = wide_y_in[way, k : k + 1, :]
@@ -712,10 +720,7 @@
             here, near = fine.neighbours(smo0, k, r, m)
             out[k, r : r + m, :] = (1.0 - OMEGA) * here + (src0[k, r : r + m, :] + near) * fine.idg[k, r : r + m, :]
 
-    wait_send(
-        z_dens + z_vals + y_both + dens1_copies + copies2 + column_dens + y_smooth + layer_dens
-        + column_src + layer_src + swap_z + swap_y + swap_d
-    )
+    wait_send(y_smooth + layer_src + base2_far)
 
 
 def coefficient_scratch(planes, rows, cols):
@@ -753,7 +758,7 @@
             pltpu.VMEM((16, 4, 8, 128), F32),
             pltpu.VMEM((16, 4, 8, 128), F32),
             pltpu.VMEM((66, 8, 128), F32),
-            coarsest, coarsest, longer, coarsest,
+            coarsest, coarsest, coarsest, longer, coarsest,
             padded, padded, longer, longer, pltpu.VMEM((6, 8, 128), F32),
             pltpu.VMEM((8, 256), F32),
             pltpu.VMEM((8, 32, 128), F32),

time: 66.3 us -> 65.6 us (0.989)
  Pallas kernels: 65.4 us -> 64.7 us
    pallas_call x1, Pallas kernels: 65.4 us -> 64.7 us  [per_device(): pl.pallas_call(kernel, out_shape=jax.ShapeDtypeStruct(density.shape, F32)...]
where the time goes in v9:
time: 65.6 us; the launch traced here: 65.4 us
  Pallas kernels  64.7 us (99%)
  local copies, waits for them, and re-layouts  0.71 us (1%)
    pallas_call x1, Pallas kernels, per_device(): pl.pallas_call(kernel, out_shape=jax.ShapeDtypeStruct(density.shape, F32)...  64.7 us

profile of v9, /device:TPU:2, one launch (start us, length us, event | category | flops | bytes accessed | tf_op | source)
XLA Modules:
  0.0 65.4 jit_solution(8160923794767740484)
XLA Ops:
  0.0 64.7 %shard_map.37 = f32[4,32,512]{2,1,0:T(8,128)S(1)} custom-call(f32[4,32,512]{2,1,0:T(8,128)} %dens_in.1, f32[4,32,512]{2,1,0:T(8,128)} %right_in.1, f32[4,32,512]{2,1,0:T(8,128)} %guess_in.1), custom_call_target="tpu_custom_call" | custom-call | flops 20000000 | bytes 1048576 | tf_op jit(solution)/shard_map/pallas_call | solution.py:737
  64.7 0.7 %copy.5 = f32[4,32,512]{2,1,0:T(8,128)} copy(f32[4,32,512]{2,1,0:T(8,128)S(1)} %shard_map.37) | data formatting | bytes 524288

commit v10 on v9

--- a/solution.py
+++ b/solution.py
@@ -152,7 +152,7 @@
         for dy in (0, 1, -1):
             around.append((dz, dy, ((gz + dz + nz) % nz, (gy + dy + ny) % ny)))
     corners = [(dz, dy, device) for dz, dy, device in around if dy]
-    greeted = column + [device for _, _, device in around] + faces[2:] + layer
+    greeted = column + [device for _, _, device in around] + layer
 
     barrier = pltpu.get_barrier_semaphore()
     for device in greeted:
@@ -696,8 +696,12 @@
             for k in range(6):
                 parent_z = (k + first) // 2
                 near_z = parent_z + 2 * ((k + first) % 2) - 1
-                value = 0.75 * fine_rows[parent_z, 0:tall, :] + 0.25 * fine_rows[near_z, 0:tall, :]
-                target[k, rows, cols] = target[k, rows, cols] + value if add else value
+                if add and k in (0, 5):
+                    kept, taken = slice(8, tall - 8), slice(8, tall - 8)
+                else:
+                    kept, taken = rows, slice(0, tall)
+                value = 0.75 * fine_rows[parent_z, taken, :] + 0.25 * fine_rows[near_z, taken, :]
+                target[k, kept, cols] = target[k, kept, cols] + value if add else value
 
     prolong(ups, up1, 2, slice(8, 40), spread_x1, False)
     ups = []

time: 65.6 us -> 65.5 us (level)
  no operation moved by 1% of the time
where the time goes in v10:
time: 65.5 us; the launch traced here: 65.4 us
  Pallas kernels  64.7 us (99%)
  local copies, waits for them, and re-layouts  0.71 us (1%)
    pallas_call x1, Pallas kernels, per_device(): pl.pallas_call(kernel, out_shape=jax.ShapeDtypeStruct(density.shape, F32)...  64.7 us

profile of v10, /device:TPU:2, one launch (start us, length us, event | category | flops | bytes accessed | tf_op | source)
XLA Modules:
  0.0 65.4 jit_solution(6480850424559749876)
XLA Ops:
  0.0 64.7 %shard_map.37 = f32[4,32,512]{2,1,0:T(8,128)S(1)} custom-call(f32[4,32,512]{2,1,0:T(8,128)} %dens_in.1, f32[4,32,512]{2,1,0:T(8,128)} %right_in.1, f32[4,32,512]{2,1,0:T(8,128)} %guess_in.1), custom_call_target="tpu_custom_call" | custom-call | flops 20000000 | bytes 1048576 | tf_op jit(solution)/shard_map/pallas_call | solution.py:741
  64.7 0.7 %copy.5 = f32[4,32,512]{2,1,0:T(8,128)} copy(f32[4,32,512]{2,1,0:T(8,128)S(1)} %shard_map.37) | data formatting | bytes 524288
